TPU v7x, 256 devices: a whole 4x4x8 slice. The times are simulated.
256 devices in a mesh: replica: 8 (over y, z_hi), fsdp: 32 (over x, z_lo, core).
Axes of the slice: x: 4, y: 4, z: 8 (z_hi: 2, z_lo: 4; z = z_hi * 4 + z_lo), core: 2. Of those that a mesh axis runs over, the one named last changes fastest.
Arguments:
- activations: bfloat16 [8, 4096, 8192], P('replica', 'fsdp'), may hold values from -18 to 18, as said below
- norm_gain: float32 [8, 8192], P('replica'), may hold values from 0.5 to 1.5
- key_weight: bfloat16 [8, 8192, 512], P('replica', 'fsdp'), may hold values from -0.0625 to 0.0625
- key_cotangent: bfloat16 [8, 4096, 512], P('replica', 'fsdp'), may hold values from -6 to 6
- local_fragment: float32 [8, 8192, 512], P('replica', 'fsdp'), may hold values from -6 to 6
- global_fragment: float32 [8192, 512], P('fsdp'), may hold values from -6 to 6
- momentum_codes: bfloat16 [8192, 512], P('fsdp'), may hold values from -1 to 1
- momentum_scales: float32 [8192, 4], P('fsdp'), may hold values from 0.05 to 0.5
Outputs:
- keys: float32 [8, 4096, 512], P('replica', 'fsdp')
- weight_grad: float32 [8, 8192, 512], P('replica', 'fsdp')
- gain_grad: float32 [8, 8192], P('replica', 'fsdp')
- input_gradient_rows: float32 [8, 4096, 8192], P('replica', 'fsdp')
- new_global: float32 [8192, 512], P('fsdp')
- new_codes: bfloat16 [8192, 512], P('fsdp')
- new_scales: float32 [8192, 4], P('fsdp')
Inputs may be any that keep to these rules, and one draw needn't show every extreme that they name: Each token's activations carry their own scale, between 0.3 and 3 times that of the others in spread.
All inputs are finite; a program needn't handle non-finite values. Where the computation divides by a largest or mean magnitude, that divisor is 1e-20 or more.
Results may differ from a plain program's by a relative error of at most 0.0029.
Values may be sent and summed in bfloat16 or wider, within the bound.
No kernel may reach another device: no remote copies, remote signals or barrier semaphores. Data moves between devices by JAX's collectives and lax.ppermute only.
A program may use at most 128 MiB of HBM per device.

v0:
```python
import jax
import jax.numpy as jnp
from jax import lax
from jax.sharding import PartitionSpec as P

EPS = 1e-05
MU = 0.9
RATE = 0.7


def outer_update(glob, pseudo, codes, scales):
    rows, width = glob.shape
    blocks = scales.shape[1]
    span = width // blocks
    momentum = codes.astype(jnp.float32).reshape(rows, blocks, span) * scales[:, :, None]
    moved = MU * momentum + pseudo.reshape(rows, blocks, span)
    new_global = glob - RATE * (pseudo + MU * moved.reshape(rows, width))
    new_scales = jnp.max(jnp.abs(moved), axis=-1) + 1e-06
    new_codes = (moved / new_scales[:, :, None]).reshape(rows, width).astype(jnp.bfloat16)
    return (new_global, new_codes, new_scales)


def body(
    activations,
    norm_gain,
    key_weight,
    key_cotangent,
    local_fragment,
    global_fragment,
    momentum_codes,
    momentum_scales,
):
    input_float = activations[0].astype(jnp.float32)
    inverse_root_mean = lax.rsqrt(jnp.mean(input_float * input_float, axis=-1, keepdims=True) + EPS)
    centered_input = input_float * inverse_root_mean
    gain_vector = norm_gain[0]
    normalized_rows = (centered_input * gain_vector).astype(jnp.bfloat16)
    weight = key_weight[0]
    grads = key_cotangent[0]
    keys = jnp.dot(
        normalized_rows,
        lax.all_gather(weight, "fsdp", axis=0, tiled=True),
        preferred_element_type=jnp.float32,
    )
    normalized_cotangent = lax.dot_general(
        grads,
        lax.all_gather(weight, "fsdp", axis=0, tiled=True),
        (((1,), (1,)), ((), ())),
        preferred_element_type=jnp.float32,
    )
    gain_product = jnp.sum(normalized_cotangent * centered_input, axis=0)
    centered_cotangent = normalized_cotangent * gain_vector
    inner_product = jnp.mean(centered_cotangent * centered_input, axis=-1, keepdims=True)
    input_gradient_rows = inverse_root_mean * (centered_cotangent - centered_input * inner_product)
    weight_term = lax.dot_general(
        normalized_rows, grads, (((0,), (0,)), ((), ())), preferred_element_type=jnp.float32
    )
    weight_grad, gain_grad = (
        lax.psum_scatter(weight_term, "fsdp", scatter_dimension=0, tiled=True),
        lax.psum_scatter(gain_product, "fsdp", scatter_dimension=0, tiled=True),
    )
    replicas = lax.axis_size("replica")
    delta = global_fragment - local_fragment[0]
    pseudo = lax.psum(delta, "replica") / replicas
    new_global, new_codes, new_scales = outer_update(
        global_fragment, pseudo, momentum_codes, momentum_scales
    )
    return (
        keys[None],
        weight_grad[None],
        gain_grad[None],
        input_gradient_rows[None],
        new_global,
        new_codes,
        new_scales,
    )


def solution(mesh):
    in_specs = (
        P("replica", "fsdp", None),
        P("replica", None),
        P("replica", "fsdp", None),
        P("replica", "fsdp", None),
        P("replica", "fsdp", None),
        P("fsdp", None),
        P("fsdp", None),
        P("fsdp", None),
    )
    out_specs = (
        P("replica", "fsdp", None),
        P("replica", "fsdp", None),
        P("replica", "fsdp"),
        P("replica", "fsdp", None),
        P("fsdp", None),
        P("fsdp", None),
        P("fsdp", None),
    )
    return jax.shard_map(body, mesh=mesh, in_specs=in_specs, out_specs=out_specs, check_vma=False)
```

profile of v0, /device:TPU:1, one launch (start us, length us, event | category | flops | bytes accessed | tf_op | source)
XLA Modules:
  0.0 315.9 jit_solution(3489079752382131486)
XLA Ops:
  8.0 0.0 copy-start
  8.0 0.0 copy-start.1
  8.0 0.0 copy-start.4
  8.0 0.0 all-reduce.3.cloned.1.call-start
  8.1 2.2 bitcast_subtract_fusion
  10.3 0.0 all-reduce.3.cloned.1.call-update
  10.3 0.0 all-gather.3.cloned.1.call-start
  10.4 0.5 all-gather.3.cloned.1.call-update
  10.9 0.0 reduce-scatter.2.cloned.1.call-start
  11.0 2.1 fusion.16
  13.0 0.0 copy-done
  13.1 0.0 copy-done.1
  13.1 0.0 copy-done.4
  13.1 8.2 %fusion.20 = f32[8192,512]{1,0:T(8,128)} fusion(bf16[1,128,8192]{2,1,0:T(8,128)(2,1)S(1)} %copy-done.1, f32[8192]{0:T(1024)S(1)} %bitcast.78, f32[128]{0:T(128)S(1)} %add_rsqrt_fusion, bf16[1,128,512]{2,1,0:T(8,128)(2,1)S(1)} %copy-done), kind=kOutput, calls=%fused_computation.22 | convolution fusion | flops 1077936128 | bytes 19038720 | tf_op jit(solution)/shard_map/dot_general | solution.py:55
  21.2 0.0 copy-start.6
  21.2 0.0 copy-start.5
  21.3 0.0 reduce-scatter.2.cloned.1.call-update
  21.3 0.0 copy-start.3
  21.3 0.6 copy-done.6
  21.9 0.6 dynamic-slice
  23.2 0.0 copy-done.5
  23.2 0.1 copy.17
  23.3 1.1 reshape.57
  24.4 116.6 %all-reduce.3.cloned.1.call-done = f32[256,512]{1,0:T(8,128)} async-done(((f32[256,512]{1,0:T(8,128)}), f32[256,512]{1,0:T(8,128)}) %all-reduce.3.cloned.1.call-update) | async-done | bytes 524304 | tf_op jit(solution)/shard_map/psum | solution.py:64
  141.1 1.9 broadcast_multiply_fusion
  143.0 2.0 reshape.58
  145.0 1.7 abs_reduce_fusion
  146.7 0.7 copy.18
  147.4 0.3 div.27
  147.7 0.3 mul.109
  148.0 0.0 copy-done.3
  148.0 2.3 fusion.32
  150.3 0.0 all-gather.3.cloned.1.call-done
  150.3 8.4 %fusion.12 = (f32[128]{0:T(128)S(1)}, f32[8192]{0:T(1024)S(1)}, f32[128,8192]{1,0:T(8,128)}) fusion(bf16[1,128,8192]{2,1,0:T(8,128)(2,1)S(1)} %copy-done.1, f32[8192]{0:T(1024)S(1)} %bitcast.79, f32[128]{0:T(128)S(1)} %add_rsqrt_fusion, bf16[1,8192,512]{2,1,0:T(8,128)(2,1)} %all-gather.3.cloned.1.call-done, bf16[1,128,512]{2,1,0:T(8,128)(2,1)S(1)} %copy-done), kind=kOutput, calls=%fused_computation.14 | convolution fusion | flops 1081073536 | bytes 14877696 | tf_op jit(solution)/shard_map/dot_general | solution.py:45
  158.7 140.5 %all-reduce = f32[8192]{0:T(1024)S(1)} all-reduce(f32[8192]{0:T(1024)S(1)} %get-tuple-element.15), channel_id=4, replica_groups=mesh['replica'=8,'fsdp'=32] {'fsdp'}, use_global_device_ids=true, to_apply=%region_3.0.clone | all-reduce | flops 8192 | bytes 65536
  299.2 0.6 dynamic-slice.1
  299.8 0.0 copy-start.2
  299.8 5.6 %fusion.27 = f32[1,128,512]{2,1,0:T(8,128)} fusion(bf16[1,8192,512]{2,1,0:T(8,128)(2,1)} %all-gather.3.cloned.1.call-done, bf16[1,128,8192]{2,1,0:T(8,128)(2,1)S(1)} %copy-done.1, f32[8192]{0:T(1024)S(1)} %bitcast.80, f32[128]{0:T(128)S(1)} %add_rsqrt_fusion), kind=kOutput, calls=%fused_computation.27 | convolution fusion | flops 1077936128 | bytes 10781184 | tf_op jit(solution)/shard_map/dot_general | solution.py:40
  305.4 0.0 copy-done.2
  305.4 3.0 fusion.15
  308.4 0.0 reduce-scatter.2.cloned.1.call-done
  (3 shorter events, 0.0 us)
Async XLA Ops:
  8.0 5.0 %copy-start = (bf16[1,128,512]{2,1,0:T(8,128)(2,1)S(1)}, bf16[1,128,512]{2,1,0:T(8,128)(2,1)}, u32[]{:S(2)}) copy-start(bf16[1,128,512]{2,1,0:T(8,128)(2,1)} %param.11) | copy-start | bytes 393220
  8.0 5.0 %copy-start.1 = (bf16[1,128,8192]{2,1,0:T(8,128)(2,1)S(1)}, bf16[1,128,8192]{2,1,0:T(8,128)(2,1)}, u32[]{:S(2)}) copy-start(bf16[1,128,8192]{2,1,0:T(8,128)(2,1)} %param.8) | copy-start | bytes 6291460
  8.0 5.0 %copy-start.4 = (f32[1,8192]{1,0:T(1,128)S(1)}, f32[1,8192]{1,0:T(1,128)}, u32[]{:S(2)}) copy-start(f32[1,8192]{1,0:T(1,128)} %param.9) | copy-start | bytes 98308
  8.0 133.0 %all-reduce.3.cloned.1.call-start = ((), (), s32[]{:S(2)}) async-start(), calls=%async_computation.2 | async-start | bytes 1048576 | tf_op jit(solution)/shard_map/psum | solution.py:64
  10.3 140.0 %all-gather.3.cloned.1.call-start = ((), (), s32[]{:S(2)}) async-start(), calls=%async_computation.3 | async-start | bytes 8650752 | tf_op jit(solution)/shard_map/all_gather | solution.py:42
  10.9 297.5 %reduce-scatter.2.cloned.1.call-start = ((), (), s32[]{:S(2)}) async-start(), calls=%async_computation.1 | async-start | bytes 17301504 | tf_op jit(solution)/shard_map/reduce_scatter | solution.py:59
  21.2 0.7 copy-start.6
  21.2 1.9 copy-start.5
  21.3 126.8 %copy-start.3 = (f32[256,512]{1,0:T(8,128)S(1)}, f32[256,512]{1,0:T(8,128)}, u32[]{:S(2)}) copy-start(f32[256,512]{1,0:T(8,128)} %param.13) | copy-start | bytes 1572868
  299.8 5.6 %copy-start.2 = (f32[128,8192]{1,0:T(8,128)S(1)}, f32[128,8192]{1,0:T(8,128)}, u32[]{:S(2)}) copy-start(f32[128,8192]{1,0:T(8,128)} %get-tuple-element.18) | copy-start | bytes 12582916
Sparse Core Ops, SparseCore 0:
  12.1 128.9 all-reduce.2
Sparse Core Ops, SparseCore 1:
  12.7 87.0 all-gather.2
  102.7 199.1 reduce-scatter.1
where the time goes:
time: 320 us; the launch traced here: 316 us
  blocking collectives  140 us (44%)
  waiting for transfers between devices  117 us (37%)
  matrix products  22.2 us (7%)
  between operations  16.2 us (5%)
  other arithmetic  13.2 us (4%)
  local copies, waits for them, and re-layouts  6.48 us (2%)
    unnamed x1, blocking collectives  140 us
    psum x1, waiting for transfers between devices, body(): pseudo = lax.psum(delta, 'replica') / replicas  117 us
    dot_general x1, matrix products, body(): lax.dot_general(grads, lax.all_gather(weight, 'fsdp', axis=0, tiled=True)...  8.37 us
    dot_general x1, matrix products, body(): lax.dot_general(normalized_rows, grads, (((0,), (0,)), ((), ())), preferr...  8.17 us
  transfers between devices with their start and end apart: 3, of which 1 were waited for; matrix products, arithmetic and copies ran while one was open for 12% of the time, Pallas kernels for 0%

commit v1 on v0

v1 whole, which is shorter than its diff:
```python
import functools

import jax
import jax.numpy as jnp
from jax import lax
from jax.experimental import pallas as pl
from jax.experimental.pallas import tpu as pltpu
from jax.sharding import PartitionSpec as P

EPS = 1e-05
MU = 0.9
RATE = 0.7
X, Z, C = 4, 4, 2
Y, H = 4, 2
OFFSETS = (0, 1, 3, 2)
FIRST = ((0, (0, 1), (0, 0), None), (1, (0,), (1, 0), None), (2, (0,), (1, 1), None))
SECOND = (
    (0, (2, 3), (0, 0), (1, 2)),
    (0, (0, 1), None, (1, 0)),
    (1, (0,), None, (1, 4)),
    (2, (0,), None, (1, 5)),
)
THIRD = ((1, (1, 2, 3), (0, 0), (1, 0)), (2, (1, 2, 3), (0, 3), (1, 3)))
LAST = ((3, (0, 1, 2, 3), (0, 0), (1, 0)),)
VMEM_LIMIT = 56 * 1024 * 1024
F32 = jnp.float32
BF16 = jnp.bfloat16


def index_of(x, z, c):
    return (x * Z + z) * C + c


def shift(value, dx=0, flip=0, swap=0):
    moves = [
        (index_of(x, z, c), index_of((x + dx) % X, z ^ flip, c ^ swap))
        for x in range(X)
        for z in range(Z)
        for c in range(C)
    ]
    return lax.ppermute(value, "fsdp", moves)


def trade(value, flip=0, far=0):
    moves = [(y * H + h, (y ^ flip) * H + (h ^ far)) for y in range(Y) for h in range(H)]
    return lax.ppermute(value, "replica", moves)


def params(**kw):
    return pltpu.CompilerParams(vmem_limit_bytes=VMEM_LIMIT, **kw)


def norm_kernel(place, acts, gain, cot, rinv, *slots):
    value = acts[...].astype(F32)
    inverse = lax.rsqrt(jnp.mean(value * value, axis=-1, keepdims=True) + EPS)
    rinv[...] = jnp.broadcast_to(inverse, rinv.shape)
    width = acts.shape[1] // X
    for step in range(X):
        start = pl.multiple_of(lax.rem(place[0] + step, X) * width, width)
        part = acts[:, pl.ds(start, width)].astype(F32) * inverse
        slots[step][:, :width] = (part * gain[:, pl.ds(start, width)]).astype(BF16)
        slots[step][:, width:] = cot[...]


def normalise(place, acts, gain, cot):
    tokens, width = acts.shape
    keys = cot.shape[1]
    rows = 32
    part = width // X + keys
    whole = lambda i, place: (0, 0)
    return pl.pallas_call(
        norm_kernel,
        grid_spec=pltpu.PrefetchScalarGridSpec(
            num_scalar_prefetch=1,
            grid=(tokens // rows,),
            in_specs=[
                pl.BlockSpec((rows, width), lambda i, place: (i, 0)),
                pl.BlockSpec((1, width), whole),
                pl.BlockSpec((rows, keys), lambda i, place: (i, 0)),
            ],
            out_specs=[pl.BlockSpec((rows, 128), lambda i, place: (i, 0))]
            + [pl.BlockSpec((rows, part), lambda i, place: (i, 0))] * X,
        ),
        out_shape=[jax.ShapeDtypeStruct((tokens, 128), F32)]
        + [jax.ShapeDtypeStruct((tokens, part), BF16)] * X,
        compiler_params=params(),
        name="normalise",
    )(place, acts, gain, cot)


def pack_kernel(span, place, r0, r1, r2, r3, features):
    tokens = r0.shape[0]
    width = Z * C * span
    for number, r in enumerate((r0, r1, r2, r3)):
        part = slice(number * tokens, (number + 1) * tokens)
        for flip in range(Z):
            start = (place[1] ^ flip) * (C * span) + (1 - place[2]) * span
            features[part, flip * span : (flip + 1) * span] = r[
                :, pl.ds(pl.multiple_of(start, span), span)
            ]
        features[part, Z * span :] = r[:, width:]


def pack(place, rows, span, keys):
    tokens = rows[0].shape[0] * X
    vmem = pl.BlockSpec(memory_space=pltpu.VMEM)
    return pl.pallas_call(
        functools.partial(pack_kernel, span),
        in_specs=[pl.BlockSpec(memory_space=pltpu.SMEM)] + [vmem] * X,
        out_specs=vmem,
        out_shape=jax.ShapeDtypeStruct((tokens, Z * span + keys), BF16),
        compiler_params=params(),
        name="pack",
    )(place, *rows)


def wgrad_kernel(place, r0, r1, r2, r3, other, kept, sent):
    span, keys = kept.shape[1:]
    width = Z * C * span
    mine = (r0, r1, r2, r3)
    cots = jnp.concatenate([r[:, width:] for r in mine] + [other[:, Z * span :]], axis=0)
    for flip in range(Z):
        start = pl.multiple_of((place[1] ^ flip) * (C * span) + place[2] * span, span)
        rows = jnp.concatenate(
            [r[:, pl.ds(start, span)] for r in mine]
            + [other[:, flip * span : (flip + 1) * span]],
            axis=0,
        )
        total = lax.dot_general(
            rows, cots, (((0,), (0,)), ((), ())), preferred_element_type=F32
        )
        if flip % 2:
            sent[flip // 2] = total.astype(BF16)
        else:
            kept[flip // 2] = total


def wgrad_part(place, rows, other, span, keys):
    vmem = pl.BlockSpec(memory_space=pltpu.VMEM)
    return pl.pallas_call(
        wgrad_kernel,
        in_specs=[pl.BlockSpec(memory_space=pltpu.SMEM)] + [vmem] * (X + 1),
        out_specs=[vmem] * 2,
        out_shape=[
            jax.ShapeDtypeStruct((2, span, keys), F32),
            jax.ShapeDtypeStruct((2, span, keys), BF16),
        ],
        compiler_params=params(),
        name="wgrad_part",
    )(place, *rows, other)


def pieces_of(layout, refs, place, part):
    span = part // (Z * C)
    pieces = []
    for slot, flips, *sources in layout:
        block = lax.rem(place[0] + OFFSETS[slot], X)
        for source, which in zip(sources, (place[2], 1 - place[2])):
            if source is None:
                continue
            number, first = source
            for row, flip in enumerate(flips, first):
                local = pl.multiple_of((place[1] ^ flip) * (C * span) + which * span, span)
                start = pl.multiple_of(block * part + local, span)
                rows = slice(row * span, (row + 1) * span)
                pieces.append((slot, start, local, refs[number], rows))
    return pieces


def keys_sum(pieces, acts, gain, inverse):
    total = None
    for _, start, _, ref, rows in pieces:
        lanes = pl.ds(start, rows.stop - rows.start)
        hat = acts[:, lanes].astype(F32) * inverse
        normed = (hat * gain[:, lanes]).astype(BF16)
        term = jnp.dot(normed, ref[rows, :], preferred_element_type=F32)
        total = term if total is None else total + term
    return total


def cotangent_of(cots, ref, rows):
    return lax.dot_general(
        cots, ref[rows, :], (((1,), (1,)), ((), ())), preferred_element_type=F32
    )


def early_kernel(layout, started, place, acts, gain, rinv, cot, *refs):
    weights, (keys, scaled) = refs[started:-2], refs[-2:]
    part = acts.shape[1] // X
    inverse = rinv[:, :1]
    pieces = pieces_of(layout, weights, place, part)
    total = keys_sum(pieces, acts, gain, inverse)
    keys[...] = refs[0][...] + total if started else total
    cots = cot[...]
    for number, (_, start, _, ref, rows) in enumerate(pieces):
        span = rows.stop - rows.start
        scaled[number] = inverse * cotangent_of(cots, ref, rows) * gain[:, pl.ds(start, span)]


def backward_early(place, acts, gain, rinv, cot, before, layout, weights):
    tokens, width = acts.shape
    span = width // (X * Z * C)
    pieces = sum(len(flips) * (2 - sources.count(None)) for _, flips, *sources in layout)
    vmem = pl.BlockSpec(memory_space=pltpu.VMEM)
    return pl.pallas_call(
        functools.partial(early_kernel, layout, len(before)),
        in_specs=[pl.BlockSpec(memory_space=pltpu.SMEM)]
        + [vmem] * (4 + len(before) + len(weights)),
        out_specs=[vmem, vmem],
        out_shape=[
            jax.ShapeDtypeStruct((tokens, cot.shape[1]), F32),
            jax.ShapeDtypeStruct((pieces, tokens, span), F32),
        ],
        compiler_params=params(),
        name="backward_early",
    )(place, acts, gain, rinv, cot, *before, *weights)


def late_kernel(
    layout, done, place, acts, gain, rinv, cot, early, *refs
):
    sources, refs = refs[: len(done)], refs[len(done) :]
    weights, (keys, dx, held, arrive, leave) = refs[:-5], refs[-5:]
    tokens, width = acts.shape
    part = width // X
    loads = [[] for _ in range(X)]
    count = 0
    for source, entries in zip(sources, done):
        for number, (slot, _, local, _, rows) in enumerate(
            pieces_of(entries, [None] * 16, place, part)
        ):
            load = pltpu.make_async_copy(
                source.at[number],
                held.at[slot, :, pl.ds(local, rows.stop - rows.start)],
                arrive.at[count],
            )
            load.start()
            loads[slot].append(load)
            count += 1
    inverse = rinv[:, :1]
    pieces = pieces_of(layout, weights, place, part)
    total = early[...] + keys_sum(pieces, acts, gain, inverse)
    keys[...] = total
    cots = cot[...]
    inner = jnp.sum(total * cots.astype(F32), axis=-1, keepdims=True) / width
    factor = inverse * inverse * inner

    def send(slot):
        start = pl.multiple_of(lax.rem(place[0] + OFFSETS[slot], X) * part, part)
        copy = pltpu.make_async_copy(held.at[slot], dx.at[:, pl.ds(start, part)], leave.at[slot])
        copy.start()
        return copy

    copies = []
    for slot in range(X - 1):
        for load in loads[slot]:
            load.wait()
        start = pl.multiple_of(lax.rem(place[0] + OFFSETS[slot], X) * part, part)
        held[slot] = held[slot] - acts[:, pl.ds(start, part)].astype(F32) * factor
        copies.append(send(slot))
    for slot, start, local, ref, rows in pieces:
        span = rows.stop - rows.start
        lanes = pl.ds(start, span)
        held[slot, :, pl.ds(local, span)] = (
            inverse * cotangent_of(cots, ref, rows) * gain[:, lanes]
            - acts[:, lanes].astype(F32) * factor
        )
    copies.append(send(X - 1))
    for copy in copies:
        copy.wait()


def backward_late(place, acts, gain, rinv, cot, early, sources, done, layout, weights):
    tokens, width = acts.shape
    vmem = pl.BlockSpec(memory_space=pltpu.VMEM)
    hbm = pl.BlockSpec(memory_space=pl.ANY)
    return pl.pallas_call(
        functools.partial(late_kernel, layout, done),
        in_specs=[pl.BlockSpec(memory_space=pltpu.SMEM)]
        + [vmem] * 5
        + [hbm] * len(sources)
        + [vmem] * len(weights),
        out_specs=[vmem, hbm],
        out_shape=[
            jax.ShapeDtypeStruct((tokens, cot.shape[1]), F32),
            jax.ShapeDtypeStruct((tokens, width), F32),
        ],
        scratch_shapes=[
            pltpu.VMEM((X, tokens, width // X), F32),
            pltpu.SemaphoreType.DMA((sum(source.shape[0] for source in sources),)),
            pltpu.SemaphoreType.DMA((X,)),
        ],
        compiler_params=params(),
        name="backward_late",
    )(place, acts, gain, rinv, cot, early, *sources, *weights)


def delta_kernel(place, glob, local, keep, send):
    rows = keep.shape[1]
    for flip, out, row in ((0, keep, 0), (3, keep, 1), (1, send, 0), (2, send, 1)):
        part = pl.ds(pl.multiple_of((place[3] ^ flip) * rows, rows), rows)
        out[row] = glob[part, :] - local[part, :]


def delta(place, glob, local):
    rows, width = glob.shape
    vmem = pl.BlockSpec(memory_space=pltpu.VMEM)
    return pl.pallas_call(
        delta_kernel,
        in_specs=[pl.BlockSpec(memory_space=pltpu.SMEM), vmem, vmem],
        out_specs=[vmem, vmem],
        out_shape=[jax.ShapeDtypeStruct((2, rows // Y, width), F32)] * 2,
        compiler_params=params(),
        name="delta",
    )(place, glob, local)


def outer_kernel(place, p0, p1, p2, p3, glob, codes, scales, new_global, new_codes, new_scales):
    rows = p0.shape[0]
    blocks = scales.shape[0]
    span = p0.shape[1] // blocks
    columns = jnp.concatenate([scales[...]] * (128 // blocks), axis=0).T
    spread = 128 // blocks
    for flip, part in enumerate((p0, p1, p2, p3)):
        start = pl.multiple_of((place[3] ^ flip) * rows, rows)
        new_global[pl.ds(start, rows), :] = part[...]
    maxima = []
    for block in range(blocks):
        lanes = slice(block * span, (block + 1) * span)
        pseudo = new_global[:, lanes]
        momentum = codes[:, lanes].astype(F32) * columns[:, block : block + 1]
        moved = MU * momentum + pseudo
        new_global[:, lanes] = glob[:, lanes] - RATE * (pseudo + MU * moved)
        scale = jnp.max(jnp.abs(moved), axis=-1, keepdims=True) + 1e-06
        new_codes[:, lanes] = (moved / scale).astype(BF16)
        maxima.append(jnp.broadcast_to(scale, (Y * rows, spread)))
    across = jnp.concatenate(maxima, axis=-1).T
    new_scales[...] = jnp.concatenate(
        [across[start : start + 1] for start in range(0, 128, spread)], axis=0
    )


def outer_update(place, parts, glob, codes, scales):
    vmem = pl.BlockSpec(memory_space=pltpu.VMEM)
    new_global, new_codes, new_scales = pl.pallas_call(
        outer_kernel,
        in_specs=[pl.BlockSpec(memory_space=pltpu.SMEM)] + [vmem] * (Y + 3),
        out_specs=[vmem] * 3,
        out_shape=[
            jax.ShapeDtypeStruct(glob.shape, F32),
            jax.ShapeDtypeStruct(codes.shape, BF16),
            jax.ShapeDtypeStruct(scales.shape[::-1], F32),
        ],
        compiler_params=params(),
        name="outer_update",
    )(place, *parts, glob, codes, scales.T)
    return new_global, new_codes, new_scales.T


def together(*values):
    return lax.optimization_barrier(values)


def body(
    activations,
    norm_gain,
    key_weight,
    key_cotangent,
    local_fragment,
    global_fragment,
    momentum_codes,
    momentum_scales,
):
    acts, weight, cot = activations[0], key_weight[0], key_cotangent[0]
    here, replica = lax.axis_index("fsdp"), lax.axis_index("replica")
    place = jnp.stack([here // (Z * C), (here // C) % Z, here % C, replica // H]).astype(jnp.int32)
    span = weight.shape[0]

    width = cot.shape[1]
    second = shift(weight, flip=1)
    near3, near1 = shift(weight, dx=1), shift(weight, dx=-1)
    rinv, *slots = normalise(place, acts, norm_gain, cot)
    *slots, second, near3, near1, glob = together(*slots, second, near3, near1, global_fragment)

    rows = [slots[0]] + [shift(slots[d], dx=d) for d in (1, 3, 2)]
    pair = jnp.concatenate([weight, second], axis=0)
    third = shift(pair, flip=2)
    near = jnp.concatenate([near1, near3], axis=0)
    keep, send = delta(place, glob, local_fragment[0])
    keep = keep + trade(send, flip=1)
    came = trade(keep[1], flip=3)
    early, first = backward_early(place, acts, norm_gain, rinv, cot, (), FIRST, (pair, near))
    *rows, third, came, early = together(*rows, third, came, early)

    rest = jnp.concatenate([second, third], axis=0)
    far3, far1 = shift(rest, dx=1), shift(rest, dx=-1)
    total = keep[0] + came
    other = shift(pack(place, rows, span, width), swap=1)
    kept, sent = wgrad_part(place, rows, other, span, width)
    base = jnp.concatenate([pair, third, near], axis=0)
    base_mate = shift(base, swap=1)
    early, sent = together(early, sent)
    early, second_part = backward_early(
        place, acts, norm_gain, rinv, cot, (early,), SECOND, (third, base_mate)
    )
    back = shift(sent, flip=1)
    far3, far1, back, early, total = together(far3, far1, back, early, total)

    across_a = shift(jnp.concatenate([near1, far1[:span]], axis=0), dx=-1)
    across_b = shift(far3[span:], dx=1)
    far = jnp.concatenate([far1, far3], axis=0)
    far_mate = shift(far, swap=1)
    last = (kept[1] + back[1].astype(F32)).astype(BF16)
    end = shift(last, flip=2)
    came = trade(total, far=1)
    early, third_part = backward_early(
        place, acts, norm_gain, rinv, cot, (early,), THIRD, (far, far_mate)
    )
    across_a, across_b, early, end, came = together(across_a, across_b, early, end, came)
    across = jnp.concatenate([across_a, across_b], axis=0)
    across_mate = shift(across, swap=1)
    pseudo = (total + came) / (Y * H)
    parts = [pseudo] + [trade(pseudo, flip=flip) for flip in range(1, Y)]
    weight_grad = kept[0] + back[0].astype(F32) + end.astype(F32)
    gain_here = lax.dynamic_slice_in_dim(norm_gain[0], here * span, span)
    gain_grad = jnp.sum(weight.astype(F32) * weight_grad, axis=-1) / gain_here
    across_mate, gain_grad = together(across_mate, gain_grad)
    keys, input_gradient_rows = backward_late(
        place, acts, norm_gain, rinv, cot, early, (first, second_part, third_part),
        (FIRST, SECOND, THIRD), LAST, (across, across_mate),
    )
    keys, *parts = together(keys, *parts)
    new_global, new_codes, new_scales = outer_update(
        place, parts, global_fragment, momentum_codes, momentum_scales
    )
    return (
        keys[None],
        weight_grad[None],
        gain_grad[None],
        input_gradient_rows[None],
        new_global,
        new_codes,
        new_scales,
    )


def solution(mesh):
    in_specs = (
        P("replica", "fsdp", None),
        P("replica", None),
        P("replica", "fsdp", None),
        P("replica", "fsdp", None),
        P("replica", "fsdp", None),
        P("fsdp", None),
        P("fsdp", None),
        P("fsdp", None),
    )
    out_specs = (
        P("replica", "fsdp", None),
        P("replica", "fsdp", None),
        P("replica", "fsdp"),
        P("replica", "fsdp", None),
        P("fsdp", None),
        P("fsdp", None),
        P("fsdp", None),
    )
    return jax.shard_map(body, mesh=mesh, in_specs=in_specs, out_specs=out_specs, check_vma=False)
```

time: 320 us -> 121 us (0.38); the launches traced: 316 us -> 120 us
  blocking collectives: 140 us -> 0 us
  waiting for transfers between devices: 117 us -> 27.5 us
  Pallas kernels: 0 us -> 38.2 us
  starting transfers between devices: 0.12 us -> 37.3 us
  matrix products: 22.2 us -> 0 us
  between operations: 16.2 us -> 0.91 us
  other arithmetic: 13.2 us -> 5.07 us
  local copies, waits for them, and re-layouts: 6.48 us -> 11.2 us
    unnamed x1 -> x0, blocking collectives: 140 us -> none
    psum x1 -> x0, waiting for transfers between devices: 117 us -> none  [body(): pseudo = lax.psum(delta, 'replica') / replicas]
    pallas_call x0 -> x9, Pallas kernels: none -> 38.2 us  [the longest x3 13.5 us: backward_early(): pl.pallas_call(functools.partial(early_kernel, layout, len(before)), in_s...]
    ppermute x0 -> x23, starting transfers between devices: none -> 37.3 us  [the longest x17 24.6 us: shift(): return lax.ppermute(value, 'fsdp', moves)]
    ppermute x0 -> x23, waiting for transfers between devices: none -> 27.5 us  [the longest x17 21.4 us: shift(): return lax.ppermute(value, 'fsdp', moves)]
    dot_general x3 -> x0, matrix products: 22.2 us -> none  [the longest x1 8.37 us: body(): lax.dot_general(grads, lax.all_gather(weight, 'fsdp', axis=0, tiled=True)...]
    unnamed x18 -> x40, local copies, waits for them, and re-layouts: 2.69 us -> 9.68 us
  transfers between devices with their start and end apart: 3 -> 23, of which waited for: 1 -> 7; matrix products, arithmetic and copies ran while one was open for 12% -> 8% of each run, Pallas kernels for 0% -> 27%
where the time goes in v1:
time: 121 us; the launch traced here: 120 us
  Pallas kernels  38.2 us (32%)
  starting transfers between devices  37.3 us (31%)
  waiting for transfers between devices  27.5 us (23%)
  local copies, waits for them, and re-layouts  11.2 us (9%)
  other arithmetic  5.07 us (4%)
    ppermute x17, starting transfers between devices, shift(): return lax.ppermute(value, 'fsdp', moves)  24.6 us
    ppermute x17, waiting for transfers between devices, shift(): return lax.ppermute(value, 'fsdp', moves)  21.4 us
    pallas_call x3, Pallas kernels, backward_early(): pl.pallas_call(functools.partial(early_kernel, layout, len(before)), in_s...  13.5 us
    ppermute x6, starting transfers between devices, trade(): return lax.ppermute(value, 'replica', moves)  12.7 us
    unnamed x40, local copies, waits for them, and re-layouts  9.68 us
    pallas_call x1, Pallas kernels, backward_late(): pl.pallas_call(functools.partial(late_kernel, layout, done), in_specs=[pl...  7.43 us
    ppermute x6, waiting for transfers between devices, trade(): return lax.ppermute(value, 'replica', moves)  6.11 us
    pallas_call x1, Pallas kernels, normalise(): pl.pallas_call(norm_kernel, grid_spec=pltpu.PrefetchScalarGridSpec(num_sc...  5.06 us
  transfers between devices with their start and end apart: 23, of which 7 were waited for; matrix products, arithmetic and copies ran while one was open for 8% of the time, Pallas kernels for 27%

profile of v1, /device:TPU:1, one launch (start us, length us, event | category | flops | bytes accessed | tf_op | source)
XLA Modules:
  0.0 120.2 jit_solution(1874654181397068218)
XLA Ops:
  0.6 3.4 %collective-permute-start.2 = (bf16[256,512]{1,0:T(8,128)(2,1)}, bf16[256,512]{1,0:T(8,128)(2,1)S(1)}, u32[]{:S(2)}, u32[]{:S(2)}) collective-permute-start(bf16[256,512]{1,0:T(8,128)(2,1)} %bitcast.42), channel_id=1, source_target_pairs={{0,24},{1,25},{2,26},{3,27},{4,28},{5,29},{6,30},{7,31},{8,0},{9,1... | collective-permute-start | bytes 786440 | tf_op jit(solution)/shard_map/ppermute | solution.py:41
  4.0 1.6 %collective-permute-start = (bf16[256,512]{1,0:T(8,128)(2,1)}, bf16[256,512]{1,0:T(8,128)(2,1)S(1)}, u32[]{:S(2)}, u32[]{:S(2)}) collective-permute-start(bf16[256,512]{1,0:T(8,128)(2,1)} %bitcast.44), channel_id=1, source_target_pairs={{0,2},{1,3},{2,0},{3,1},{4,6},{5,7},{6,4},{7,5},{8,10},{9,11},{10,... | collective-permute-start | bytes 786440 | tf_op jit(solution)/shard_map/ppermute | solution.py:41
  5.7 0.6 pad_add_fusion.place
  6.2 5.1 %normalise.1 = (f32[128,128]{1,0:T(8,128)}, bf16[128,2560]{1,0:T(8,128)(2,1)}, bf16[128,2560]{1,0:T(8,128)(2,1)}, bf16[128,2560]{1,0:T(8,128)(2,1)}, bf16[128,2560]{1,0:T(8,128)(2,1)}) custom-call(s32[4]{0:T(128)} %pad_add_fusion.place, bf16[128,8192]{1,0:T(8,128)(2,1)} %bitcast.32, f32[1,8192]{1,0:T(1,128)} %gain.9, bf16[128,512]{1,0:T(8,128)(2,1)} %bitcast.37), custom_call_target="tpu_custom_call" | custom-call | tf_op jit(solution)/shard_map/normalise/pallas_call | solution.py:71
  11.3 1.0 collective-permute-done.1
  12.3 2.7 %collective-permute-start.4 = (bf16[128,2560]{1,0:T(8,128)(2,1)}, bf16[128,2560]{1,0:T(8,128)(2,1)S(1)}, u32[]{:S(2)}, u32[]{:S(2)}) collective-permute-start(bf16[128,2560]{1,0:T(8,128)(2,1)} %get-tuple-element.70), channel_id=1, source_target_pairs={{0,24},{1,25},{2,26},{3,27},{4,28},{5,29},{6,30},{7,31},{8,0},{9,1... | collective-permute-start | bytes 1966088 | tf_op jit(solution)/shard_map/ppermute | solution.py:41
  15.2 2.1 %delta.1 = (f32[2,64,512]{2,1,0:T(8,128)}, f32[2,64,512]{2,1,0:T(8,128)}) custom-call(s32[4]{0:T(128)} %pad_add_fusion.place, f32[256,512]{1,0:T(8,128)} %glob.2, f32[256,512]{1,0:T(8,128)} %bitcast.46), custom_call_target="tpu_custom_call" | custom-call | tf_op jit(solution)/shard_map/delta/pallas_call | solution.py:308
  17.3 1.3 %collective-permute-start.7 = (f32[2,64,512]{2,1,0:T(8,128)}, f32[2,64,512]{2,1,0:T(8,128)S(1)}, u32[]{:S(2)}, u32[]{:S(2)}) collective-permute-start(f32[2,64,512]{2,1,0:T(8,128)} %get-tuple-element.74), channel_id=1, source_target_pairs={{0,64},{32,96},{64,0},{96,32},{128,192},{160,224},{192,128},{224,1... | collective-permute-start | bytes 786440 | tf_op jit(solution)/shard_map/ppermute | solution.py:46
  18.7 3.1 %collective-permute-start.6 = (bf16[512,512]{1,0:T(8,128)(2,1)S(1)}, bf16[512,512]{1,0:T(8,128)(2,1)S(1)}, u32[]{:S(2)}, u32[]{:S(2)}) collective-permute-start(bf16[512,512]{1,0:T(8,128)(2,1)S(1)} %pad_maximum_fusion.2.refs_0_), channel_id=1, source_target_pairs={{0,4},{1,5},{2,6},{3,7},{4,0},{5,1},{6,2},{7,3},{8,12},{9,13},{10,... | collective-permute-start | bytes 1572872 | tf_op jit(solution)/shard_map/ppermute | solution.py:41
  21.7 1.3 %collective-permute-done.7 = f32[2,64,512]{2,1,0:T(8,128)S(1)} collective-permute-done((f32[2,64,512]{2,1,0:T(8,128)}, f32[2,64,512]{2,1,0:T(8,128)S(1)}, u32[]{:S(2)}, u32[]{:S(2)}) %collective-permute-start.7) | collective-permute-done | bytes 262176 | tf_op jit(solution)/shard_map/ppermute | solution.py:46
  23.0 1.0 add.37
  24.0 2.8 %collective-permute-start.8 = (f32[64,512]{1,0:T(8,128)S(1)}, f32[64,512]{1,0:T(8,128)S(1)}, u32[]{:S(2)}, u32[]{:S(2)}) collective-permute-start(f32[64,512]{1,0:T(8,128)S(1)} %slice_bitcast_fusion.1), channel_id=1, source_target_pairs={{0,192},{32,224},{64,128},{96,160},{128,64},{160,96},{192,0},{224,... | collective-permute-start | bytes 393224 | tf_op jit(solution)/shard_map/ppermute | solution.py:46
  26.9 0.8 pad_maximum_fusion.refs_1_
  27.7 3.4 %backward_early.3 = (f32[128,512]{1,0:T(8,128)}, f32[4,128,256]{2,1,0:T(8,128)}) custom-call(s32[4]{0:T(128)} %pad_add_fusion.place, bf16[128,8192]{1,0:T(8,128)(2,1)} %bitcast.33, f32[1,8192]{1,0:T(1,128)} %gain.9, f32[128,128]{1,0:T(8,128)} %get-tuple-element.61.rinv, bf16[128,512]{1,0:T(8,128)(2,1)} %bitcast.38, bf16[512,512]{1,0:T(8,128)(2,1)} %copy-done.7, ...), custom_call_target="tpu_custom_call" | custom-call | tf_op jit(solution)/shard_map/backward_early/pallas_call | solution.py:205
  31.1 13.1 %collective-permute-done.6.refs_1_ = bf16[512,512]{1,0:T(8,128)(2,1)S(1)} collective-permute-done((bf16[512,512]{1,0:T(8,128)(2,1)S(1)}, bf16[512,512]{1,0:T(8,128)(2,1)S(1)}, u32[]{:S(2)}, u32[]{:S(2)}) %collective-permute-start.6) | collective-permute-done | bytes 524320 | tf_op jit(solution)/shard_map/ppermute | solution.py:41
  44.2 0.8 copy-done.1
  45.6 3.0 %pack.1 = bf16[512,1536]{1,0:T(8,128)(2,1)} custom-call(s32[4]{0:T(128)} %pad_add_fusion.place, bf16[128,2560]{1,0:T(8,128)(2,1)} %get-tuple-element.79.r0, bf16[128,2560]{1,0:T(8,128)(2,1)} %copy-done.1, bf16[128,2560]{1,0:T(8,128)(2,1)} %copy-done.2, bf16[128,2560]{1,0:T(8,128)(2,1)} %copy-done.3), custom_call_target="tpu_custom_call" | custom-call | tf_op jit(solution)/shard_map/pack/pallas_call | solution.py:107
  48.6 1.6 %collective-permute-start.11 = (bf16[512,1536]{1,0:T(8,128)(2,1)}, bf16[512,1536]{1,0:T(8,128)(2,1)S(1)}, u32[]{:S(2)}, u32[]{:S(2)}) collective-permute-start(bf16[512,1536]{1,0:T(8,128)(2,1)} %pack.1), channel_id=1, source_target_pairs={{0,1},{1,0},{2,3},{3,2},{4,5},{5,4},{6,7},{7,6},{8,9},{9,8},{10,11... | collective-permute-start | bytes 4718600 | tf_op jit(solution)/shard_map/ppermute | solution.py:41
  50.2 0.7 constant_dynamic-update-slice_fusion.6
  50.9 0.7 constant_dynamic-update-slice_fusion.5
  51.7 0.9 constant_dynamic-update-slice_fusion.4
  52.5 0.7 constant_dynamic-update-slice_fusion.3
  53.3 0.7 constant_dynamic-update-slice_fusion.2
  54.0 1.5 %collective-permute-start.10 = (bf16[768,512]{1,0:T(8,128)(2,1)S(1)}, bf16[768,512]{1,0:T(8,128)(2,1)S(1)}, u32[]{:S(2)}, u32[]{:S(2)}) collective-permute-start(bf16[768,512]{1,0:T(8,128)(2,1)S(1)} %get-tuple-element.118), channel_id=1, source_target_pairs={{0,24},{1,25},{2,26},{3,27},{4,28},{5,29},{6,30},{7,31},{8,0},{9,1... | collective-permute-start | bytes 2359304 | tf_op jit(solution)/shard_map/ppermute | solution.py:41
  55.5 1.2 copy-done.8
  56.7 4.4 %wgrad_part.1 = (f32[2,256,512]{2,1,0:T(8,128)}, bf16[2,256,512]{2,1,0:T(8,128)(2,1)}) custom-call(s32[4]{0:T(128)} %pad_add_fusion.place, bf16[128,2560]{1,0:T(8,128)(2,1)} %get-tuple-element.79.r0, bf16[128,2560]{1,0:T(8,128)(2,1)} %copy-done.1, bf16[128,2560]{1,0:T(8,128)(2,1)} %copy-done.2, bf16[128,2560]{1,0:T(8,128)(2,1)} %copy-done.3, ...), custom_call_target="tpu_custom_call" | custom-call | tf_op jit(solution)/shard_map/wgrad_part/pallas_call | solution.py:140
  61.0 1.6 %collective-permute-start.12 = (bf16[2,256,512]{2,1,0:T(8,128)(2,1)}, bf16[2,256,512]{2,1,0:T(8,128)(2,1)S(1)}, u32[]{:S(2)}, u32[]{:S(2)}) collective-permute-start(bf16[2,256,512]{2,1,0:T(8,128)(2,1)} %get-tuple-element.84), channel_id=1, source_target_pairs={{0,2},{1,3},{2,0},{3,1},{4,6},{5,7},{6,4},{7,5},{8,10},{9,11},{10,... | collective-permute-start | bytes 1572872 | tf_op jit(solution)/shard_map/ppermute | solution.py:41
  62.7 1.1 copy-done.9
  63.9 4.5 %backward_early.4 = (f32[128,512]{1,0:T(8,128)}, f32[8,128,256]{2,1,0:T(8,128)}) custom-call(s32[4]{0:T(128)} %pad_add_fusion.place, bf16[128,8192]{1,0:T(8,128)(2,1)} %bitcast.34, f32[1,8192]{1,0:T(1,128)} %gain.9, f32[128,128]{1,0:T(8,128)} %get-tuple-element.61.rinv, bf16[128,512]{1,0:T(8,128)(2,1)} %bitcast.39, f32[128,512]{1,0:T(8,128)} %get-tuple-element.85.refs_0_, ...), custom_call_target="tpu_custom_call" | custom-call | tf_op jit(solution)/shard_map/backward_early/pallas_call | solution.py:205
  68.4 4.2 %collective-permute-done.10 = bf16[768,512]{1,0:T(8,128)(2,1)S(1)} collective-permute-done((bf16[768,512]{1,0:T(8,128)(2,1)S(1)}, bf16[768,512]{1,0:T(8,128)(2,1)S(1)}, u32[]{:S(2)}, u32[]{:S(2)}) %collective-permute-start.10) | collective-permute-done | bytes 786464 | tf_op jit(solution)/shard_map/ppermute | solution.py:41
  72.6 2.4 %collective-permute-done.9 = bf16[768,512]{1,0:T(8,128)(2,1)S(1)} collective-permute-done((bf16[768,512]{1,0:T(8,128)(2,1)S(1)}, bf16[768,512]{1,0:T(8,128)(2,1)S(1)}, u32[]{:S(2)}, u32[]{:S(2)}) %collective-permute-start.9) | collective-permute-done | bytes 786464 | tf_op jit(solution)/shard_map/ppermute | solution.py:41
  75.1 1.8 %collective-permute-start.16 = (bf16[1536,512]{1,0:T(8,128)(2,1)S(1)}, bf16[1536,512]{1,0:T(8,128)(2,1)S(1)}, u32[]{:S(2)}, u32[]{:S(2)}) collective-permute-start(bf16[1536,512]{1,0:T(8,128)(2,1)S(1)} %constant_dynamic-update-slice_fusion.7.refs_1_), channel_id=1, source_target_pairs={{0,1},{1,0},{2,3},{3,2},{4,5},{5,4},{6,7},{7,6},{8,9},{9,8},{10,11... | collective-permute-start | bytes 4718600 | tf_op jit(solution)/shard_map/ppermute | solution.py:41
  77.0 2.7 %collective-permute-start.14 = (bf16[512,512]{1,0:T(8,128)(2,1)S(1)}, bf16[512,512]{1,0:T(8,128)(2,1)S(1)}, u32[]{:S(2)}, u32[]{:S(2)}) collective-permute-start(bf16[512,512]{1,0:T(8,128)(2,1)S(1)} %pad_maximum_fusion.1), channel_id=1, source_target_pairs={{0,24},{1,25},{2,26},{3,27},{4,28},{5,29},{6,30},{7,31},{8,0},{9,1... | collective-permute-start | bytes 1572872 | tf_op jit(solution)/shard_map/ppermute | solution.py:41
  79.8 3.1 %collective-permute-start.17 = (bf16[256,512]{1,0:T(8,128)(2,1)S(1)}, bf16[256,512]{1,0:T(8,128)(2,1)S(1)}, u32[]{:S(2)}, u32[]{:S(2)}) collective-permute-start(bf16[256,512]{1,0:T(8,128)(2,1)S(1)} %fusion), channel_id=1, source_target_pairs={{0,4},{1,5},{2,6},{3,7},{4,0},{5,1},{6,2},{7,3},{8,12},{9,13},{10,... | collective-permute-start | bytes 786440 | tf_op jit(solution)/shard_map/ppermute | solution.py:41
  82.9 5.1 %collective-permute-start.18 = (f32[64,512]{1,0:T(8,128)S(1)}, f32[64,512]{1,0:T(8,128)S(1)}, u32[]{:S(2)}, u32[]{:S(2)}) collective-permute-start(f32[64,512]{1,0:T(8,128)S(1)} %fusion.2), channel_id=1, source_target_pairs={{0,32},{32,0},{64,96},{96,64},{128,160},{160,128},{192,224},{224,1... | collective-permute-start | bytes 393224 | tf_op jit(solution)/shard_map/ppermute | solution.py:46
  88.0 1.2 %copy-done.10 = bf16[1536,512]{1,0:T(8,128)(2,1)} copy-done((bf16[1536,512]{1,0:T(8,128)(2,1)}, bf16[1536,512]{1,0:T(8,128)(2,1)S(1)}, u32[]{:S(2)}) %copy-start.10) | copy-done | bytes 1572888
  89.2 5.5 %backward_early.5 = (f32[128,512]{1,0:T(8,128)}, f32[12,128,256]{2,1,0:T(8,128)}) custom-call(s32[4]{0:T(128)} %pad_add_fusion.place, bf16[128,8192]{1,0:T(8,128)(2,1)} %bitcast.35, f32[1,8192]{1,0:T(1,128)} %gain.9, f32[128,128]{1,0:T(8,128)} %get-tuple-element.61.rinv, bf16[128,512]{1,0:T(8,128)(2,1)} %bitcast.40, f32[128,512]{1,0:T(8,128)} %get-tuple-element.90.refs_0_, ...), custom_call_target="tpu_custom_call" | custom-call | tf_op jit(solution)/shard_map/backward_early/pallas_call | solution.py:205
  94.7 4.8 %collective-permute-done.18 = f32[64,512]{1,0:T(8,128)S(1)} collective-permute-done((f32[64,512]{1,0:T(8,128)S(1)}, f32[64,512]{1,0:T(8,128)S(1)}, u32[]{:S(2)}, u32[]{:S(2)}) %collective-permute-start.18) | collective-permute-done | bytes 131104 | tf_op jit(solution)/shard_map/ppermute | solution.py:46
  99.5 0.7 collective-permute-done.17
  100.3 1.2 %collective-permute-start.19 = (bf16[1024,512]{1,0:T(8,128)(2,1)S(1)}, bf16[1024,512]{1,0:T(8,128)(2,1)S(1)}, u32[]{:S(2)}, u32[]{:S(2)}) collective-permute-start(bf16[1024,512]{1,0:T(8,128)(2,1)S(1)} %constant_dynamic-update-slice_fusion.9.refs_3_), channel_id=1, source_target_pairs={{0,1},{1,0},{2,3},{3,2},{4,5},{5,4},{6,7},{7,6},{8,9},{9,8},{10,11... | collective-permute-start | bytes 3145736 | tf_op jit(solution)/shard_map/ppermute | solution.py:41
  101.6 0.7 constant_dynamic-slice_fusion
  102.3 2.8 %collective-permute-start.22 = (f32[64,512]{1,0:T(8,128)S(1)}, f32[64,512]{1,0:T(8,128)S(1)}, u32[]{:S(2)}, u32[]{:S(2)}) collective-permute-start(f32[64,512]{1,0:T(8,128)S(1)} %add_multiply_fusion.p0), channel_id=1, source_target_pairs={{0,192},{32,224},{64,128},{96,160},{128,64},{160,96},{192,0},{224,... | collective-permute-start | bytes 393224 | tf_op jit(solution)/shard_map/ppermute | solution.py:46
  105.8 2.0 %fusion.1 = (f32[1,256,512]{2,1,0:T(8,128)}, f32[256]{0:T(256)S(1)}) fusion(bf16[256,512]{1,0:T(8,128)(2,1)S(1)} %collective-permute-done.17, bf16[2,256,512]{2,1,0:T(8,128)(2,1)S(1)} %collective-permute-done.12, f32[2,256,512]{2,1,0:T(8,128)} %get-tuple-element.92, bf16[1,256,512]{2,1,0:T(8,128)(2,1)S(1)} %copy-done.5), kind=kLoop, calls=%fused_computation.7 | loop fusion | flops 917248 | bytes 1836032 | tf_op jit(solution)/shard_map/broadcast_in_dim | solution.py:438
  107.7 0.6 div.40
  108.3 0.9 copy-done.11
  109.2 7.4 %backward_late.1 = (f32[128,512]{1,0:T(8,128)}, f32[128,8192]{1,0:T(8,128)}) custom-call(s32[4]{0:T(128)} %pad_add_fusion.place, bf16[128,8192]{1,0:T(8,128)(2,1)} %bitcast.36, f32[1,8192]{1,0:T(1,128)} %gain.9, f32[128,128]{1,0:T(8,128)} %get-tuple-element.61.rinv, bf16[128,512]{1,0:T(8,128)(2,1)} %bitcast.41, f32[128,512]{1,0:T(8,128)} %get-tuple-element.95.early, ...), custom_call_target="tpu_custom_call" | custom-call | tf_op jit(solution)/shard_map/backward_late/pallas_call | solution.py:277
  116.8 0.6 copy-done.14
  117.5 2.8 %outer_update.1 = (f32[256,512]{1,0:T(8,128)}, bf16[256,512]{1,0:T(8,128)(2,1)}, f32[4,256]{1,0:T(4,128)}) custom-call(s32[4]{0:T(128)} %pad_add_fusion.place, f32[64,512]{1,0:T(8,128)} %copy-done.13, f32[64,512]{1,0:T(8,128)} %copy-done.16, f32[64,512]{1,0:T(8,128)} %copy-done.15, f32[64,512]{1,0:T(8,128)} %copy-done.14, f32[256,512]{1,0:T(8,128)} %glob.2, ...), custom_call_target="tpu_custom_call" | custom-call | tf_op jit(solution)/shard_map/outer_update/pallas_call | solution.py:345
  (64 shorter events, 2.1 us)
Async XLA Ops:
  0.6 10.7 %collective-permute-start.2 = (bf16[256,512]{1,0:T(8,128)(2,1)}, bf16[256,512]{1,0:T(8,128)(2,1)S(1)}, u32[]{:S(2)}, u32[]{:S(2)}) collective-permute-start(bf16[256,512]{1,0:T(8,128)(2,1)} %bitcast.42), channel_id=1, source_target_pairs={{0,24},{1,25},{2,26},{3,27},{4,28},{5,29},{6,30},{7,31},{8,0},{9,1... | collective-permute-start | bytes 786440 | tf_op jit(solution)/shard_map/ppermute | solution.py:41
  4.0 8.3 %collective-permute-start.1 = (bf16[256,512]{1,0:T(8,128)(2,1)}, bf16[256,512]{1,0:T(8,128)(2,1)S(1)}, u32[]{:S(2)}, u32[]{:S(2)}) collective-permute-start(bf16[256,512]{1,0:T(8,128)(2,1)} %bitcast.43), channel_id=1, source_target_pairs={{0,8},{1,9},{2,10},{3,11},{4,12},{5,13},{6,14},{7,15},{8,16},{9,17... | collective-permute-start | bytes 786440 | tf_op jit(solution)/shard_map/ppermute | solution.py:41
  4.0 8.3 %collective-permute-start = (bf16[256,512]{1,0:T(8,128)(2,1)}, bf16[256,512]{1,0:T(8,128)(2,1)S(1)}, u32[]{:S(2)}, u32[]{:S(2)}) collective-permute-start(bf16[256,512]{1,0:T(8,128)(2,1)} %bitcast.44), channel_id=1, source_target_pairs={{0,2},{1,3},{2,0},{3,1},{4,6},{5,7},{6,4},{7,5},{8,10},{9,11},{10,... | collective-permute-start | bytes 786440 | tf_op jit(solution)/shard_map/ppermute | solution.py:41
  6.2 12.4 %copy-start.5 = (bf16[1,256,512]{2,1,0:T(8,128)(2,1)S(1)}, bf16[1,256,512]{2,1,0:T(8,128)(2,1)}, u32[]{:S(2)}) copy-start(bf16[1,256,512]{2,1,0:T(8,128)(2,1)} %param.10) | copy-start | bytes 786436
  12.3 31.9 %collective-permute-start.3 = (bf16[128,2560]{1,0:T(8,128)(2,1)}, bf16[128,2560]{1,0:T(8,128)(2,1)S(1)}, u32[]{:S(2)}, u32[]{:S(2)}) collective-permute-start(bf16[128,2560]{1,0:T(8,128)(2,1)} %get-tuple-element.69), channel_id=1, source_target_pairs={{0,8},{1,9},{2,10},{3,11},{4,12},{5,13},{6,14},{7,15},{8,16},{9,17... | collective-permute-start | bytes 1966088 | tf_op jit(solution)/shard_map/ppermute | solution.py:41
  12.3 31.9 %collective-permute-start.4 = (bf16[128,2560]{1,0:T(8,128)(2,1)}, bf16[128,2560]{1,0:T(8,128)(2,1)S(1)}, u32[]{:S(2)}, u32[]{:S(2)}) collective-permute-start(bf16[128,2560]{1,0:T(8,128)(2,1)} %get-tuple-element.70), channel_id=1, source_target_pairs={{0,24},{1,25},{2,26},{3,27},{4,28},{5,29},{6,30},{7,31},{8,0},{9,1... | collective-permute-start | bytes 1966088 | tf_op jit(solution)/shard_map/ppermute | solution.py:41
  15.0 29.3 %collective-permute-start.5 = (bf16[128,2560]{1,0:T(8,128)(2,1)}, bf16[128,2560]{1,0:T(8,128)(2,1)S(1)}, u32[]{:S(2)}, u32[]{:S(2)}) collective-permute-start(bf16[128,2560]{1,0:T(8,128)(2,1)} %get-tuple-element.71), channel_id=1, source_target_pairs={{0,16},{1,17},{2,18},{3,19},{4,20},{5,21},{6,22},{7,23},{8,24},{9,... | collective-permute-start | bytes 1966088 | tf_op jit(solution)/shard_map/ppermute | solution.py:41
  17.3 5.7 %collective-permute-start.7 = (f32[2,64,512]{2,1,0:T(8,128)}, f32[2,64,512]{2,1,0:T(8,128)S(1)}, u32[]{:S(2)}, u32[]{:S(2)}) collective-permute-start(f32[2,64,512]{2,1,0:T(8,128)} %get-tuple-element.74), channel_id=1, source_target_pairs={{0,64},{32,96},{64,0},{96,32},{128,192},{160,224},{192,128},{224,1... | collective-permute-start | bytes 786440 | tf_op jit(solution)/shard_map/ppermute | solution.py:46
  18.6 9.0 %copy-start.7 = (bf16[512,512]{1,0:T(8,128)(2,1)}, bf16[512,512]{1,0:T(8,128)(2,1)S(1)}, u32[]{:S(2)}) copy-start(bf16[512,512]{1,0:T(8,128)(2,1)S(1)} %pad_maximum_fusion.2.refs_0_) | copy-start | bytes 1572868
  18.7 25.5 %collective-permute-start.6 = (bf16[512,512]{1,0:T(8,128)(2,1)S(1)}, bf16[512,512]{1,0:T(8,128)(2,1)S(1)}, u32[]{:S(2)}, u32[]{:S(2)}) collective-permute-start(bf16[512,512]{1,0:T(8,128)(2,1)S(1)} %pad_maximum_fusion.2.refs_0_), channel_id=1, source_target_pairs={{0,4},{1,5},{2,6},{3,7},{4,0},{5,1},{6,2},{7,3},{8,12},{9,13},{10,... | collective-permute-start | bytes 1572872 | tf_op jit(solution)/shard_map/ppermute | solution.py:41
  24.0 7.1 %collective-permute-start.8 = (f32[64,512]{1,0:T(8,128)S(1)}, f32[64,512]{1,0:T(8,128)S(1)}, u32[]{:S(2)}, u32[]{:S(2)}) collective-permute-start(f32[64,512]{1,0:T(8,128)S(1)} %slice_bitcast_fusion.1), channel_id=1, source_target_pairs={{0,192},{32,224},{64,128},{96,160},{128,64},{160,96},{192,0},{224,... | collective-permute-start | bytes 393224 | tf_op jit(solution)/shard_map/ppermute | solution.py:46
  44.2 16.8 %copy-start.6 = (bf16[512,512]{1,0:T(8,128)(2,1)}, bf16[512,512]{1,0:T(8,128)(2,1)S(1)}, u32[]{:S(2)}) copy-start(bf16[512,512]{1,0:T(8,128)(2,1)S(1)} %collective-permute-done.6.refs_1_) | copy-start | bytes 1572868
  44.2 0.9 copy-start.1
  44.2 1.1 copy-start.2
  44.2 1.3 %copy-start.3 = (bf16[128,2560]{1,0:T(8,128)(2,1)}, bf16[128,2560]{1,0:T(8,128)(2,1)S(1)}, u32[]{:S(2)}) copy-start(bf16[128,2560]{1,0:T(8,128)(2,1)S(1)} %collective-permute-done.5.r3) | copy-start | bytes 1966084
  48.6 6.9 %collective-permute-start.11 = (bf16[512,1536]{1,0:T(8,128)(2,1)}, bf16[512,1536]{1,0:T(8,128)(2,1)S(1)}, u32[]{:S(2)}, u32[]{:S(2)}) collective-permute-start(bf16[512,1536]{1,0:T(8,128)(2,1)} %pack.1), channel_id=1, source_target_pairs={{0,1},{1,0},{2,3},{3,2},{4,5},{5,4},{6,7},{7,6},{8,9},{9,8},{10,11... | collective-permute-start | bytes 4718600 | tf_op jit(solution)/shard_map/ppermute | solution.py:41
  54.0 8.7 %collective-permute-start.13 = (bf16[1536,512]{1,0:T(8,128)(2,1)}, bf16[1536,512]{1,0:T(8,128)(2,1)S(1)}, u32[]{:S(2)}, u32[]{:S(2)}) collective-permute-start(bf16[1536,512]{1,0:T(8,128)(2,1)} %constant_dynamic-update-slice_fusion.2), channel_id=1, source_target_pairs={{0,1},{1,0},{2,3},{3,2},{4,5},{5,4},{6,7},{7,6},{8,9},{9,8},{10,11... | collective-permute-start | bytes 4718600 | tf_op jit(solution)/shard_map/ppermute | solution.py:41
  54.0 18.6 %collective-permute-start.10 = (bf16[768,512]{1,0:T(8,128)(2,1)S(1)}, bf16[768,512]{1,0:T(8,128)(2,1)S(1)}, u32[]{:S(2)}, u32[]{:S(2)}) collective-permute-start(bf16[768,512]{1,0:T(8,128)(2,1)S(1)} %get-tuple-element.118), channel_id=1, source_target_pairs={{0,24},{1,25},{2,26},{3,27},{4,28},{5,29},{6,30},{7,31},{8,0},{9,1... | collective-permute-start | bytes 2359304 | tf_op jit(solution)/shard_map/ppermute | solution.py:41
  55.4 19.5 %collective-permute-start.9 = (bf16[768,512]{1,0:T(8,128)(2,1)S(1)}, bf16[768,512]{1,0:T(8,128)(2,1)S(1)}, u32[]{:S(2)}, u32[]{:S(2)}) collective-permute-start(bf16[768,512]{1,0:T(8,128)(2,1)S(1)} %get-tuple-element.118), channel_id=1, source_target_pairs={{0,8},{1,9},{2,10},{3,11},{4,12},{5,13},{6,14},{7,15},{8,16},{9,17... | collective-permute-start | bytes 2359304 | tf_op jit(solution)/shard_map/ppermute | solution.py:41
  55.5 1.2 %copy-start.8 = (bf16[512,1536]{1,0:T(8,128)(2,1)}, bf16[512,1536]{1,0:T(8,128)(2,1)S(1)}, u32[]{:S(2)}) copy-start(bf16[512,1536]{1,0:T(8,128)(2,1)S(1)} %collective-permute-done.11.other) | copy-start | bytes 4718596
  61.0 13.9 %collective-permute-start.12 = (bf16[2,256,512]{2,1,0:T(8,128)(2,1)}, bf16[2,256,512]{2,1,0:T(8,128)(2,1)S(1)}, u32[]{:S(2)}, u32[]{:S(2)}) collective-permute-start(bf16[2,256,512]{2,1,0:T(8,128)(2,1)} %get-tuple-element.84), channel_id=1, source_target_pairs={{0,2},{1,3},{2,0},{3,1},{4,6},{5,7},{6,4},{7,5},{8,10},{9,11},{10,... | collective-permute-start | bytes 1572872 | tf_op jit(solution)/shard_map/ppermute | solution.py:41
  62.7 1.1 copy-start.9
  75.1 4.7 %copy-start = (bf16[1536,512]{1,0:T(8,128)(2,1)}, bf16[1536,512]{1,0:T(8,128)(2,1)S(1)}, u32[]{:S(2)}) copy-start(bf16[1536,512]{1,0:T(8,128)(2,1)S(1)} %constant_dynamic-update-slice_fusion.7.refs_1_) | copy-start | bytes 4718596
  75.1 4.6 %copy-start.12 = (f32[2,256,512]{2,1,0:T(8,128)S(1)}, f32[2,256,512]{2,1,0:T(8,128)}, u32[]{:S(2)}) copy-start(f32[2,256,512]{2,1,0:T(8,128)} %get-tuple-element.92) | copy-start | bytes 3145732
  75.1 12.9 %collective-permute-start.16 = (bf16[1536,512]{1,0:T(8,128)(2,1)S(1)}, bf16[1536,512]{1,0:T(8,128)(2,1)S(1)}, u32[]{:S(2)}, u32[]{:S(2)}) collective-permute-start(bf16[1536,512]{1,0:T(8,128)(2,1)S(1)} %constant_dynamic-update-slice_fusion.7.refs_1_), channel_id=1, source_target_pairs={{0,1},{1,0},{2,3},{3,2},{4,5},{5,4},{6,7},{7,6},{8,9},{9,8},{10,11... | collective-permute-start | bytes 4718600 | tf_op jit(solution)/shard_map/ppermute | solution.py:41
  77.0 23.3 %collective-permute-start.15 = (bf16[512,512]{1,0:T(8,128)(2,1)S(1)}, bf16[512,512]{1,0:T(8,128)(2,1)S(1)}, u32[]{:S(2)}, u32[]{:S(2)}) collective-permute-start(bf16[512,512]{1,0:T(8,128)(2,1)S(1)} %slice.27), channel_id=1, source_target_pairs={{0,8},{1,9},{2,10},{3,11},{4,12},{5,13},{6,14},{7,15},{8,16},{9,17... | collective-permute-start | bytes 1572872 | tf_op jit(solution)/shard_map/ppermute | solution.py:41
  77.0 23.2 %collective-permute-start.14 = (bf16[512,512]{1,0:T(8,128)(2,1)S(1)}, bf16[512,512]{1,0:T(8,128)(2,1)S(1)}, u32[]{:S(2)}, u32[]{:S(2)}) collective-permute-start(bf16[512,512]{1,0:T(8,128)(2,1)S(1)} %pad_maximum_fusion.1), channel_id=1, source_target_pairs={{0,24},{1,25},{2,26},{3,27},{4,28},{5,29},{6,30},{7,31},{8,0},{9,1... | collective-permute-start | bytes 1572872 | tf_op jit(solution)/shard_map/ppermute | solution.py:41
  79.8 20.5 %collective-permute-start.17 = (bf16[256,512]{1,0:T(8,128)(2,1)S(1)}, bf16[256,512]{1,0:T(8,128)(2,1)S(1)}, u32[]{:S(2)}, u32[]{:S(2)}) collective-permute-start(bf16[256,512]{1,0:T(8,128)(2,1)S(1)} %fusion), channel_id=1, source_target_pairs={{0,4},{1,5},{2,6},{3,7},{4,0},{5,1},{6,2},{7,3},{8,12},{9,13},{10,... | collective-permute-start | bytes 786440 | tf_op jit(solution)/shard_map/ppermute | solution.py:41
  82.9 16.6 %collective-permute-start.18 = (f32[64,512]{1,0:T(8,128)S(1)}, f32[64,512]{1,0:T(8,128)S(1)}, u32[]{:S(2)}, u32[]{:S(2)}) collective-permute-start(f32[64,512]{1,0:T(8,128)S(1)} %fusion.2), channel_id=1, source_target_pairs={{0,32},{32,0},{64,96},{96,64},{128,160},{160,128},{192,224},{224,1... | collective-permute-start | bytes 393224 | tf_op jit(solution)/shard_map/ppermute | solution.py:46
  88.0 1.2 %copy-start.10 = (bf16[1536,512]{1,0:T(8,128)(2,1)}, bf16[1536,512]{1,0:T(8,128)(2,1)S(1)}, u32[]{:S(2)}) copy-start(bf16[1536,512]{1,0:T(8,128)(2,1)S(1)} %collective-permute-done.16.refs_2_) | copy-start | bytes 4718596
  100.3 8.0 %copy-start.4 = (bf16[1024,512]{1,0:T(8,128)(2,1)}, bf16[1024,512]{1,0:T(8,128)(2,1)S(1)}, u32[]{:S(2)}) copy-start(bf16[1024,512]{1,0:T(8,128)(2,1)S(1)} %constant_dynamic-update-slice_fusion.9.refs_3_) | copy-start | bytes 3145732
  100.3 7.9 %collective-permute-start.19 = (bf16[1024,512]{1,0:T(8,128)(2,1)S(1)}, bf16[1024,512]{1,0:T(8,128)(2,1)S(1)}, u32[]{:S(2)}, u32[]{:S(2)}) collective-permute-start(bf16[1024,512]{1,0:T(8,128)(2,1)S(1)} %constant_dynamic-update-slice_fusion.9.refs_3_), channel_id=1, source_target_pairs={{0,1},{1,0},{2,3},{3,2},{4,5},{5,4},{6,7},{7,6},{8,9},{9,8},{10,11... | collective-permute-start | bytes 3145736 | tf_op jit(solution)/shard_map/ppermute | solution.py:41
  102.3 14.4 %copy-start.13 = (f32[64,512]{1,0:T(8,128)}, f32[64,512]{1,0:T(8,128)S(1)}, u32[]{:S(2)}) copy-start(f32[64,512]{1,0:T(8,128)S(1)} %add_multiply_fusion.p0) | copy-start | bytes 393220
  102.3 14.4 %collective-permute-start.22 = (f32[64,512]{1,0:T(8,128)S(1)}, f32[64,512]{1,0:T(8,128)S(1)}, u32[]{:S(2)}, u32[]{:S(2)}) collective-permute-start(f32[64,512]{1,0:T(8,128)S(1)} %add_multiply_fusion.p0), channel_id=1, source_target_pairs={{0,192},{32,224},{64,128},{96,160},{128,64},{160,96},{192,0},{224,... | collective-permute-start | bytes 393224 | tf_op jit(solution)/shard_map/ppermute | solution.py:46
  105.1 11.6 %collective-permute-start.21 = (f32[64,512]{1,0:T(8,128)S(1)}, f32[64,512]{1,0:T(8,128)S(1)}, u32[]{:S(2)}, u32[]{:S(2)}) collective-permute-start(f32[64,512]{1,0:T(8,128)S(1)} %add_multiply_fusion.p0), channel_id=1, source_target_pairs={{0,128},{32,160},{64,192},{96,224},{128,0},{160,32},{192,64},{224,... | collective-permute-start | bytes 393224 | tf_op jit(solution)/shard_map/ppermute | solution.py:46
  105.4 11.3 %collective-permute-start.20 = (f32[64,512]{1,0:T(8,128)S(1)}, f32[64,512]{1,0:T(8,128)S(1)}, u32[]{:S(2)}, u32[]{:S(2)}) collective-permute-start(f32[64,512]{1,0:T(8,128)S(1)} %add_multiply_fusion.p0), channel_id=1, source_target_pairs={{0,64},{32,96},{64,0},{96,32},{128,192},{160,224},{192,128},{224,1... | collective-permute-start | bytes 393224 | tf_op jit(solution)/shard_map/ppermute | solution.py:46
  108.3 1.0 copy-start.11
  116.7 0.6 copy-start.14
  116.7 0.7 copy-start.15
  116.8 0.7 copy-start.16

commit v2 on v1

--- a/solution.py
+++ b/solution.py
@@ -13,15 +13,20 @@
 X, Z, C = 4, 4, 2
 Y, H = 4, 2
 OFFSETS = (0, 1, 3, 2)
-FIRST = ((0, (0, 1), (0, 0), None), (1, (0,), (1, 0), None), (2, (0,), (1, 1), None))
+FIRST = (
+    (0, (0,), (0, 0), None),
+    (0, (1,), (1, 0), None),
+    (1, (0,), (2, 0), None),
+    (2, (0,), (3, 0), None),
+)
 SECOND = (
-    (0, (2, 3), (0, 0), (1, 2)),
+    (0, (2, 3), (0, 0), (2, 0)),
     (0, (0, 1), None, (1, 0)),
-    (1, (0,), None, (1, 4)),
-    (2, (0,), None, (1, 5)),
+    (1, (0,), None, (1, 2)),
+    (2, (0,), None, (1, 3)),
 )
 THIRD = ((1, (1, 2, 3), (0, 0), (1, 0)), (2, (1, 2, 3), (0, 3), (1, 3)))
-LAST = ((3, (0, 1, 2, 3), (0, 0), (1, 0)),)
+LAST = ((3, (0, 1), (0, 0), (1, 0)), (3, (2, 3), (2, 0), (3, 0)))
 VMEM_LIMIT = 56 * 1024 * 1024
 F32 = jnp.float32
 BF16 = jnp.bfloat16
@@ -55,17 +60,22 @@
     inverse = lax.rsqrt(jnp.mean(value * value, axis=-1, keepdims=True) + EPS)
     rinv[...] = jnp.broadcast_to(inverse, rinv.shape)
     width = acts.shape[1] // X
+    span = width // (Z * C)
     for step in range(X):
-        start = pl.multiple_of(lax.rem(place[0] + step, X) * width, width)
-        part = acts[:, pl.ds(start, width)].astype(F32) * inverse
-        slots[step][:, :width] = (part * gain[:, pl.ds(start, width)]).astype(BF16)
+        base = lax.rem(place[0] + step, X) * width
+        for number in range(Z * C):
+            core, flip = number // Z, number % Z
+            local = (place[1] ^ flip) * (C * span) + (place[2] ^ core) * span
+            lanes = pl.ds(pl.multiple_of(base + local, span), span)
+            part = acts[:, lanes].astype(F32) * inverse
+            slots[step][:, number * span : (number + 1) * span] = (part * gain[:, lanes]).astype(BF16)
         slots[step][:, width:] = cot[...]
 
 
 def normalise(place, acts, gain, cot):
     tokens, width = acts.shape
     keys = cot.shape[1]
-    rows = 32
+    rows = 64
     part = width // X + keys
     whole = lambda i, place: (0, 0)
     return pl.pallas_call(
@@ -88,66 +98,78 @@
     )(place, acts, gain, cot)
 
 
-def pack_kernel(span, place, r0, r1, r2, r3, features):
+def pack_kernel(r0, r1, r2, r3, second, third, features, rest, wide, blocks, arrive, leave):
     tokens = r0.shape[0]
-    width = Z * C * span
+    skip = r0.shape[1] - features.shape[1]
+    span = second.shape[0]
+    moves = [
+        (second, blocks.at[pl.ds(0, span)], rest.at[pl.ds(0, span)]),
+        (third, blocks.at[pl.ds(span, third.shape[0])], rest.at[pl.ds(span, third.shape[0])]),
+    ]
     for number, r in enumerate((r0, r1, r2, r3)):
-        part = slice(number * tokens, (number + 1) * tokens)
-        for flip in range(Z):
-            start = (place[1] ^ flip) * (C * span) + (1 - place[2]) * span
-            features[part, flip * span : (flip + 1) * span] = r[
-                :, pl.ds(pl.multiple_of(start, span), span)
-            ]
-        features[part, Z * span :] = r[:, width:]
-
-
-def pack(place, rows, span, keys):
-    tokens = rows[0].shape[0] * X
-    vmem = pl.BlockSpec(memory_space=pltpu.VMEM)
-    return pl.pallas_call(
-        functools.partial(pack_kernel, span),
-        in_specs=[pl.BlockSpec(memory_space=pltpu.SMEM)] + [vmem] * X,
-        out_specs=vmem,
-        out_shape=jax.ShapeDtypeStruct((tokens, Z * span + keys), BF16),
+        part = pl.ds(number * tokens, tokens)
+        moves.append((r.at[:, pl.ds(skip, features.shape[1])], wide.at[part], features.at[part]))
+    loads = [pltpu.make_async_copy(m[0], m[1], arrive.at[i]) for i, m in enumerate(moves)]
+    stores = [pltpu.make_async_copy(m[1], m[2], leave.at[i]) for i, m in enumerate(moves)]
+    for load in loads:
+        load.start()
+    for load, store in zip(loads, stores):
+        load.wait()
+        store.start()
+    for store in stores:
+        store.wait()
+
+
+def pack(rows, second, third, span):
+    tokens, width = rows[0].shape
+    hbm = pl.BlockSpec(memory_space=pl.ANY)
+    shapes = [
+        (X * tokens, width - Z * span),
+        (second.shape[0] + third.shape[0], second.shape[1]),
+    ]
+    return pl.pallas_call(
+        pack_kernel,
+        in_specs=[hbm] * (X + 2),
+        out_specs=[hbm] * 2,
+        out_shape=[jax.ShapeDtypeStruct(shape, BF16) for shape in shapes],
+        scratch_shapes=[pltpu.VMEM(shape, BF16) for shape in shapes]
+        + [pltpu.SemaphoreType.DMA((X + 2,))] * 2,
         compiler_params=params(),
         name="pack",
-    )(place, *rows)
-
-
-def wgrad_kernel(place, r0, r1, r2, r3, other, kept, sent):
-    span, keys = kept.shape[1:]
-    width = Z * C * span
+    )(*rows, second, third)
+
+
+def wgrad_kernel(r0, r1, r2, r3, other, kept, sent1, sent3):
+    span = kept.shape[1]
+    own, width = Z * span, Z * C * span
     mine = (r0, r1, r2, r3)
-    cots = jnp.concatenate([r[:, width:] for r in mine] + [other[:, Z * span :]], axis=0)
+    cots = jnp.concatenate([r[:, width:] for r in mine] + [other[:, own:]], axis=0)
     for flip in range(Z):
-        start = pl.multiple_of((place[1] ^ flip) * (C * span) + place[2] * span, span)
-        rows = jnp.concatenate(
-            [r[:, pl.ds(start, span)] for r in mine]
-            + [other[:, flip * span : (flip + 1) * span]],
-            axis=0,
-        )
+        lanes = slice(flip * span, (flip + 1) * span)
+        rows = jnp.concatenate([r[:, lanes] for r in mine] + [other[:, lanes]], axis=0)
         total = lax.dot_general(
             rows, cots, (((0,), (0,)), ((), ())), preferred_element_type=F32
         )
         if flip % 2:
-            sent[flip // 2] = total.astype(BF16)
+            (sent3 if flip == 3 else sent1)[...] = total.astype(BF16)
         else:
             kept[flip // 2] = total
 
 
-def wgrad_part(place, rows, other, span, keys):
+def wgrad_part(rows, other, span, keys):
     vmem = pl.BlockSpec(memory_space=pltpu.VMEM)
     return pl.pallas_call(
         wgrad_kernel,
-        in_specs=[pl.BlockSpec(memory_space=pltpu.SMEM)] + [vmem] * (X + 1),
-        out_specs=[vmem] * 2,
+        in_specs=[vmem] * (X + 1),
+        out_specs=[vmem] * 3,
         out_shape=[
             jax.ShapeDtypeStruct((2, span, keys), F32),
-            jax.ShapeDtypeStruct((2, span, keys), BF16),
+            jax.ShapeDtypeStruct((span, keys), BF16),
+            jax.ShapeDtypeStruct((span, keys), BF16),
         ],
         compiler_params=params(),
         name="wgrad_part",
-    )(place, *rows, other)
+    )(*rows, other)
 
 
 def pieces_of(layout, refs, place, part):
@@ -184,8 +206,12 @@
     )
 
 
-def early_kernel(layout, started, place, acts, gain, rinv, cot, *refs):
-    weights, (keys, scaled) = refs[started:-2], refs[-2:]
+def early_kernel(layout, started, hold, place, acts, gain, rinv, cot, *refs):
+    weights, (keys, scaled) = refs[started : -2 - hold], refs[-2 - hold :][:2]
+    if hold:
+        span = weights[0].shape[0]
+        for number, ref in enumerate(weights):
+            refs[-1][number * span : (number + 1) * span, :] = ref[...]
     part = acts.shape[1] // X
     inverse = rinv[:, :1]
     pieces = pieces_of(layout, weights, place, part)
@@ -197,20 +223,21 @@
         scaled[number] = inverse * cotangent_of(cots, ref, rows) * gain[:, pl.ds(start, span)]
 
 
-def backward_early(place, acts, gain, rinv, cot, before, layout, weights):
+def backward_early(place, acts, gain, rinv, cot, before, layout, weights, hold=0):
     tokens, width = acts.shape
     span = width // (X * Z * C)
     pieces = sum(len(flips) * (2 - sources.count(None)) for _, flips, *sources in layout)
     vmem = pl.BlockSpec(memory_space=pltpu.VMEM)
     return pl.pallas_call(
-        functools.partial(early_kernel, layout, len(before)),
+        functools.partial(early_kernel, layout, len(before), hold),
         in_specs=[pl.BlockSpec(memory_space=pltpu.SMEM)]
         + [vmem] * (4 + len(before) + len(weights)),
-        out_specs=[vmem, vmem],
+        out_specs=[vmem] * (2 + hold),
         out_shape=[
             jax.ShapeDtypeStruct((tokens, cot.shape[1]), F32),
             jax.ShapeDtypeStruct((pieces, tokens, span), F32),
-        ],
+        ]
+        + [jax.ShapeDtypeStruct((len(weights) * span, cot.shape[1]), BF16)] * hold,
         compiler_params=params(),
         name="backward_early",
     )(place, acts, gain, rinv, cot, *before, *weights)
@@ -383,51 +410,50 @@
     *slots, second, near3, near1, glob = together(*slots, second, near3, near1, global_fragment)
 
     rows = [slots[0]] + [shift(slots[d], dx=d) for d in (1, 3, 2)]
-    pair = jnp.concatenate([weight, second], axis=0)
-    third = shift(pair, flip=2)
-    near = jnp.concatenate([near1, near3], axis=0)
+    third = shift(jnp.concatenate([weight, second], axis=0), flip=2)
     keep, send = delta(place, glob, local_fragment[0])
     keep = keep + trade(send, flip=1)
     came = trade(keep[1], flip=3)
-    early, first = backward_early(place, acts, norm_gain, rinv, cot, (), FIRST, (pair, near))
+    early, first, hold = backward_early(
+        place, acts, norm_gain, rinv, cot, (), FIRST, (weight, second, near1, near3), hold=1
+    )
     *rows, third, came, early = together(*rows, third, came, early)
 
-    rest = jnp.concatenate([second, third], axis=0)
+    other, rest = pack(rows, second, third, span)
+    other = shift(other, swap=1)
     far3, far1 = shift(rest, dx=1), shift(rest, dx=-1)
     total = keep[0] + came
-    other = shift(pack(place, rows, span, width), swap=1)
-    kept, sent = wgrad_part(place, rows, other, span, width)
-    base = jnp.concatenate([pair, third, near], axis=0)
-    base_mate = shift(base, swap=1)
-    early, sent = together(early, sent)
+    kept, sent1, sent3 = wgrad_part(rows, other, span, width)
+    hold_mate, third_mate = shift(hold, swap=1), shift(third, swap=1)
+    early, sent1 = together(early, sent1)
     early, second_part = backward_early(
-        place, acts, norm_gain, rinv, cot, (early,), SECOND, (third, base_mate)
-    )
-    back = shift(sent, flip=1)
-    far3, far1, back, early, total = together(far3, far1, back, early, total)
+        place, acts, norm_gain, rinv, cot, (early,), SECOND, (third, hold_mate, third_mate)
+    )
+    back3 = shift(sent3, flip=1)
+    far3, far1, early, total, back3 = together(far3, far1, early, total, back3)
 
     across_a = shift(jnp.concatenate([near1, far1[:span]], axis=0), dx=-1)
     across_b = shift(far3[span:], dx=1)
     far = jnp.concatenate([far1, far3], axis=0)
     far_mate = shift(far, swap=1)
-    last = (kept[1] + back[1].astype(F32)).astype(BF16)
+    came = trade(total, far=1)
+    last = (kept[1] + back3.astype(F32)).astype(BF16)
     end = shift(last, flip=2)
-    came = trade(total, far=1)
+    back1 = shift(sent1, flip=1)
     early, third_part = backward_early(
         place, acts, norm_gain, rinv, cot, (early,), THIRD, (far, far_mate)
     )
-    across_a, across_b, early, end, came = together(across_a, across_b, early, end, came)
-    across = jnp.concatenate([across_a, across_b], axis=0)
-    across_mate = shift(across, swap=1)
+    early, end, back1 = together(early, end, back1)
+    weight_grad = kept[0] + back1.astype(F32) + end.astype(F32)
+    gain_here = lax.dynamic_slice_in_dim(norm_gain[0], here * span, span)
+    gain_grad = jnp.sum(weight.astype(F32) * weight_grad, axis=-1) / gain_here
+    across_a, across_b, early, gain_grad, came = together(across_a, across_b, early, gain_grad, came)
+    mate_a, mate_b = shift(across_a, swap=1), shift(across_b, swap=1)
     pseudo = (total + came) / (Y * H)
     parts = [pseudo] + [trade(pseudo, flip=flip) for flip in range(1, Y)]
-    weight_grad = kept[0] + back[0].astype(F32) + end.astype(F32)
-    gain_here = lax.dynamic_slice_in_dim(norm_gain[0], here * span, span)
-    gain_grad = jnp.sum(weight.astype(F32) * weight_grad, axis=-1) / gain_here
-    across_mate, gain_grad = together(across_mate, gain_grad)
     keys, input_gradient_rows = backward_late(
         place, acts, norm_gain, rinv, cot, early, (first, second_part, third_part),
-        (FIRST, SECOND, THIRD), LAST, (across, across_mate),
+        (FIRST, SECOND, THIRD), LAST, (across_a, mate_a, across_b, mate_b),
     )
     keys, *parts = together(keys, *parts)
     new_global, new_codes, new_scales = outer_update(

time: 121 us -> 114 us (0.942)
  waiting for transfers between devices: 27.5 us -> 22.3 us
  local copies, waits for them, and re-layouts: 11.2 us -> 8.72 us
  starting transfers between devices: 37.3 us -> 38.8 us
  Pallas kernels: 38.2 us -> 36.8 us
    ppermute x6, waiting for transfers between devices: 6.11 us -> 1.33 us  [trade(): return lax.ppermute(value, 'replica', moves)]
    unnamed x40 -> x53, local copies, waits for them, and re-layouts: 9.68 us -> 7.13 us
    ppermute x17 -> x20, starting transfers between devices: 24.6 us -> 26.1 us  [shift(): return lax.ppermute(value, 'fsdp', moves)]
    ppermute x17 -> x20, waiting for transfers between devices: 21.4 us -> 21 us  [shift(): return lax.ppermute(value, 'fsdp', moves)]
  transfers between devices with their start and end apart: 23 -> 26, of which waited for: 7 -> 6; matrix products, arithmetic and copies ran while one was open for 8% -> 6% of each run, Pallas kernels for 27% -> 28%
where the time goes in v2:
time: 114 us; the launch traced here: 113 us
  starting transfers between devices  38.8 us (34%)
  Pallas kernels  36.8 us (32%)
  waiting for transfers between devices  22.3 us (20%)
  local copies, waits for them, and re-layouts  8.72 us (8%)
  other arithmetic  5.68 us (5%)
    ppermute x20, starting transfers between devices, shift(): return lax.ppermute(value, 'fsdp', moves)  26.1 us
    ppermute x20, waiting for transfers between devices, shift(): return lax.ppermute(value, 'fsdp', moves)  21 us
    pallas_call x3, Pallas kernels, backward_early(): pl.pallas_call(functools.partial(early_kernel, layout, len(before), hold)...  13.8 us
    ppermute x6, starting transfers between devices, trade(): return lax.ppermute(value, 'replica', moves)  12.7 us
    pallas_call x1, Pallas kernels, backward_late(): pl.pallas_call(functools.partial(late_kernel, layout, done), in_specs=[pl...  7.4 us
    unnamed x53, local copies, waits for them, and re-layouts  7.13 us
    pallas_call x1, Pallas kernels, wgrad_part(): pl.pallas_call(wgrad_kernel, in_specs=[vmem] * (X + 1), out_specs=[vmem]...  4.25 us
    pallas_call x1, Pallas kernels, normalise(): pl.pallas_call(norm_kernel, grid_spec=pltpu.PrefetchScalarGridSpec(num_sc...  3.96 us
  transfers between devices with their start and end apart: 26, of which 6 were waited for; matrix products, arithmetic and copies ran while one was open for 6% of the time, Pallas kernels for 28%

profile of v2, /device:TPU:1, one launch (start us, length us, event | category | flops | bytes accessed | tf_op | source)
XLA Modules:
  0.0 113.3 jit_solution(12641324877353776941)
XLA Ops:
  0.6 2.6 %collective-permute-start = (bf16[256,512]{1,0:T(8,128)(2,1)}, bf16[256,512]{1,0:T(8,128)(2,1)S(1)}, u32[]{:S(2)}, u32[]{:S(2)}) collective-permute-start(bf16[256,512]{1,0:T(8,128)(2,1)} %bitcast.45), channel_id=1, source_target_pairs={{0,2},{1,3},{2,0},{3,1},{4,6},{5,7},{6,4},{7,5},{8,10},{9,11},{10,... | collective-permute-start | bytes 786440 | tf_op jit(solution)/shard_map/ppermute | solution.py:46
  3.2 1.2 %collective-permute-start.1 = (bf16[256,512]{1,0:T(8,128)(2,1)}, bf16[256,512]{1,0:T(8,128)(2,1)S(1)}, u32[]{:S(2)}, u32[]{:S(2)}) collective-permute-start(bf16[256,512]{1,0:T(8,128)(2,1)} %bitcast.46), channel_id=1, source_target_pairs={{0,8},{1,9},{2,10},{3,11},{4,12},{5,13},{6,14},{7,15},{8,16},{9,17... | collective-permute-start | bytes 786440 | tf_op jit(solution)/shard_map/ppermute | solution.py:46
  4.4 1.5 %collective-permute-start.2 = (bf16[256,512]{1,0:T(8,128)(2,1)}, bf16[256,512]{1,0:T(8,128)(2,1)S(1)}, u32[]{:S(2)}, u32[]{:S(2)}) collective-permute-start(bf16[256,512]{1,0:T(8,128)(2,1)} %bitcast.47), channel_id=1, source_target_pairs={{0,24},{1,25},{2,26},{3,27},{4,28},{5,29},{6,30},{7,31},{8,0},{9,1... | collective-permute-start | bytes 786440 | tf_op jit(solution)/shard_map/ppermute | solution.py:46
  5.9 0.6 pad_add_fusion.place
  6.5 4.0 %normalise.1 = (f32[128,128]{1,0:T(8,128)}, bf16[128,2560]{1,0:T(8,128)(2,1)}, bf16[128,2560]{1,0:T(8,128)(2,1)}, bf16[128,2560]{1,0:T(8,128)(2,1)}, bf16[128,2560]{1,0:T(8,128)(2,1)}) custom-call(s32[4]{0:T(128)} %pad_add_fusion.place, bf16[128,8192]{1,0:T(8,128)(2,1)} %bitcast.35, f32[1,8192]{1,0:T(1,128)} %gain.9, bf16[128,512]{1,0:T(8,128)(2,1)} %bitcast.40), custom_call_target="tpu_custom_call" | custom-call | tf_op jit(solution)/shard_map/normalise/pallas_call | solution.py:81
  10.4 1.0 collective-permute-done.1.refs_3_
  11.5 0.9 collective-permute-start.3
  12.4 1.8 %collective-permute-start.4 = (bf16[128,2560]{1,0:T(8,128)(2,1)}, bf16[128,2560]{1,0:T(8,128)(2,1)S(1)}, u32[]{:S(2)}, u32[]{:S(2)}) collective-permute-start(bf16[128,2560]{1,0:T(8,128)(2,1)} %get-tuple-element.74), channel_id=1, source_target_pairs={{0,24},{1,25},{2,26},{3,27},{4,28},{5,29},{6,30},{7,31},{8,0},{9,1... | collective-permute-start | bytes 1966088 | tf_op jit(solution)/shard_map/ppermute | solution.py:46
  14.2 0.9 collective-permute-start.5
  15.1 2.1 %delta.1 = (f32[2,64,512]{2,1,0:T(8,128)}, f32[2,64,512]{2,1,0:T(8,128)}) custom-call(s32[4]{0:T(128)} %pad_add_fusion.place, f32[256,512]{1,0:T(8,128)} %glob.2, f32[256,512]{1,0:T(8,128)} %bitcast.50), custom_call_target="tpu_custom_call" | custom-call | tf_op jit(solution)/shard_map/delta/pallas_call | solution.py:335
  17.1 1.3 %collective-permute-start.7 = (f32[2,64,512]{2,1,0:T(8,128)}, f32[2,64,512]{2,1,0:T(8,128)S(1)}, u32[]{:S(2)}, u32[]{:S(2)}) collective-permute-start(f32[2,64,512]{2,1,0:T(8,128)} %get-tuple-element.79), channel_id=1, source_target_pairs={{0,64},{32,96},{64,0},{96,32},{128,192},{160,224},{192,128},{224,1... | collective-permute-start | bytes 786440 | tf_op jit(solution)/shard_map/ppermute | solution.py:51
  18.5 3.1 %collective-permute-start.6 = (bf16[512,512]{1,0:T(8,128)(2,1)S(1)}, bf16[512,512]{1,0:T(8,128)(2,1)S(1)}, u32[]{:S(2)}, u32[]{:S(2)}) collective-permute-start(bf16[512,512]{1,0:T(8,128)(2,1)S(1)} %pad_maximum_fusion), channel_id=1, source_target_pairs={{0,4},{1,5},{2,6},{3,7},{4,0},{5,1},{6,2},{7,3},{8,12},{9,13},{10,... | collective-permute-start | bytes 1572872 | tf_op jit(solution)/shard_map/ppermute | solution.py:46
  21.6 1.3 %collective-permute-done.7 = f32[2,64,512]{2,1,0:T(8,128)S(1)} collective-permute-done((f32[2,64,512]{2,1,0:T(8,128)}, f32[2,64,512]{2,1,0:T(8,128)S(1)}, u32[]{:S(2)}, u32[]{:S(2)}) %collective-permute-start.7) | collective-permute-done | bytes 262176 | tf_op jit(solution)/shard_map/ppermute | solution.py:51
  22.9 1.0 add.33
  23.9 2.8 %collective-permute-start.8 = (f32[64,512]{1,0:T(8,128)S(1)}, f32[64,512]{1,0:T(8,128)S(1)}, u32[]{:S(2)}, u32[]{:S(2)}) collective-permute-start(f32[64,512]{1,0:T(8,128)S(1)} %slice_bitcast_fusion.1), channel_id=1, source_target_pairs={{0,192},{32,224},{64,128},{96,160},{128,64},{160,96},{192,0},{224,... | collective-permute-start | bytes 393224 | tf_op jit(solution)/shard_map/ppermute | solution.py:51
  26.7 3.8 %backward_early.3 = (f32[128,512]{1,0:T(8,128)}, f32[4,128,256]{2,1,0:T(8,128)}, bf16[1024,512]{1,0:T(8,128)(2,1)}) custom-call(s32[4]{0:T(128)} %pad_add_fusion.place, bf16[128,8192]{1,0:T(8,128)(2,1)} %bitcast.36, f32[1,8192]{1,0:T(1,128)} %gain.9, f32[128,128]{1,0:T(8,128)} %get-tuple-element.66.rinv, bf16[128,512]{1,0:T(8,128)(2,1)} %bitcast.41, ...), custom_call_target="tpu_custom_call" | custom-call | tf_op jit(solution)/shard_map/backward_early/pallas_call | solution.py:231
  30.5 14.6 %collective-permute-done.6.third.refs_1_ = bf16[512,512]{1,0:T(8,128)(2,1)S(1)} collective-permute-done((bf16[512,512]{1,0:T(8,128)(2,1)S(1)}, bf16[512,512]{1,0:T(8,128)(2,1)S(1)}, u32[]{:S(2)}, u32[]{:S(2)}) %collective-permute-start.6) | collective-permute-done | bytes 524320 | tf_op jit(solution)/shard_map/ppermute | solution.py:46
  45.1 0.7 copy-done.7
  46.5 2.6 %pack.1 = (bf16[512,1536]{1,0:T(8,128)(2,1)}, bf16[768,512]{1,0:T(8,128)(2,1)}) custom-call(bf16[128,2560]{1,0:T(8,128)(2,1)} %get-tuple-element.82.r0, bf16[128,2560]{1,0:T(8,128)(2,1)} %copy-done.1, bf16[128,2560]{1,0:T(8,128)(2,1)} %copy-done.2, bf16[128,2560]{1,0:T(8,128)(2,1)} %copy-done.3, bf16[256,512]{1,0:T(8,128)(2,1)} %copy-done.6, ...), custom_call_target="tpu_custom_call" | custom-call | tf_op jit(solution)/shard_map/pack/pallas_call | solution.py:130
  49.2 0.7 collective-permute-start.11
  49.9 0.8 collective-permute-start.9
  50.7 1.9 %collective-permute-start.10 = (bf16[768,512]{1,0:T(8,128)(2,1)}, bf16[768,512]{1,0:T(8,128)(2,1)S(1)}, u32[]{:S(2)}, u32[]{:S(2)}) collective-permute-start(bf16[768,512]{1,0:T(8,128)(2,1)} %get-tuple-element.87), channel_id=1, source_target_pairs={{0,24},{1,25},{2,26},{3,27},{4,28},{5,29},{6,30},{7,31},{8,0},{9,1... | collective-permute-start | bytes 2359304 | tf_op jit(solution)/shard_map/ppermute | solution.py:46
  52.6 1.0 collective-permute-start.13
  53.6 0.6 collective-permute-done.11.other
  54.2 1.1 %copy-done.9 = bf16[512,1536]{1,0:T(8,128)(2,1)} copy-done((bf16[512,1536]{1,0:T(8,128)(2,1)}, bf16[512,1536]{1,0:T(8,128)(2,1)S(1)}, u32[]{:S(2)}) %copy-start.9) | copy-done | bytes 1572888
  55.4 4.3 %wgrad_part.1 = (f32[2,256,512]{2,1,0:T(8,128)}, bf16[256,512]{1,0:T(8,128)(2,1)}, bf16[256,512]{1,0:T(8,128)(2,1)}) custom-call(bf16[128,2560]{1,0:T(8,128)(2,1)} %get-tuple-element.82.r0, bf16[128,2560]{1,0:T(8,128)(2,1)} %copy-done.1, bf16[128,2560]{1,0:T(8,128)(2,1)} %copy-done.2, bf16[128,2560]{1,0:T(8,128)(2,1)} %copy-done.3, bf16[512,1536]{1,0:T(8,128)(2,1)} %copy-done.9), custom_call_target="tpu_custom_call" | custom-call | tf_op jit(solution)/shard_map/wgrad_part/pallas_call | solution.py:161
  59.7 0.9 copy-done.10
  60.6 0.8 copy-done.17
  61.4 4.4 %backward_early.4 = (f32[128,512]{1,0:T(8,128)}, f32[8,128,256]{2,1,0:T(8,128)}) custom-call(s32[4]{0:T(128)} %pad_add_fusion.place, bf16[128,8192]{1,0:T(8,128)(2,1)} %bitcast.37, f32[1,8192]{1,0:T(1,128)} %gain.9, f32[128,128]{1,0:T(8,128)} %get-tuple-element.66.rinv, bf16[128,512]{1,0:T(8,128)(2,1)} %bitcast.42, f32[128,512]{1,0:T(8,128)} %get-tuple-element.91.refs_0_, ...), custom_call_target="tpu_custom_call" | custom-call | tf_op jit(solution)/shard_map/backward_early/pallas_call | solution.py:231
  65.9 4.2 %collective-permute-done.9 = bf16[768,512]{1,0:T(8,128)(2,1)S(1)} collective-permute-done((bf16[768,512]{1,0:T(8,128)(2,1)}, bf16[768,512]{1,0:T(8,128)(2,1)S(1)}, u32[]{:S(2)}, u32[]{:S(2)}) %collective-permute-start.9) | collective-permute-done | bytes 786464 | tf_op jit(solution)/shard_map/ppermute | solution.py:46
  70.1 0.7 copy-done.19
  70.9 1.3 %collective-permute-start.17 = (bf16[1536,512]{1,0:T(8,128)(2,1)S(1)}, bf16[1536,512]{1,0:T(8,128)(2,1)S(1)}, u32[]{:S(2)}, u32[]{:S(2)}) collective-permute-start(bf16[1536,512]{1,0:T(8,128)(2,1)S(1)} %constant_dynamic-update-slice_fusion.refs_1_), channel_id=1, source_target_pairs={{0,1},{1,0},{2,3},{3,2},{4,5},{5,4},{6,7},{7,6},{8,9},{9,8},{10,11... | collective-permute-start | bytes 4718600 | tf_op jit(solution)/shard_map/ppermute | solution.py:46
  72.6 0.8 fusion.1
  73.4 2.4 %collective-permute-start.18 = (bf16[256,512]{1,0:T(8,128)(2,1)}, bf16[256,512]{1,0:T(8,128)(2,1)}, u32[]{:S(2)}, u32[]{:S(2)}) collective-permute-start(bf16[256,512]{1,0:T(8,128)(2,1)} %fusion.1), channel_id=1, source_target_pairs={{0,4},{1,5},{2,6},{3,7},{4,0},{5,1},{6,2},{7,3},{8,12},{9,13},{10,... | collective-permute-start | bytes 786440 | tf_op jit(solution)/shard_map/ppermute | solution.py:46
  75.8 0.8 pad_maximum_fusion.1
  76.6 0.8 slice.21
  77.5 2.7 %collective-permute-start.15 = (bf16[512,512]{1,0:T(8,128)(2,1)}, bf16[512,512]{1,0:T(8,128)(2,1)}, u32[]{:S(2)}, u32[]{:S(2)}) collective-permute-start(bf16[512,512]{1,0:T(8,128)(2,1)} %pad_maximum_fusion.1), channel_id=1, source_target_pairs={{0,24},{1,25},{2,26},{3,27},{4,28},{5,29},{6,30},{7,31},{8,0},{9,1... | collective-permute-start | bytes 1572872 | tf_op jit(solution)/shard_map/ppermute | solution.py:46
  80.1 0.7 constant_dynamic-slice_fusion
  80.8 4.7 %collective-permute-start.20 = (f32[64,512]{1,0:T(8,128)S(1)}, f32[64,512]{1,0:T(8,128)S(1)}, u32[]{:S(2)}, u32[]{:S(2)}) collective-permute-start(f32[64,512]{1,0:T(8,128)S(1)} %fusion.3), channel_id=1, source_target_pairs={{0,32},{32,0},{64,96},{96,64},{128,160},{160,128},{192,224},{224,1... | collective-permute-start | bytes 393224 | tf_op jit(solution)/shard_map/ppermute | solution.py:51
  85.5 5.5 %backward_early.5 = (f32[128,512]{1,0:T(8,128)}, f32[12,128,256]{2,1,0:T(8,128)}) custom-call(s32[4]{0:T(128)} %pad_add_fusion.place, bf16[128,8192]{1,0:T(8,128)(2,1)} %bitcast.38, f32[1,8192]{1,0:T(1,128)} %gain.9, f32[128,128]{1,0:T(8,128)} %get-tuple-element.66.rinv, bf16[128,512]{1,0:T(8,128)(2,1)} %bitcast.43, f32[128,512]{1,0:T(8,128)} %get-tuple-element.98.refs_0_, ...), custom_call_target="tpu_custom_call" | custom-call | tf_op jit(solution)/shard_map/backward_early/pallas_call | solution.py:231
  91.1 1.9 %fusion.2 = (f32[1,256,512]{2,1,0:T(8,128)}, f32[256]{0:T(256)S(1)}) fusion(bf16[256,512]{1,0:T(8,128)(2,1)} %collective-permute-done.18, bf16[256,512]{1,0:T(8,128)(2,1)S(1)} %collective-permute-done.19, f32[2,256,512]{2,1,0:T(8,128)S(1)} %copy-done.12, bf16[1,256,512]{2,1,0:T(8,128)(2,1)S(1)} %copy-done.5), kind=kLoop, calls=%fused_computation.7 | loop fusion | flops 917248 | bytes 1836032 | tf_op jit(solution)/shard_map/broadcast_in_dim | solution.py:464
  94.0 3.2 %collective-permute-start.21 = (bf16[512,512]{1,0:T(8,128)(2,1)}, bf16[512,512]{1,0:T(8,128)(2,1)S(1)}, u32[]{:S(2)}, u32[]{:S(2)}) collective-permute-start(bf16[512,512]{1,0:T(8,128)(2,1)} %collective-permute-done.15.refs_3_), channel_id=1, source_target_pairs={{0,1},{1,0},{2,3},{3,2},{4,5},{5,4},{6,7},{7,6},{8,9},{9,8},{10,11... | collective-permute-start | bytes 1572872 | tf_op jit(solution)/shard_map/ppermute | solution.py:46
  97.8 2.6 %collective-permute-start.24 = (f32[64,512]{1,0:T(8,128)S(1)}, f32[64,512]{1,0:T(8,128)S(1)}, u32[]{:S(2)}, u32[]{:S(2)}) collective-permute-start(f32[64,512]{1,0:T(8,128)S(1)} %add_multiply_fusion.p0), channel_id=1, source_target_pairs={{0,128},{32,160},{64,192},{96,224},{128,0},{160,32},{192,64},{224,... | collective-permute-start | bytes 393224 | tf_op jit(solution)/shard_map/ppermute | solution.py:51
  100.4 0.9 collective-permute-start.25
  101.4 0.8 copy-done.15
  102.3 7.4 %backward_late.1 = (f32[128,512]{1,0:T(8,128)}, f32[128,8192]{1,0:T(8,128)}) custom-call(s32[4]{0:T(128)} %pad_add_fusion.place, bf16[128,8192]{1,0:T(8,128)(2,1)} %bitcast.39, f32[1,8192]{1,0:T(1,128)} %gain.9, f32[128,128]{1,0:T(8,128)} %get-tuple-element.66.rinv, bf16[128,512]{1,0:T(8,128)(2,1)} %bitcast.44, f32[128,512]{1,0:T(8,128)} %get-tuple-element.107.early, ...), custom_call_target="tpu_custom_call" | custom-call | tf_op jit(solution)/shard_map/backward_late/pallas_call | solution.py:304
  109.8 0.6 copy-done.22
  110.5 2.8 %outer_update.1 = (f32[256,512]{1,0:T(8,128)}, bf16[256,512]{1,0:T(8,128)(2,1)}, f32[4,256]{1,0:T(4,128)}) custom-call(s32[4]{0:T(128)} %pad_add_fusion.place, f32[64,512]{1,0:T(8,128)} %copy-done.18, f32[64,512]{1,0:T(8,128)} %copy-done.22, f32[64,512]{1,0:T(8,128)} %copy-done.23, f32[64,512]{1,0:T(8,128)} %copy-done.24, f32[256,512]{1,0:T(8,128)} %glob.2, ...), custom_call_target="tpu_custom_call" | custom-call | tf_op jit(solution)/shard_map/outer_update/pallas_call | solution.py:372
  (80 shorter events, 3.3 us)
Async XLA Ops:
  0.6 9.8 %collective-permute-start = (bf16[256,512]{1,0:T(8,128)(2,1)}, bf16[256,512]{1,0:T(8,128)(2,1)S(1)}, u32[]{:S(2)}, u32[]{:S(2)}) collective-permute-start(bf16[256,512]{1,0:T(8,128)(2,1)} %bitcast.45), channel_id=1, source_target_pairs={{0,2},{1,3},{2,0},{3,1},{4,6},{5,7},{6,4},{7,5},{8,10},{9,11},{10,... | collective-permute-start | bytes 786440 | tf_op jit(solution)/shard_map/ppermute | solution.py:46
  3.2 8.3 %collective-permute-start.1 = (bf16[256,512]{1,0:T(8,128)(2,1)}, bf16[256,512]{1,0:T(8,128)(2,1)S(1)}, u32[]{:S(2)}, u32[]{:S(2)}) collective-permute-start(bf16[256,512]{1,0:T(8,128)(2,1)} %bitcast.46), channel_id=1, source_target_pairs={{0,8},{1,9},{2,10},{3,11},{4,12},{5,13},{6,14},{7,15},{8,16},{9,17... | collective-permute-start | bytes 786440 | tf_op jit(solution)/shard_map/ppermute | solution.py:46
  4.4 7.1 %collective-permute-start.2 = (bf16[256,512]{1,0:T(8,128)(2,1)}, bf16[256,512]{1,0:T(8,128)(2,1)S(1)}, u32[]{:S(2)}, u32[]{:S(2)}) collective-permute-start(bf16[256,512]{1,0:T(8,128)(2,1)} %bitcast.47), channel_id=1, source_target_pairs={{0,24},{1,25},{2,26},{3,27},{4,28},{5,29},{6,30},{7,31},{8,0},{9,1... | collective-permute-start | bytes 786440 | tf_op jit(solution)/shard_map/ppermute | solution.py:46
  6.5 12.0 %copy-start.4 = (bf16[1,256,512]{2,1,0:T(8,128)(2,1)S(1)}, bf16[1,256,512]{2,1,0:T(8,128)(2,1)}, u32[]{:S(2)}) copy-start(bf16[1,256,512]{2,1,0:T(8,128)(2,1)} %param.10) | copy-start | bytes 786436
  10.4 13.5 %copy-start.6 = (bf16[256,512]{1,0:T(8,128)(2,1)}, bf16[256,512]{1,0:T(8,128)(2,1)S(1)}, u32[]{:S(2)}) copy-start(bf16[256,512]{1,0:T(8,128)(2,1)S(1)} %collective-permute-done.refs_1_.second) | copy-start | bytes 786436
  11.5 12.4 %copy-start.21 = (bf16[256,512]{1,0:T(8,128)(2,1)}, bf16[256,512]{1,0:T(8,128)(2,1)S(1)}, u32[]{:S(2)}) copy-start(bf16[256,512]{1,0:T(8,128)(2,1)S(1)} %collective-permute-done.1.refs_3_) | copy-start | bytes 786436
  11.5 12.4 %copy-start.13 = (bf16[256,512]{1,0:T(8,128)(2,1)}, bf16[256,512]{1,0:T(8,128)(2,1)S(1)}, u32[]{:S(2)}) copy-start(bf16[256,512]{1,0:T(8,128)(2,1)S(1)} %collective-permute-done.2.refs_2_) | copy-start | bytes 786436
  11.5 33.6 %collective-permute-start.3 = (bf16[128,2560]{1,0:T(8,128)(2,1)}, bf16[128,2560]{1,0:T(8,128)(2,1)S(1)}, u32[]{:S(2)}, u32[]{:S(2)}) collective-permute-start(bf16[128,2560]{1,0:T(8,128)(2,1)} %get-tuple-element.73), channel_id=1, source_target_pairs={{0,8},{1,9},{2,10},{3,11},{4,12},{5,13},{6,14},{7,15},{8,16},{9,17... | collective-permute-start | bytes 1966088 | tf_op jit(solution)/shard_map/ppermute | solution.py:46
  12.4 32.7 %collective-permute-start.4 = (bf16[128,2560]{1,0:T(8,128)(2,1)}, bf16[128,2560]{1,0:T(8,128)(2,1)S(1)}, u32[]{:S(2)}, u32[]{:S(2)}) collective-permute-start(bf16[128,2560]{1,0:T(8,128)(2,1)} %get-tuple-element.74), channel_id=1, source_target_pairs={{0,24},{1,25},{2,26},{3,27},{4,28},{5,29},{6,30},{7,31},{8,0},{9,1... | collective-permute-start | bytes 1966088 | tf_op jit(solution)/shard_map/ppermute | solution.py:46
  14.2 30.9 %collective-permute-start.5 = (bf16[128,2560]{1,0:T(8,128)(2,1)}, bf16[128,2560]{1,0:T(8,128)(2,1)S(1)}, u32[]{:S(2)}, u32[]{:S(2)}) collective-permute-start(bf16[128,2560]{1,0:T(8,128)(2,1)} %get-tuple-element.75), channel_id=1, source_target_pairs={{0,16},{1,17},{2,18},{3,19},{4,20},{5,21},{6,22},{7,23},{8,24},{9,... | collective-permute-start | bytes 1966088 | tf_op jit(solution)/shard_map/ppermute | solution.py:46
  17.1 5.7 %collective-permute-start.7 = (f32[2,64,512]{2,1,0:T(8,128)}, f32[2,64,512]{2,1,0:T(8,128)S(1)}, u32[]{:S(2)}, u32[]{:S(2)}) collective-permute-start(f32[2,64,512]{2,1,0:T(8,128)} %get-tuple-element.79), channel_id=1, source_target_pairs={{0,64},{32,96},{64,0},{96,32},{128,192},{160,224},{192,128},{224,1... | collective-permute-start | bytes 786440 | tf_op jit(solution)/shard_map/ppermute | solution.py:51
  18.5 26.6 %collective-permute-start.6 = (bf16[512,512]{1,0:T(8,128)(2,1)S(1)}, bf16[512,512]{1,0:T(8,128)(2,1)S(1)}, u32[]{:S(2)}, u32[]{:S(2)}) collective-permute-start(bf16[512,512]{1,0:T(8,128)(2,1)S(1)} %pad_maximum_fusion), channel_id=1, source_target_pairs={{0,4},{1,5},{2,6},{3,7},{4,0},{5,1},{6,2},{7,3},{8,12},{9,13},{10,... | collective-permute-start | bytes 1572872 | tf_op jit(solution)/shard_map/ppermute | solution.py:46
  23.9 6.6 %collective-permute-start.8 = (f32[64,512]{1,0:T(8,128)S(1)}, f32[64,512]{1,0:T(8,128)S(1)}, u32[]{:S(2)}, u32[]{:S(2)}) collective-permute-start(f32[64,512]{1,0:T(8,128)S(1)} %slice_bitcast_fusion.1), channel_id=1, source_target_pairs={{0,192},{32,224},{64,128},{96,160},{128,64},{160,96},{192,0},{224,... | collective-permute-start | bytes 393224 | tf_op jit(solution)/shard_map/ppermute | solution.py:51
  45.1 0.8 copy-start.7
  45.1 1.0 copy-start.1
  45.1 1.2 %copy-start.2 = (bf16[128,2560]{1,0:T(8,128)(2,1)}, bf16[128,2560]{1,0:T(8,128)(2,1)S(1)}, u32[]{:S(2)}) copy-start(bf16[128,2560]{1,0:T(8,128)(2,1)S(1)} %collective-permute-done.4.r2) | copy-start | bytes 1966084
  45.1 1.4 %copy-start.3 = (bf16[128,2560]{1,0:T(8,128)(2,1)}, bf16[128,2560]{1,0:T(8,128)(2,1)S(1)}, u32[]{:S(2)}) copy-start(bf16[128,2560]{1,0:T(8,128)(2,1)S(1)} %collective-permute-done.5.r3) | copy-start | bytes 1966084
  46.5 3.3 %copy-start.25 = (bf16[1024,512]{1,0:T(8,128)(2,1)S(1)}, bf16[1024,512]{1,0:T(8,128)(2,1)}, u32[]{:S(2)}) copy-start(bf16[1024,512]{1,0:T(8,128)(2,1)} %get-tuple-element.92) | copy-start | bytes 3145732
  49.2 5.1 %collective-permute-start.11 = (bf16[512,1536]{1,0:T(8,128)(2,1)}, bf16[512,1536]{1,0:T(8,128)(2,1)S(1)}, u32[]{:S(2)}, u32[]{:S(2)}) collective-permute-start(bf16[512,1536]{1,0:T(8,128)(2,1)} %get-tuple-element.89), channel_id=1, source_target_pairs={{0,1},{1,0},{2,3},{3,2},{4,5},{5,4},{6,7},{7,6},{8,9},{9,8},{10,11... | collective-permute-start | bytes 4718600 | tf_op jit(solution)/shard_map/ppermute | solution.py:46
  49.8 9.8 %collective-permute-start.12 = (bf16[1024,512]{1,0:T(8,128)(2,1)S(1)}, bf16[1024,512]{1,0:T(8,128)(2,1)S(1)}, u32[]{:S(2)}, u32[]{:S(2)}) collective-permute-start(bf16[1024,512]{1,0:T(8,128)(2,1)S(1)} %copy-done.25), channel_id=1, source_target_pairs={{0,1},{1,0},{2,3},{3,2},{4,5},{5,4},{6,7},{7,6},{8,9},{9,8},{10,11... | collective-permute-start | bytes 3145736 | tf_op jit(solution)/shard_map/ppermute | solution.py:46
  49.9 20.1 %collective-permute-start.9 = (bf16[768,512]{1,0:T(8,128)(2,1)}, bf16[768,512]{1,0:T(8,128)(2,1)S(1)}, u32[]{:S(2)}, u32[]{:S(2)}) collective-permute-start(bf16[768,512]{1,0:T(8,128)(2,1)} %get-tuple-element.87), channel_id=1, source_target_pairs={{0,8},{1,9},{2,10},{3,11},{4,12},{5,13},{6,14},{7,15},{8,16},{9,17... | collective-permute-start | bytes 2359304 | tf_op jit(solution)/shard_map/ppermute | solution.py:46
  50.7 19.3 %collective-permute-start.10 = (bf16[768,512]{1,0:T(8,128)(2,1)}, bf16[768,512]{1,0:T(8,128)(2,1)S(1)}, u32[]{:S(2)}, u32[]{:S(2)}) collective-permute-start(bf16[768,512]{1,0:T(8,128)(2,1)} %get-tuple-element.87), channel_id=1, source_target_pairs={{0,24},{1,25},{2,26},{3,27},{4,28},{5,29},{6,30},{7,31},{8,0},{9,1... | collective-permute-start | bytes 2359304 | tf_op jit(solution)/shard_map/ppermute | solution.py:46
  52.6 7.1 %collective-permute-start.13 = (bf16[512,512]{1,0:T(8,128)(2,1)}, bf16[512,512]{1,0:T(8,128)(2,1)S(1)}, u32[]{:S(2)}, u32[]{:S(2)}) collective-permute-start(bf16[512,512]{1,0:T(8,128)(2,1)} %copy-done.7), channel_id=1, source_target_pairs={{0,1},{1,0},{2,3},{3,2},{4,5},{5,4},{6,7},{7,6},{8,9},{9,8},{10,11... | collective-permute-start | bytes 1572872 | tf_op jit(solution)/shard_map/ppermute | solution.py:46
  54.2 1.1 %copy-start.9 = (bf16[512,1536]{1,0:T(8,128)(2,1)}, bf16[512,1536]{1,0:T(8,128)(2,1)S(1)}, u32[]{:S(2)}) copy-start(bf16[512,1536]{1,0:T(8,128)(2,1)S(1)} %collective-permute-done.11.other) | copy-start | bytes 4718596
  59.6 10.5 %collective-permute-start.14 = (bf16[256,512]{1,0:T(8,128)(2,1)}, bf16[256,512]{1,0:T(8,128)(2,1)S(1)}, u32[]{:S(2)}, u32[]{:S(2)}) collective-permute-start(bf16[256,512]{1,0:T(8,128)(2,1)} %get-tuple-element.95), channel_id=1, source_target_pairs={{0,2},{1,3},{2,0},{3,1},{4,6},{5,7},{6,4},{7,5},{8,10},{9,11},{10,... | collective-permute-start | bytes 786440 | tf_op jit(solution)/shard_map/ppermute | solution.py:46
  59.7 1.0 copy-start.10
  60.6 0.8 copy-start.17
  70.8 1.6 %copy-start.11 = (f32[2,256,512]{2,1,0:T(8,128)S(1)}, f32[2,256,512]{2,1,0:T(8,128)}, u32[]{:S(2)}) copy-start(f32[2,256,512]{2,1,0:T(8,128)} %get-tuple-element.100) | copy-start | bytes 3145732
  70.8 1.8 %copy-start.20 = (bf16[256,512]{1,0:T(8,128)(2,1)S(1)}, bf16[256,512]{1,0:T(8,128)(2,1)}, u32[]{:S(2)}) copy-start(bf16[256,512]{1,0:T(8,128)(2,1)} %copy-done.19) | copy-start | bytes 786436
  70.8 5.0 %copy-start.14 = (bf16[256,512]{1,0:T(8,128)(2,1)S(1)}, bf16[256,512]{1,0:T(8,128)(2,1)}, u32[]{:S(2)}) copy-start(bf16[256,512]{1,0:T(8,128)(2,1)} %copy-done.13) | copy-start | bytes 786436
  70.9 6.5 %copy-start = (bf16[1536,512]{1,0:T(8,128)(2,1)}, bf16[1536,512]{1,0:T(8,128)(2,1)S(1)}, u32[]{:S(2)}) copy-start(bf16[1536,512]{1,0:T(8,128)(2,1)S(1)} %constant_dynamic-update-slice_fusion.refs_1_) | copy-start | bytes 4718596
  70.9 9.9 %collective-permute-start.17 = (bf16[1536,512]{1,0:T(8,128)(2,1)S(1)}, bf16[1536,512]{1,0:T(8,128)(2,1)S(1)}, u32[]{:S(2)}, u32[]{:S(2)}) collective-permute-start(bf16[1536,512]{1,0:T(8,128)(2,1)S(1)} %constant_dynamic-update-slice_fusion.refs_1_), channel_id=1, source_target_pairs={{0,1},{1,0},{2,3},{3,2},{4,5},{5,4},{6,7},{7,6},{8,9},{9,8},{10,11... | collective-permute-start | bytes 4718600 | tf_op jit(solution)/shard_map/ppermute | solution.py:46
  72.3 18.8 %collective-permute-start.19 = (bf16[256,512]{1,0:T(8,128)(2,1)}, bf16[256,512]{1,0:T(8,128)(2,1)S(1)}, u32[]{:S(2)}, u32[]{:S(2)}) collective-permute-start(bf16[256,512]{1,0:T(8,128)(2,1)} %get-tuple-element.102), channel_id=1, source_target_pairs={{0,2},{1,3},{2,0},{3,1},{4,6},{5,7},{6,4},{7,5},{8,10},{9,11},{10,... | collective-permute-start | bytes 786440 | tf_op jit(solution)/shard_map/ppermute | solution.py:46
  73.4 17.6 %collective-permute-start.18 = (bf16[256,512]{1,0:T(8,128)(2,1)}, bf16[256,512]{1,0:T(8,128)(2,1)}, u32[]{:S(2)}, u32[]{:S(2)}) collective-permute-start(bf16[256,512]{1,0:T(8,128)(2,1)} %fusion.1), channel_id=1, source_target_pairs={{0,4},{1,5},{2,6},{3,7},{4,0},{5,1},{6,2},{7,3},{8,12},{9,13},{10,... | collective-permute-start | bytes 786440 | tf_op jit(solution)/shard_map/ppermute | solution.py:46
  77.5 16.0 %collective-permute-start.15 = (bf16[512,512]{1,0:T(8,128)(2,1)}, bf16[512,512]{1,0:T(8,128)(2,1)}, u32[]{:S(2)}, u32[]{:S(2)}) collective-permute-start(bf16[512,512]{1,0:T(8,128)(2,1)} %pad_maximum_fusion.1), channel_id=1, source_target_pairs={{0,24},{1,25},{2,26},{3,27},{4,28},{5,29},{6,30},{7,31},{8,0},{9,1... | collective-permute-start | bytes 1572872 | tf_op jit(solution)/shard_map/ppermute | solution.py:46
  80.1 13.9 %collective-permute-start.16 = (bf16[512,512]{1,0:T(8,128)(2,1)}, bf16[512,512]{1,0:T(8,128)(2,1)}, u32[]{:S(2)}, u32[]{:S(2)}) collective-permute-start(bf16[512,512]{1,0:T(8,128)(2,1)} %slice.21), channel_id=1, source_target_pairs={{0,8},{1,9},{2,10},{3,11},{4,12},{5,13},{6,14},{7,15},{8,16},{9,17... | collective-permute-start | bytes 1572872 | tf_op jit(solution)/shard_map/ppermute | solution.py:46
  80.8 10.2 %copy-start.5 = (bf16[1,256,512]{2,1,0:T(8,128)(2,1)S(1)}, bf16[1,256,512]{2,1,0:T(8,128)(2,1)}, u32[]{:S(2)}) copy-start(bf16[1,256,512]{2,1,0:T(8,128)(2,1)} %param.10) | copy-start | bytes 786436
  80.8 10.2 %copy-start.12 = (f32[2,256,512]{2,1,0:T(8,128)S(1)}, f32[2,256,512]{2,1,0:T(8,128)}, u32[]{:S(2)}) copy-start(f32[2,256,512]{2,1,0:T(8,128)} %get-tuple-element.100) | copy-start | bytes 3145732
  80.8 4.7 %copy-start.8 = (bf16[1536,512]{1,0:T(8,128)(2,1)}, bf16[1536,512]{1,0:T(8,128)(2,1)S(1)}, u32[]{:S(2)}) copy-start(bf16[1536,512]{1,0:T(8,128)(2,1)S(1)} %collective-permute-done.17.refs_2_) | copy-start | bytes 4718596
  80.8 12.7 %collective-permute-start.20 = (f32[64,512]{1,0:T(8,128)S(1)}, f32[64,512]{1,0:T(8,128)S(1)}, u32[]{:S(2)}, u32[]{:S(2)}) collective-permute-start(f32[64,512]{1,0:T(8,128)S(1)} %fusion.3), channel_id=1, source_target_pairs={{0,32},{32,0},{64,96},{96,64},{128,160},{160,128},{192,224},{224,1... | collective-permute-start | bytes 393224 | tf_op jit(solution)/shard_map/ppermute | solution.py:51
  94.0 7.3 %collective-permute-start.21 = (bf16[512,512]{1,0:T(8,128)(2,1)}, bf16[512,512]{1,0:T(8,128)(2,1)S(1)}, u32[]{:S(2)}, u32[]{:S(2)}) collective-permute-start(bf16[512,512]{1,0:T(8,128)(2,1)} %collective-permute-done.15.refs_3_), channel_id=1, source_target_pairs={{0,1},{1,0},{2,3},{3,2},{4,5},{5,4},{6,7},{7,6},{8,9},{9,8},{10,11... | collective-permute-start | bytes 1572872 | tf_op jit(solution)/shard_map/ppermute | solution.py:46
  97.3 4.1 %collective-permute-start.22 = (bf16[512,512]{1,0:T(8,128)(2,1)}, bf16[512,512]{1,0:T(8,128)(2,1)S(1)}, u32[]{:S(2)}, u32[]{:S(2)}) collective-permute-start(bf16[512,512]{1,0:T(8,128)(2,1)} %collective-permute-done.16.refs_5_), channel_id=1, source_target_pairs={{0,1},{1,0},{2,3},{3,2},{4,5},{5,4},{6,7},{7,6},{8,9},{9,8},{10,11... | collective-permute-start | bytes 1572872 | tf_op jit(solution)/shard_map/ppermute | solution.py:46
  97.4 12.4 %copy-start.18 = (f32[64,512]{1,0:T(8,128)}, f32[64,512]{1,0:T(8,128)S(1)}, u32[]{:S(2)}) copy-start(f32[64,512]{1,0:T(8,128)S(1)} %add_multiply_fusion.p0) | copy-start | bytes 393220
  97.4 12.4 %collective-permute-start.23 = (f32[64,512]{1,0:T(8,128)S(1)}, f32[64,512]{1,0:T(8,128)S(1)}, u32[]{:S(2)}, u32[]{:S(2)}) collective-permute-start(f32[64,512]{1,0:T(8,128)S(1)} %add_multiply_fusion.p0), channel_id=1, source_target_pairs={{0,64},{32,96},{64,0},{96,32},{128,192},{160,224},{192,128},{224,1... | collective-permute-start | bytes 393224 | tf_op jit(solution)/shard_map/ppermute | solution.py:51
  97.8 12.0 %collective-permute-start.24 = (f32[64,512]{1,0:T(8,128)S(1)}, f32[64,512]{1,0:T(8,128)S(1)}, u32[]{:S(2)}, u32[]{:S(2)}) collective-permute-start(f32[64,512]{1,0:T(8,128)S(1)} %add_multiply_fusion.p0), channel_id=1, source_target_pairs={{0,128},{32,160},{64,192},{96,224},{128,0},{160,32},{192,64},{224,... | collective-permute-start | bytes 393224 | tf_op jit(solution)/shard_map/ppermute | solution.py:51
  100.4 9.4 %collective-permute-start.25 = (f32[64,512]{1,0:T(8,128)S(1)}, f32[64,512]{1,0:T(8,128)S(1)}, u32[]{:S(2)}, u32[]{:S(2)}) collective-permute-start(f32[64,512]{1,0:T(8,128)S(1)} %add_multiply_fusion.p0), channel_id=1, source_target_pairs={{0,192},{32,224},{64,128},{96,160},{128,64},{160,96},{192,0},{224,... | collective-permute-start | bytes 393224 | tf_op jit(solution)/shard_map/ppermute | solution.py:51
  101.3 0.8 copy-start.15
  101.3 1.0 copy-start.16
  (4 other events, 2.8 us)

commit v3 on v2

--- a/solution.py
+++ b/solution.py
@@ -20,7 +20,7 @@
     (2, (0,), (3, 0), None),
 )
 SECOND = (
-    (0, (2, 3), (0, 0), (2, 0)),
+    (0, (2, 3), (0, 0), (1, 4)),
     (0, (0, 1), None, (1, 0)),
     (1, (0,), None, (1, 2)),
     (2, (0,), None, (1, 3)),
@@ -98,7 +98,9 @@
     )(place, acts, gain, cot)
 
 
-def pack_kernel(r0, r1, r2, r3, second, third, features, rest, wide, blocks, arrive, leave):
+def pack_kernel(
+    r0, r1, r2, r3, second, third, hold, features, rest, base, wide, blocks, early, arrive, leave
+):
     tokens = r0.shape[0]
     skip = r0.shape[1] - features.shape[1]
     span = second.shape[0]
@@ -106,37 +108,43 @@
         (second, blocks.at[pl.ds(0, span)], rest.at[pl.ds(0, span)]),
         (third, blocks.at[pl.ds(span, third.shape[0])], rest.at[pl.ds(span, third.shape[0])]),
     ]
+    moves.append((hold, early, base.at[pl.ds(0, hold.shape[0])]))
     for number, r in enumerate((r0, r1, r2, r3)):
         part = pl.ds(number * tokens, tokens)
         moves.append((r.at[:, pl.ds(skip, features.shape[1])], wide.at[part], features.at[part]))
     loads = [pltpu.make_async_copy(m[0], m[1], arrive.at[i]) for i, m in enumerate(moves)]
     stores = [pltpu.make_async_copy(m[1], m[2], leave.at[i]) for i, m in enumerate(moves)]
+    again = pltpu.make_async_copy(
+        moves[1][1], base.at[pl.ds(hold.shape[0], third.shape[0])], leave.at[len(moves)]
+    )
     for load in loads:
         load.start()
     for load, store in zip(loads, stores):
         load.wait()
         store.start()
-    for store in stores:
+    again.start()
+    for store in stores + [again]:
         store.wait()
 
 
-def pack(rows, second, third, span):
+def pack(rows, second, third, hold, span):
     tokens, width = rows[0].shape
     hbm = pl.BlockSpec(memory_space=pl.ANY)
     shapes = [
         (X * tokens, width - Z * span),
         (second.shape[0] + third.shape[0], second.shape[1]),
+        (hold.shape[0] + third.shape[0], second.shape[1]),
     ]
     return pl.pallas_call(
         pack_kernel,
-        in_specs=[hbm] * (X + 2),
-        out_specs=[hbm] * 2,
+        in_specs=[hbm] * (X + 3),
+        out_specs=[hbm] * 3,
         out_shape=[jax.ShapeDtypeStruct(shape, BF16) for shape in shapes],
-        scratch_shapes=[pltpu.VMEM(shape, BF16) for shape in shapes]
-        + [pltpu.SemaphoreType.DMA((X + 2,))] * 2,
+        scratch_shapes=[pltpu.VMEM(shape, BF16) for shape in (*shapes[:2], hold.shape)]
+        + [pltpu.SemaphoreType.DMA((X + 3,)), pltpu.SemaphoreType.DMA((X + 4,))],
         compiler_params=params(),
         name="pack",
-    )(*rows, second, third)
+    )(*rows, second, third, hold)
 
 
 def wgrad_kernel(r0, r1, r2, r3, other, kept, sent1, sent3):
@@ -243,56 +251,51 @@
     )(place, acts, gain, rinv, cot, *before, *weights)
 
 
-def late_kernel(
-    layout, done, place, acts, gain, rinv, cot, early, *refs
-):
+def late_kernel(layout, done, place, acts, gain, rinv, cot, early, *refs):
     sources, refs = refs[: len(done)], refs[len(done) :]
-    weights, (keys, dx, held, arrive, leave) = refs[:-5], refs[-5:]
+    weights, (keys, dx, held, leave) = refs[:-4], refs[-4:]
     tokens, width = acts.shape
     part = width // X
-    loads = [[] for _ in range(X)]
-    count = 0
-    for source, entries in zip(sources, done):
-        for number, (slot, _, local, _, rows) in enumerate(
-            pieces_of(entries, [None] * 16, place, part)
-        ):
-            load = pltpu.make_async_copy(
-                source.at[number],
-                held.at[slot, :, pl.ds(local, rows.stop - rows.start)],
-                arrive.at[count],
-            )
-            load.start()
-            loads[slot].append(load)
-            count += 1
     inverse = rinv[:, :1]
     pieces = pieces_of(layout, weights, place, part)
     total = early[...] + keys_sum(pieces, acts, gain, inverse)
     keys[...] = total
     cots = cot[...]
     inner = jnp.sum(total * cots.astype(F32), axis=-1, keepdims=True) / width
-    factor = inverse * inverse * inner
+    factor = rinv[...] * rinv[...] * jnp.broadcast_to(inner, rinv.shape)
+    lane = factor.shape[1]
+    copies = []
 
     def send(slot):
         start = pl.multiple_of(lax.rem(place[0] + OFFSETS[slot], X) * part, part)
-        copy = pltpu.make_async_copy(held.at[slot], dx.at[:, pl.ds(start, part)], leave.at[slot])
+        lanes = pl.ds(start, part)
+        copy = pltpu.make_async_copy(held.at[:, lanes], dx.at[:, lanes], leave.at[slot])
         copy.start()
-        return copy
-
-    copies = []
+        copies.append(copy)
+
     for slot in range(X - 1):
-        for load in loads[slot]:
-            load.wait()
-        start = pl.multiple_of(lax.rem(place[0] + OFFSETS[slot], X) * part, part)
-        held[slot] = held[slot] - acts[:, pl.ds(start, part)].astype(F32) * factor
-        copies.append(send(slot))
-    for slot, start, local, ref, rows in pieces:
-        span = rows.stop - rows.start
-        lanes = pl.ds(start, span)
-        held[slot, :, pl.ds(local, span)] = (
-            inverse * cotangent_of(cots, ref, rows) * gain[:, lanes]
-            - acts[:, lanes].astype(F32) * factor
-        )
-    copies.append(send(X - 1))
+        for source, entries in zip(sources, done):
+            for number, (at, start, _, _, rows) in enumerate(
+                pieces_of(entries, [None] * 16, place, part)
+            ):
+                if at != slot:
+                    continue
+                for first in range(0, rows.stop - rows.start, lane):
+                    lanes = pl.ds(pl.multiple_of(start + first, lane), lane)
+                    held[:, lanes] = (
+                        source[number, :, first : first + lane]
+                        - acts[:, lanes].astype(F32) * factor
+                    )
+        send(slot)
+    for slot, start, _, ref, rows in pieces:
+        cotangent = cotangent_of(cots, ref, rows)
+        for first in range(0, rows.stop - rows.start, lane):
+            lanes = pl.ds(pl.multiple_of(start + first, lane), lane)
+            held[:, lanes] = (
+                rinv[...] * cotangent[:, first : first + lane] * gain[:, lanes]
+                - acts[:, lanes].astype(F32) * factor
+            )
+    send(X - 1)
     for copy in copies:
         copy.wait()
 
@@ -300,55 +303,51 @@
 def backward_late(place, acts, gain, rinv, cot, early, sources, done, layout, weights):
     tokens, width = acts.shape
     vmem = pl.BlockSpec(memory_space=pltpu.VMEM)
-    hbm = pl.BlockSpec(memory_space=pl.ANY)
     return pl.pallas_call(
         functools.partial(late_kernel, layout, done),
         in_specs=[pl.BlockSpec(memory_space=pltpu.SMEM)]
-        + [vmem] * 5
-        + [hbm] * len(sources)
-        + [vmem] * len(weights),
-        out_specs=[vmem, hbm],
+        + [vmem] * (5 + len(sources) + len(weights)),
+        out_specs=[vmem, pl.BlockSpec(memory_space=pl.ANY)],
         out_shape=[
             jax.ShapeDtypeStruct((tokens, cot.shape[1]), F32),
             jax.ShapeDtypeStruct((tokens, width), F32),
         ],
-        scratch_shapes=[
-            pltpu.VMEM((X, tokens, width // X), F32),
-            pltpu.SemaphoreType.DMA((sum(source.shape[0] for source in sources),)),
-            pltpu.SemaphoreType.DMA((X,)),
-        ],
+        scratch_shapes=[pltpu.VMEM((tokens, width), F32), pltpu.SemaphoreType.DMA((X,))],
         compiler_params=params(),
         name="backward_late",
     )(place, acts, gain, rinv, cot, early, *sources, *weights)
 
 
-def delta_kernel(place, glob, local, keep, send):
-    rows = keep.shape[1]
-    for flip, out, row in ((0, keep, 0), (3, keep, 1), (1, send, 0), (2, send, 1)):
-        part = pl.ds(pl.multiple_of((place[3] ^ flip) * rows, rows), rows)
-        out[row] = glob[part, :] - local[part, :]
-
-
-def delta(place, glob, local):
+def delta_kernel(place, glob, local, out):
+    out[...] = glob[...] - local[...]
+
+
+def delta(place, glob, local, first, stride):
     rows, width = glob.shape
-    vmem = pl.BlockSpec(memory_space=pltpu.VMEM)
+    block = (1, rows // Y, width)
+    theirs = pl.BlockSpec(block, lambda i, place: (place[3] ^ (first + stride * i), 0, 0))
+    parts = (Y, rows // Y, width)
     return pl.pallas_call(
         delta_kernel,
-        in_specs=[pl.BlockSpec(memory_space=pltpu.SMEM), vmem, vmem],
-        out_specs=[vmem, vmem],
-        out_shape=[jax.ShapeDtypeStruct((2, rows // Y, width), F32)] * 2,
+        grid_spec=pltpu.PrefetchScalarGridSpec(
+            num_scalar_prefetch=1,
+            grid=(2,),
+            in_specs=[theirs, theirs],
+            out_specs=pl.BlockSpec(block, lambda i, place: (i, 0, 0)),
+        ),
+        out_shape=jax.ShapeDtypeStruct((2, rows // Y, width), F32),
         compiler_params=params(),
         name="delta",
-    )(place, glob, local)
-
-
-def outer_kernel(place, p0, p1, p2, p3, glob, codes, scales, new_global, new_codes, new_scales):
-    rows = p0.shape[0]
+    )(place, glob.reshape(parts), local.reshape(parts))
+
+
+def outer_kernel(place, p03, p12, glob, codes, scales, new_global, new_codes, new_scales):
+    rows = p03.shape[1]
     blocks = scales.shape[0]
-    span = p0.shape[1] // blocks
+    span = p03.shape[2] // blocks
     columns = jnp.concatenate([scales[...]] * (128 // blocks), axis=0).T
     spread = 128 // blocks
-    for flip, part in enumerate((p0, p1, p2, p3)):
+    for flip, part in ((0, p03.at[0]), (3, p03.at[1]), (1, p12.at[0]), (2, p12.at[1])):
         start = pl.multiple_of((place[3] ^ flip) * rows, rows)
         new_global[pl.ds(start, rows), :] = part[...]
     maxima = []
@@ -367,11 +366,11 @@
     )
 
 
-def outer_update(place, parts, glob, codes, scales):
+def outer_update(place, p03, p12, glob, codes, scales):
     vmem = pl.BlockSpec(memory_space=pltpu.VMEM)
     new_global, new_codes, new_scales = pl.pallas_call(
         outer_kernel,
-        in_specs=[pl.BlockSpec(memory_space=pltpu.SMEM)] + [vmem] * (Y + 3),
+        in_specs=[pl.BlockSpec(memory_space=pltpu.SMEM)] + [vmem] * 5,
         out_specs=[vmem] * 3,
         out_shape=[
             jax.ShapeDtypeStruct(glob.shape, F32),
@@ -380,7 +379,7 @@
         ],
         compiler_params=params(),
         name="outer_update",
-    )(place, *parts, glob, codes, scales.T)
+    )(place, p03, p12, glob, codes, scales.T)
     return new_global, new_codes, new_scales.T
 
 
@@ -406,58 +405,68 @@
     width = cot.shape[1]
     second = shift(weight, flip=1)
     near3, near1 = shift(weight, dx=1), shift(weight, dx=-1)
+    came = trade(delta(place, global_fragment, local_fragment[0], 1, 1), flip=1)
     rinv, *slots = normalise(place, acts, norm_gain, cot)
-    *slots, second, near3, near1, glob = together(*slots, second, near3, near1, global_fragment)
+    *slots, second, near3, near1, came, glob = together(
+        *slots, second, near3, near1, came, global_fragment
+    )
 
     rows = [slots[0]] + [shift(slots[d], dx=d) for d in (1, 3, 2)]
     third = shift(jnp.concatenate([weight, second], axis=0), flip=2)
-    keep, send = delta(place, glob, local_fragment[0])
-    keep = keep + trade(send, flip=1)
-    came = trade(keep[1], flip=3)
+    quarter = global_fragment.shape[0] // Y
+    own_delta = [
+        lax.dynamic_slice_in_dim(glob, (place[3] ^ flip) * quarter, quarter)
+        - lax.dynamic_slice_in_dim(local_fragment[0], (place[3] ^ flip) * quarter, quarter)
+        for flip in (0, 3)
+    ]
+    total = own_delta[0] + came[0] + trade(own_delta[1] + came[1], flip=3)
+    came = trade(total, far=1)
     early, first, hold = backward_early(
         place, acts, norm_gain, rinv, cot, (), FIRST, (weight, second, near1, near3), hold=1
     )
     *rows, third, came, early = together(*rows, third, came, early)
-
-    other, rest = pack(rows, second, third, span)
+    pseudo = (total + came) / (Y * H)
+
+    other, rest, base = pack(rows, second, third, hold, span)
     other = shift(other, swap=1)
     far3, far1 = shift(rest, dx=1), shift(rest, dx=-1)
-    total = keep[0] + came
+    came = trade(pseudo, flip=3)
+    other, came = together(other, came)
+    p03 = jnp.stack([pseudo, came])
+    p12 = trade(p03, flip=1)
     kept, sent1, sent3 = wgrad_part(rows, other, span, width)
-    hold_mate, third_mate = shift(hold, swap=1), shift(third, swap=1)
+    base_mate = shift(base, swap=1)
     early, sent1 = together(early, sent1)
     early, second_part = backward_early(
-        place, acts, norm_gain, rinv, cot, (early,), SECOND, (third, hold_mate, third_mate)
+        place, acts, norm_gain, rinv, cot, (early,), SECOND, (third, base_mate)
     )
     back3 = shift(sent3, flip=1)
-    far3, far1, early, total, back3 = together(far3, far1, early, total, back3)
+    far3, far1, early, back3, p12 = together(far3, far1, early, back3, p12)
 
     across_a = shift(jnp.concatenate([near1, far1[:span]], axis=0), dx=-1)
     across_b = shift(far3[span:], dx=1)
     far = jnp.concatenate([far1, far3], axis=0)
     far_mate = shift(far, swap=1)
-    came = trade(total, far=1)
     last = (kept[1] + back3.astype(F32)).astype(BF16)
     end = shift(last, flip=2)
     back1 = shift(sent1, flip=1)
     early, third_part = backward_early(
         place, acts, norm_gain, rinv, cot, (early,), THIRD, (far, far_mate)
     )
-    early, end, back1 = together(early, end, back1)
+    new_global, new_codes, new_scales = outer_update(
+        place, p03, p12, global_fragment, momentum_codes, momentum_scales
+    )
+    across_a, across_b, early, new_scales, end, back1 = together(
+        across_a, across_b, early, new_scales, end, back1
+    )
+    mate_a, mate_b = shift(across_a, swap=1), shift(across_b, swap=1)
     weight_grad = kept[0] + back1.astype(F32) + end.astype(F32)
     gain_here = lax.dynamic_slice_in_dim(norm_gain[0], here * span, span)
     gain_grad = jnp.sum(weight.astype(F32) * weight_grad, axis=-1) / gain_here
-    across_a, across_b, early, gain_grad, came = together(across_a, across_b, early, gain_grad, came)
-    mate_a, mate_b = shift(across_a, swap=1), shift(across_b, swap=1)
-    pseudo = (total + came) / (Y * H)
-    parts = [pseudo] + [trade(pseudo, flip=flip) for flip in range(1, Y)]
+    mate_a, mate_b, gain_grad = together(mate_a, mate_b, gain_grad)
     keys, input_gradient_rows = backward_late(
         place, acts, norm_gain, rinv, cot, early, (first, second_part, third_part),
         (FIRST, SECOND, THIRD), LAST, (across_a, mate_a, across_b, mate_b),
-    )
-    keys, *parts = together(keys, *parts)
-    new_global, new_codes, new_scales = outer_update(
-        place, parts, global_fragment, momentum_codes, momentum_scales
     )
     return (
         keys[None],

time: 114 us -> 115 us (level)
  local copies, waits for them, and re-layouts: 8.72 us -> 6.72 us
  waiting for transfers between devices: 22.3 us -> 23.9 us
  other arithmetic: 5.68 us -> 6.95 us
    ppermute x6 -> x5, waiting for transfers between devices: 1.33 us -> 7.3 us  [trade(): return lax.ppermute(value, 'replica', moves)]
    ppermute x20 -> x19, waiting for transfers between devices: 21 us -> 16.6 us  [shift(): return lax.ppermute(value, 'fsdp', moves)]
    add x2, other arithmetic: 1 us -> 2.72 us  [body(): total = own_delta[0] + came[0] + trade(own_delta[1] + came[1], flip=3)]
    ppermute x6 -> x5, starting transfers between devices: 12.7 us -> 11.5 us  [trade(): return lax.ppermute(value, 'replica', moves)]
    unnamed x53 -> x57, local copies, waits for them, and re-layouts: 7.13 us -> 5.93 us
    pallas_call x2, Pallas kernels: 4.67 us -> 5.86 us  [the longest x1 3.28 us: pack(): pl.pallas_call(pack_kernel, in_specs=[hbm] * (X + 3), out_specs=[hbm] * 3...]
    ppermute x20 -> x19, starting transfers between devices: 26.1 us -> 26.7 us  [shift(): return lax.ppermute(value, 'fsdp', moves)]
  transfers between devices with their start and end apart: 26 -> 24, of which waited for: 6 -> 7; matrix products, arithmetic and copies ran while one was open for 6% -> 5% of each run, Pallas kernels for 28% -> 22%
where the time goes in v3:
time: 115 us; the launch traced here: 114 us
  starting transfers between devices  38.2 us (33%)
  Pallas kernels  37.4 us (33%)
  waiting for transfers between devices  23.9 us (21%)
  other arithmetic  6.95 us (6%)
  local copies, waits for them, and re-layouts  6.72 us (6%)
    ppermute x19, starting transfers between devices, shift(): return lax.ppermute(value, 'fsdp', moves)  26.7 us
    ppermute x19, waiting for transfers between devices, shift(): return lax.ppermute(value, 'fsdp', moves)  16.6 us
    pallas_call x3, Pallas kernels, backward_early(): pl.pallas_call(functools.partial(early_kernel, layout, len(before), hold)...  13.8 us
    ppermute x5, starting transfers between devices, trade(): return lax.ppermute(value, 'replica', moves)  11.5 us
    ppermute x5, waiting for transfers between devices, trade(): return lax.ppermute(value, 'replica', moves)  7.3 us
    pallas_call x1, Pallas kernels, backward_late(): pl.pallas_call(functools.partial(late_kernel, layout, done), in_specs=[pl...  6.82 us
    unnamed x57, local copies, waits for them, and re-layouts  5.93 us
    pallas_call x1, Pallas kernels, wgrad_part(): pl.pallas_call(wgrad_kernel, in_specs=[vmem] * (X + 1), out_specs=[vmem]...  4.25 us
  transfers between devices with their start and end apart: 24, of which 7 were waited for; matrix products, arithmetic and copies ran while one was open for 5% of the time, Pallas kernels for 22%

profile of v3, /device:TPU:1, one launch (start us, length us, event | category | flops | bytes accessed | tf_op | source)
XLA Modules:
  0.0 114.3 jit_solution(1419654019207843765)
XLA Ops:
  0.7 0.6 pad_add_fusion.place
  1.3 2.6 %delta.1 = f32[2,64,512]{2,1,0:T(8,128)} custom-call(s32[4]{0:T(128)} %pad_add_fusion.place, f32[4,64,512]{2,1,0:T(8,128)} %bitcast.56, f32[4,64,512]{2,1,0:T(8,128)} %bitcast.62), custom_call_target="tpu_custom_call" | custom-call | tf_op jit(solution)/shard_map/delta/pallas_call | solution.py:330
  3.9 2.1 %collective-permute-start.3 = (f32[2,64,512]{2,1,0:T(8,128)}, f32[2,64,512]{2,1,0:T(8,128)S(1)}, u32[]{:S(2)}, u32[]{:S(2)}) collective-permute-start(f32[2,64,512]{2,1,0:T(8,128)} %delta.1), channel_id=1, source_target_pairs={{0,64},{32,96},{64,0},{96,32},{128,192},{160,224},{192,128},{224,1... | collective-permute-start | bytes 786440 | tf_op jit(solution)/shard_map/ppermute | solution.py:51
  6.0 2.5 %collective-permute-start.2 = (bf16[256,512]{1,0:T(8,128)(2,1)}, bf16[256,512]{1,0:T(8,128)(2,1)S(1)}, u32[]{:S(2)}, u32[]{:S(2)}) collective-permute-start(bf16[256,512]{1,0:T(8,128)(2,1)} %bitcast.57), channel_id=1, source_target_pairs={{0,24},{1,25},{2,26},{3,27},{4,28},{5,29},{6,30},{7,31},{8,0},{9,1... | collective-permute-start | bytes 786440 | tf_op jit(solution)/shard_map/ppermute | solution.py:46
  8.5 1.6 %collective-permute-start = (bf16[256,512]{1,0:T(8,128)(2,1)}, bf16[256,512]{1,0:T(8,128)(2,1)S(1)}, u32[]{:S(2)}, u32[]{:S(2)}) collective-permute-start(bf16[256,512]{1,0:T(8,128)(2,1)} %bitcast.59), channel_id=1, source_target_pairs={{0,2},{1,3},{2,0},{3,1},{4,6},{5,7},{6,4},{7,5},{8,10},{9,11},{10,... | collective-permute-start | bytes 786440 | tf_op jit(solution)/shard_map/ppermute | solution.py:46
  10.2 4.0 %normalise.1 = (f32[128,128]{1,0:T(8,128)}, bf16[128,2560]{1,0:T(8,128)(2,1)}, bf16[128,2560]{1,0:T(8,128)(2,1)}, bf16[128,2560]{1,0:T(8,128)(2,1)}, bf16[128,2560]{1,0:T(8,128)(2,1)}) custom-call(s32[4]{0:T(128)} %pad_add_fusion.place, bf16[128,8192]{1,0:T(8,128)(2,1)} %bitcast.46, f32[1,8192]{1,0:T(1,128)} %gain.9, bf16[128,512]{1,0:T(8,128)(2,1)} %bitcast.51), custom_call_target="tpu_custom_call" | custom-call | tf_op jit(solution)/shard_map/normalise/pallas_call | solution.py:81
  14.2 2.3 %collective-permute-done.1.refs_3_ = bf16[256,512]{1,0:T(8,128)(2,1)S(1)} collective-permute-done((bf16[256,512]{1,0:T(8,128)(2,1)}, bf16[256,512]{1,0:T(8,128)(2,1)S(1)}, u32[]{:S(2)}, u32[]{:S(2)}) %collective-permute-start.1) | collective-permute-done | bytes 262176 | tf_op jit(solution)/shard_map/ppermute | solution.py:46
  16.5 0.9 pad_maximum_fusion
  17.5 3.0 %collective-permute-start.7 = (bf16[512,512]{1,0:T(8,128)(2,1)}, bf16[512,512]{1,0:T(8,128)(2,1)S(1)}, u32[]{:S(2)}, u32[]{:S(2)}) collective-permute-start(bf16[512,512]{1,0:T(8,128)(2,1)} %pad_maximum_fusion), channel_id=1, source_target_pairs={{0,4},{1,5},{2,6},{3,7},{4,0},{5,1},{6,2},{7,3},{8,12},{9,13},{10,... | collective-permute-start | bytes 1572872 | tf_op jit(solution)/shard_map/ppermute | solution.py:46
  20.5 2.7 %collective-permute-start.5 = (bf16[128,2560]{1,0:T(8,128)(2,1)}, bf16[128,2560]{1,0:T(8,128)(2,1)S(1)}, u32[]{:S(2)}, u32[]{:S(2)}) collective-permute-start(bf16[128,2560]{1,0:T(8,128)(2,1)} %get-tuple-element.72), channel_id=1, source_target_pairs={{0,24},{1,25},{2,26},{3,27},{4,28},{5,29},{6,30},{7,31},{8,0},{9,1... | collective-permute-start | bytes 1966088 | tf_op jit(solution)/shard_map/ppermute | solution.py:46
  23.2 1.7 %bitcast_add_fusion.2 = f32[64,512]{1,0:T(8,128)} fusion(f32[2,64,512]{2,1,0:T(8,128)} %copy-done.25, f32[1,256,512]{2,1,0:T(8,128)} %param.12, s32[]{:T(128)S(6)} %select_n.38, f32[256,512]{1,0:T(8,128)S(1)} %copy-done.1), kind=kLoop, calls=%fused_computation.9 | loop fusion | flops 65536 | bytes 524292 | tf_op jit(solution)/shard_map/add | solution.py:422
  24.8 1.9 %collective-permute-start.8 = (f32[64,512]{1,0:T(8,128)}, f32[64,512]{1,0:T(8,128)}, u32[]{:S(2)}, u32[]{:S(2)}) collective-permute-start(f32[64,512]{1,0:T(8,128)} %bitcast_add_fusion.2), channel_id=1, source_target_pairs={{0,192},{32,224},{64,128},{96,160},{128,64},{160,96},{192,0},{224,... | collective-permute-start | bytes 393224 | tf_op jit(solution)/shard_map/ppermute | solution.py:51
  26.7 3.6 %collective-permute-done.8 = f32[64,512]{1,0:T(8,128)} collective-permute-done((f32[64,512]{1,0:T(8,128)}, f32[64,512]{1,0:T(8,128)}, u32[]{:S(2)}, u32[]{:S(2)}) %collective-permute-start.8) | collective-permute-done | bytes 131104 | tf_op jit(solution)/shard_map/ppermute | solution.py:51
  30.3 1.1 fusion.3
  31.4 5.2 %collective-permute-start.9 = (f32[64,512]{1,0:T(8,128)S(1)}, f32[64,512]{1,0:T(8,128)S(1)}, u32[]{:S(2)}, u32[]{:S(2)}) collective-permute-start(f32[64,512]{1,0:T(8,128)S(1)} %fusion.3), channel_id=1, source_target_pairs={{0,32},{32,0},{64,96},{96,64},{128,160},{160,128},{192,224},{224,1... | collective-permute-start | bytes 393224 | tf_op jit(solution)/shard_map/ppermute | solution.py:51
  36.6 3.7 %backward_early.3 = (f32[128,512]{1,0:T(8,128)}, f32[4,128,256]{2,1,0:T(8,128)}, bf16[1024,512]{1,0:T(8,128)(2,1)}) custom-call(s32[4]{0:T(128)} %pad_add_fusion.place, bf16[128,8192]{1,0:T(8,128)(2,1)} %bitcast.47, f32[1,8192]{1,0:T(1,128)} %gain.9, f32[128,128]{1,0:T(8,128)} %get-tuple-element.64.rinv, bf16[128,512]{1,0:T(8,128)(2,1)} %bitcast.52, ...), custom_call_target="tpu_custom_call" | custom-call | tf_op jit(solution)/shard_map/backward_early/pallas_call | solution.py:239
  40.4 6.1 %collective-permute-done.7.third.refs_1_ = bf16[512,512]{1,0:T(8,128)(2,1)S(1)} collective-permute-done((bf16[512,512]{1,0:T(8,128)(2,1)}, bf16[512,512]{1,0:T(8,128)(2,1)S(1)}, u32[]{:S(2)}, u32[]{:S(2)}) %collective-permute-start.7) | collective-permute-done | bytes 524320 | tf_op jit(solution)/shard_map/ppermute | solution.py:46
  46.4 3.2 %collective-permute-done.6.r3 = bf16[128,2560]{1,0:T(8,128)(2,1)S(1)} collective-permute-done((bf16[128,2560]{1,0:T(8,128)(2,1)}, bf16[128,2560]{1,0:T(8,128)(2,1)S(1)}, u32[]{:S(2)}, u32[]{:S(2)}) %collective-permute-start.6) | collective-permute-done | bytes 655392 | tf_op jit(solution)/shard_map/ppermute | solution.py:46
  49.7 0.8 copy-done.4
  50.5 3.3 %pack.1 = (bf16[512,1536]{1,0:T(8,128)(2,1)}, bf16[768,512]{1,0:T(8,128)(2,1)}, bf16[1536,512]{1,0:T(8,128)(2,1)}) custom-call(bf16[128,2560]{1,0:T(8,128)(2,1)} %get-tuple-element.79.r0, bf16[128,2560]{1,0:T(8,128)(2,1)} %copy-done.2, bf16[128,2560]{1,0:T(8,128)(2,1)} %copy-done.3, bf16[128,2560]{1,0:T(8,128)(2,1)} %copy-done.4, ...), custom_call_target="tpu_custom_call" | custom-call | tf_op jit(solution)/shard_map/pack/pallas_call | solution.py:138
  53.8 3.5 %collective-permute-start.12 = (bf16[512,1536]{1,0:T(8,128)(2,1)}, bf16[512,1536]{1,0:T(8,128)(2,1)S(1)}, u32[]{:S(2)}, u32[]{:S(2)}) collective-permute-start(bf16[512,1536]{1,0:T(8,128)(2,1)} %get-tuple-element.87), channel_id=1, source_target_pairs={{0,1},{1,0},{2,3},{3,2},{4,5},{5,4},{6,7},{7,6},{8,9},{9,8},{10,11... | collective-permute-start | bytes 4718600 | tf_op jit(solution)/shard_map/ppermute | solution.py:46
  57.4 2.9 %collective-permute-start.11 = (bf16[768,512]{1,0:T(8,128)(2,1)}, bf16[768,512]{1,0:T(8,128)(2,1)S(1)}, u32[]{:S(2)}, u32[]{:S(2)}) collective-permute-start(bf16[768,512]{1,0:T(8,128)(2,1)} %get-tuple-element.85), channel_id=1, source_target_pairs={{0,24},{1,25},{2,26},{3,27},{4,28},{5,29},{6,30},{7,31},{8,0},{9,1... | collective-permute-start | bytes 2359304 | tf_op jit(solution)/shard_map/ppermute | solution.py:46
  60.3 2.0 %collective-permute-start.13 = (f32[64,512]{1,0:T(8,128)S(1)}, f32[64,512]{1,0:T(8,128)S(1)}, u32[]{:S(2)}, u32[]{:S(2)}) collective-permute-start(f32[64,512]{1,0:T(8,128)S(1)} %add_multiply_fusion), channel_id=1, source_target_pairs={{0,192},{32,224},{64,128},{96,160},{128,64},{160,96},{192,0},{224,... | collective-permute-start | bytes 393224 | tf_op jit(solution)/shard_map/ppermute | solution.py:51
  62.3 3.7 %collective-permute-done.13 = f32[64,512]{1,0:T(8,128)S(1)} collective-permute-done((f32[64,512]{1,0:T(8,128)S(1)}, f32[64,512]{1,0:T(8,128)S(1)}, u32[]{:S(2)}, u32[]{:S(2)}) %collective-permute-start.13) | collective-permute-done | bytes 131104 | tf_op jit(solution)/shard_map/ppermute | solution.py:51
  66.0 1.1 copy-done.11
  67.1 4.3 %wgrad_part.1 = (f32[2,256,512]{2,1,0:T(8,128)}, bf16[256,512]{1,0:T(8,128)(2,1)}, bf16[256,512]{1,0:T(8,128)(2,1)}) custom-call(bf16[128,2560]{1,0:T(8,128)(2,1)} %get-tuple-element.79.r0, bf16[128,2560]{1,0:T(8,128)(2,1)} %copy-done.2, bf16[128,2560]{1,0:T(8,128)(2,1)} %copy-done.3, bf16[128,2560]{1,0:T(8,128)(2,1)} %copy-done.4, bf16[512,1536]{1,0:T(8,128)(2,1)} %copy-done.11), custom_call_target="tpu_custom_call" | custom-call | tf_op jit(solution)/shard_map/wgrad_part/pallas_call | solution.py:169
  71.4 0.3 collective-permute-start.16
  71.7 1.7 %collective-permute-start.15 = (bf16[256,512]{1,0:T(8,128)(2,1)}, bf16[256,512]{1,0:T(8,128)(2,1)S(1)}, u32[]{:S(2)}, u32[]{:S(2)}) collective-permute-start(bf16[256,512]{1,0:T(8,128)(2,1)} %get-tuple-element.94), channel_id=1, source_target_pairs={{0,2},{1,3},{2,0},{3,1},{4,6},{5,7},{6,4},{7,5},{8,10},{9,11},{10,... | collective-permute-start | bytes 786440 | tf_op jit(solution)/shard_map/ppermute | solution.py:46
  73.4 1.1 copy-done.9
  74.6 4.5 %backward_early.4 = (f32[128,512]{1,0:T(8,128)}, f32[8,128,256]{2,1,0:T(8,128)}) custom-call(s32[4]{0:T(128)} %pad_add_fusion.place, bf16[128,8192]{1,0:T(8,128)(2,1)} %bitcast.48, f32[1,8192]{1,0:T(1,128)} %gain.9, f32[128,128]{1,0:T(8,128)} %get-tuple-element.64.rinv, bf16[128,512]{1,0:T(8,128)(2,1)} %bitcast.53, f32[128,512]{1,0:T(8,128)} %get-tuple-element.91.refs_0_, ...), custom_call_target="tpu_custom_call" | custom-call | tf_op jit(solution)/shard_map/backward_early/pallas_call | solution.py:239
  79.1 1.0 collective-permute-done.10
  80.3 0.6 copy-done.22
  80.8 1.6 %collective-permute-start.19 = (bf16[1536,512]{1,0:T(8,128)(2,1)S(1)}, bf16[1536,512]{1,0:T(8,128)(2,1)S(1)}, u32[]{:S(2)}, u32[]{:S(2)}) collective-permute-start(bf16[1536,512]{1,0:T(8,128)(2,1)S(1)} %constant_dynamic-update-slice_fusion.refs_1_), channel_id=1, source_target_pairs={{0,1},{1,0},{2,3},{3,2},{4,5},{5,4},{6,7},{7,6},{8,9},{9,8},{10,11... | collective-permute-start | bytes 4718600 | tf_op jit(solution)/shard_map/ppermute | solution.py:46
  82.6 2.7 %collective-permute-start.17 = (bf16[512,512]{1,0:T(8,128)(2,1)S(1)}, bf16[512,512]{1,0:T(8,128)(2,1)S(1)}, u32[]{:S(2)}, u32[]{:S(2)}) collective-permute-start(bf16[512,512]{1,0:T(8,128)(2,1)S(1)} %pad_maximum_fusion.1), channel_id=1, source_target_pairs={{0,24},{1,25},{2,26},{3,27},{4,28},{5,29},{6,30},{7,31},{8,0},{9,1... | collective-permute-start | bytes 1572872 | tf_op jit(solution)/shard_map/ppermute | solution.py:46
  85.3 1.6 %collective-permute-start.21 = (bf16[256,512]{1,0:T(8,128)(2,1)S(1)}, bf16[256,512]{1,0:T(8,128)(2,1)S(1)}, u32[]{:S(2)}, u32[]{:S(2)}) collective-permute-start(bf16[256,512]{1,0:T(8,128)(2,1)S(1)} %copy-done.27), channel_id=1, source_target_pairs={{0,2},{1,3},{2,0},{3,1},{4,6},{5,7},{6,4},{7,5},{8,10},{9,11},{10,... | collective-permute-start | bytes 786440 | tf_op jit(solution)/shard_map/ppermute | solution.py:46
  87.0 0.1 collective-permute-start.20
  87.1 2.7 %outer_update.1 = (f32[256,512]{1,0:T(8,128)}, bf16[256,512]{1,0:T(8,128)(2,1)}, f32[4,256]{1,0:T(4,128)}) custom-call(s32[4]{0:T(128)} %pad_add_fusion.place, f32[2,64,512]{2,1,0:T(8,128)} %copy-done.13, f32[2,64,512]{2,1,0:T(8,128)} %copy-done.22, f32[256,512]{1,0:T(8,128)} %glob.1, bf16[256,512]{1,0:T(8,128)(2,1)} %codes.1, f32[4,256]{1,0:T(4,128)} %bitcast.65), custom_call_target="tpu_custom_call" | custom-call | tf_op jit(solution)/shard_map/outer_update/pallas_call | solution.py:371
  89.8 1.1 copy-done.10
  91.0 5.5 %backward_early.5 = (f32[128,512]{1,0:T(8,128)}, f32[12,128,256]{2,1,0:T(8,128)}) custom-call(s32[4]{0:T(128)} %pad_add_fusion.place, bf16[128,8192]{1,0:T(8,128)(2,1)} %bitcast.49, f32[1,8192]{1,0:T(1,128)} %gain.9, f32[128,128]{1,0:T(8,128)} %get-tuple-element.64.rinv, bf16[128,512]{1,0:T(8,128)(2,1)} %bitcast.54, f32[128,512]{1,0:T(8,128)} %get-tuple-element.98.refs_0_, ...), custom_call_target="tpu_custom_call" | custom-call | tf_op jit(solution)/shard_map/backward_early/pallas_call | solution.py:239
  96.5 3.9 %collective-permute-done.20 = bf16[256,512]{1,0:T(8,128)(2,1)S(1)} collective-permute-done((bf16[256,512]{1,0:T(8,128)(2,1)S(1)}, bf16[256,512]{1,0:T(8,128)(2,1)S(1)}, u32[]{:S(2)}, u32[]{:S(2)}) %collective-permute-start.20) | collective-permute-done | bytes 262176 | tf_op jit(solution)/shard_map/ppermute | solution.py:46
  100.4 2.1 %collective-permute-start.22 = (bf16[512,512]{1,0:T(8,128)(2,1)S(1)}, bf16[512,512]{1,0:T(8,128)(2,1)S(1)}, u32[]{:S(2)}, u32[]{:S(2)}) collective-permute-start(bf16[512,512]{1,0:T(8,128)(2,1)S(1)} %collective-permute-done.17.refs_3_), channel_id=1, source_target_pairs={{0,1},{1,0},{2,3},{3,2},{4,5},{5,4},{6,7},{7,6},{8,9},{9,8},{10,11... | collective-permute-start | bytes 1572872 | tf_op jit(solution)/shard_map/ppermute | solution.py:46
  102.5 0.6 collective-permute-start.23
  103.1 0.7 constant_dynamic-slice_fusion
  103.8 1.9 %fusion.2 = (f32[1,256,512]{2,1,0:T(8,128)}, f32[256]{0:T(256)S(1)}) fusion(bf16[256,512]{1,0:T(8,128)(2,1)} %copy-done.24, bf16[256,512]{1,0:T(8,128)(2,1)} %copy-done.23, f32[2,256,512]{2,1,0:T(8,128)S(1)} %copy-done.12, bf16[1,256,512]{2,1,0:T(8,128)(2,1)S(1)} %copy-done.6), kind=kLoop, calls=%fused_computation.8 | loop fusion | flops 917248 | bytes 1836032 | tf_op jit(solution)/shard_map/broadcast_in_dim | solution.py:473
  105.7 0.6 div.42
  106.3 0.8 copy-done.18
  107.1 0.2 copy-done.19
  107.3 6.8 %backward_late.1 = (f32[128,512]{1,0:T(8,128)}, f32[128,8192]{1,0:T(8,128)}) custom-call(s32[4]{0:T(128)} %pad_add_fusion.place, bf16[128,8192]{1,0:T(8,128)(2,1)} %bitcast.50, f32[1,8192]{1,0:T(1,128)} %gain.9, f32[128,128]{1,0:T(8,128)} %get-tuple-element.64.rinv, bf16[128,512]{1,0:T(8,128)(2,1)} %bitcast.55, f32[128,512]{1,0:T(8,128)} %get-tuple-element.105.early, ...), custom_call_target="tpu_custom_call" | custom-call | tf_op jit(solution)/shard_map/backward_late/pallas_call | solution.py:306
  (80 shorter events, 0.7 us)
Async XLA Ops:
  1.3 15.2 %copy-start.5 = (bf16[1,256,512]{2,1,0:T(8,128)(2,1)S(1)}, bf16[1,256,512]{2,1,0:T(8,128)(2,1)}, u32[]{:S(2)}) copy-start(bf16[1,256,512]{2,1,0:T(8,128)(2,1)} %param.10) | copy-start | bytes 786436
  3.9 10.2 %collective-permute-start.3 = (f32[2,64,512]{2,1,0:T(8,128)}, f32[2,64,512]{2,1,0:T(8,128)S(1)}, u32[]{:S(2)}, u32[]{:S(2)}) collective-permute-start(f32[2,64,512]{2,1,0:T(8,128)} %delta.1), channel_id=1, source_target_pairs={{0,64},{32,96},{64,0},{96,32},{128,192},{160,224},{192,128},{224,1... | collective-permute-start | bytes 786440 | tf_op jit(solution)/shard_map/ppermute | solution.py:51
  6.0 8.1 %collective-permute-start.2 = (bf16[256,512]{1,0:T(8,128)(2,1)}, bf16[256,512]{1,0:T(8,128)(2,1)S(1)}, u32[]{:S(2)}, u32[]{:S(2)}) collective-permute-start(bf16[256,512]{1,0:T(8,128)(2,1)} %bitcast.57), channel_id=1, source_target_pairs={{0,24},{1,25},{2,26},{3,27},{4,28},{5,29},{6,30},{7,31},{8,0},{9,1... | collective-permute-start | bytes 786440 | tf_op jit(solution)/shard_map/ppermute | solution.py:46
  8.5 8.0 %collective-permute-start.1 = (bf16[256,512]{1,0:T(8,128)(2,1)}, bf16[256,512]{1,0:T(8,128)(2,1)S(1)}, u32[]{:S(2)}, u32[]{:S(2)}) collective-permute-start(bf16[256,512]{1,0:T(8,128)(2,1)} %bitcast.58), channel_id=1, source_target_pairs={{0,8},{1,9},{2,10},{3,11},{4,12},{5,13},{6,14},{7,15},{8,16},{9,17... | collective-permute-start | bytes 786440 | tf_op jit(solution)/shard_map/ppermute | solution.py:46
  8.5 8.0 %collective-permute-start = (bf16[256,512]{1,0:T(8,128)(2,1)}, bf16[256,512]{1,0:T(8,128)(2,1)S(1)}, u32[]{:S(2)}, u32[]{:S(2)}) collective-permute-start(bf16[256,512]{1,0:T(8,128)(2,1)} %bitcast.59), channel_id=1, source_target_pairs={{0,2},{1,3},{2,0},{3,1},{4,6},{5,7},{6,4},{7,5},{8,10},{9,11},{10,... | collective-permute-start | bytes 786440 | tf_op jit(solution)/shard_map/ppermute | solution.py:46
  10.2 13.0 %copy-start.1 = (f32[256,512]{1,0:T(8,128)S(1)}, f32[256,512]{1,0:T(8,128)}, u32[]{:S(2)}) copy-start(f32[256,512]{1,0:T(8,128)} %glob.1) | copy-start | bytes 1572868
  14.1 2.4 %copy-start.25 = (f32[2,64,512]{2,1,0:T(8,128)}, f32[2,64,512]{2,1,0:T(8,128)S(1)}, u32[]{:S(2)}) copy-start(f32[2,64,512]{2,1,0:T(8,128)S(1)} %collective-permute-done.3) | copy-start | bytes 786436
  14.2 22.4 %copy-start.14 = (bf16[256,512]{1,0:T(8,128)(2,1)}, bf16[256,512]{1,0:T(8,128)(2,1)S(1)}, u32[]{:S(2)}) copy-start(bf16[256,512]{1,0:T(8,128)(2,1)S(1)} %collective-permute-done.2.refs_2_) | copy-start | bytes 786436
  16.5 20.1 %copy-start.7 = (bf16[256,512]{1,0:T(8,128)(2,1)}, bf16[256,512]{1,0:T(8,128)(2,1)S(1)}, u32[]{:S(2)}) copy-start(bf16[256,512]{1,0:T(8,128)(2,1)S(1)} %collective-permute-done.refs_1_.second) | copy-start | bytes 786436
  17.5 29.0 %collective-permute-start.7 = (bf16[512,512]{1,0:T(8,128)(2,1)}, bf16[512,512]{1,0:T(8,128)(2,1)S(1)}, u32[]{:S(2)}, u32[]{:S(2)}) collective-permute-start(bf16[512,512]{1,0:T(8,128)(2,1)} %pad_maximum_fusion), channel_id=1, source_target_pairs={{0,4},{1,5},{2,6},{3,7},{4,0},{5,1},{6,2},{7,3},{8,12},{9,13},{10,... | collective-permute-start | bytes 1572872 | tf_op jit(solution)/shard_map/ppermute | solution.py:46
  20.5 26.0 %collective-permute-start.4 = (bf16[128,2560]{1,0:T(8,128)(2,1)}, bf16[128,2560]{1,0:T(8,128)(2,1)S(1)}, u32[]{:S(2)}, u32[]{:S(2)}) collective-permute-start(bf16[128,2560]{1,0:T(8,128)(2,1)} %get-tuple-element.71), channel_id=1, source_target_pairs={{0,8},{1,9},{2,10},{3,11},{4,12},{5,13},{6,14},{7,15},{8,16},{9,17... | collective-permute-start | bytes 1966088 | tf_op jit(solution)/shard_map/ppermute | solution.py:46
  20.5 26.0 %collective-permute-start.5 = (bf16[128,2560]{1,0:T(8,128)(2,1)}, bf16[128,2560]{1,0:T(8,128)(2,1)S(1)}, u32[]{:S(2)}, u32[]{:S(2)}) collective-permute-start(bf16[128,2560]{1,0:T(8,128)(2,1)} %get-tuple-element.72), channel_id=1, source_target_pairs={{0,24},{1,25},{2,26},{3,27},{4,28},{5,29},{6,30},{7,31},{8,0},{9,1... | collective-permute-start | bytes 1966088 | tf_op jit(solution)/shard_map/ppermute | solution.py:46
  23.1 26.5 %collective-permute-start.6 = (bf16[128,2560]{1,0:T(8,128)(2,1)}, bf16[128,2560]{1,0:T(8,128)(2,1)S(1)}, u32[]{:S(2)}, u32[]{:S(2)}) collective-permute-start(bf16[128,2560]{1,0:T(8,128)(2,1)} %get-tuple-element.73), channel_id=1, source_target_pairs={{0,16},{1,17},{2,18},{3,19},{4,20},{5,21},{6,22},{7,23},{8,24},{9,... | collective-permute-start | bytes 1966088 | tf_op jit(solution)/shard_map/ppermute | solution.py:46
  24.8 5.5 %collective-permute-start.8 = (f32[64,512]{1,0:T(8,128)}, f32[64,512]{1,0:T(8,128)}, u32[]{:S(2)}, u32[]{:S(2)}) collective-permute-start(f32[64,512]{1,0:T(8,128)} %bitcast_add_fusion.2), channel_id=1, source_target_pairs={{0,192},{32,224},{64,128},{96,160},{128,64},{160,96},{192,0},{224,... | collective-permute-start | bytes 393224 | tf_op jit(solution)/shard_map/ppermute | solution.py:51
  31.4 8.9 %copy-start.20 = (f32[64,512]{1,0:T(8,128)}, f32[64,512]{1,0:T(8,128)S(1)}, u32[]{:S(2)}) copy-start(f32[64,512]{1,0:T(8,128)S(1)} %fusion.3) | copy-start | bytes 393220
  31.4 8.9 %collective-permute-start.9 = (f32[64,512]{1,0:T(8,128)S(1)}, f32[64,512]{1,0:T(8,128)S(1)}, u32[]{:S(2)}, u32[]{:S(2)}) collective-permute-start(f32[64,512]{1,0:T(8,128)S(1)} %fusion.3), channel_id=1, source_target_pairs={{0,32},{32,0},{64,96},{96,64},{128,160},{160,128},{192,224},{224,1... | collective-permute-start | bytes 393224 | tf_op jit(solution)/shard_map/ppermute | solution.py:51
  46.4 3.2 %copy-start.8 = (bf16[512,512]{1,0:T(8,128)(2,1)}, bf16[512,512]{1,0:T(8,128)(2,1)S(1)}, u32[]{:S(2)}) copy-start(bf16[512,512]{1,0:T(8,128)(2,1)S(1)} %collective-permute-done.7.third.refs_1_) | copy-start | bytes 1572868
  46.4 3.2 %copy-start.2 = (bf16[128,2560]{1,0:T(8,128)(2,1)}, bf16[128,2560]{1,0:T(8,128)(2,1)S(1)}, u32[]{:S(2)}) copy-start(bf16[128,2560]{1,0:T(8,128)(2,1)S(1)} %collective-permute-done.4.r1) | copy-start | bytes 1966084
  46.4 3.2 %copy-start.3 = (bf16[128,2560]{1,0:T(8,128)(2,1)}, bf16[128,2560]{1,0:T(8,128)(2,1)S(1)}, u32[]{:S(2)}) copy-start(bf16[128,2560]{1,0:T(8,128)(2,1)S(1)} %collective-permute-done.5.r2) | copy-start | bytes 1966084
  50.5 9.8 %copy-start.21 = (f32[64,512]{1,0:T(8,128)S(1)}, f32[64,512]{1,0:T(8,128)}, u32[]{:S(2)}) copy-start(f32[64,512]{1,0:T(8,128)} %copy-done.20) | copy-start | bytes 393220
  53.8 12.2 %collective-permute-start.12 = (bf16[512,1536]{1,0:T(8,128)(2,1)}, bf16[512,1536]{1,0:T(8,128)(2,1)S(1)}, u32[]{:S(2)}, u32[]{:S(2)}) collective-permute-start(bf16[512,1536]{1,0:T(8,128)(2,1)} %get-tuple-element.87), channel_id=1, source_target_pairs={{0,1},{1,0},{2,3},{3,2},{4,5},{5,4},{6,7},{7,6},{8,9},{9,8},{10,11... | collective-permute-start | bytes 4718600 | tf_op jit(solution)/shard_map/ppermute | solution.py:46
  57.3 16.1 %collective-permute-start.14 = (bf16[1536,512]{1,0:T(8,128)(2,1)}, bf16[1536,512]{1,0:T(8,128)(2,1)S(1)}, u32[]{:S(2)}, u32[]{:S(2)}) collective-permute-start(bf16[1536,512]{1,0:T(8,128)(2,1)} %get-tuple-element.92), channel_id=1, source_target_pairs={{0,1},{1,0},{2,3},{3,2},{4,5},{5,4},{6,7},{7,6},{8,9},{9,8},{10,11... | collective-permute-start | bytes 4718600 | tf_op jit(solution)/shard_map/ppermute | solution.py:46
  57.4 21.6 %collective-permute-start.11 = (bf16[768,512]{1,0:T(8,128)(2,1)}, bf16[768,512]{1,0:T(8,128)(2,1)S(1)}, u32[]{:S(2)}, u32[]{:S(2)}) collective-permute-start(bf16[768,512]{1,0:T(8,128)(2,1)} %get-tuple-element.85), channel_id=1, source_target_pairs={{0,24},{1,25},{2,26},{3,27},{4,28},{5,29},{6,30},{7,31},{8,0},{9,1... | collective-permute-start | bytes 2359304 | tf_op jit(solution)/shard_map/ppermute | solution.py:46
  60.3 19.8 %collective-permute-start.10 = (bf16[768,512]{1,0:T(8,128)(2,1)}, bf16[768,512]{1,0:T(8,128)(2,1)S(1)}, u32[]{:S(2)}, u32[]{:S(2)}) collective-permute-start(bf16[768,512]{1,0:T(8,128)(2,1)} %get-tuple-element.85), channel_id=1, source_target_pairs={{0,8},{1,9},{2,10},{3,11},{4,12},{5,13},{6,14},{7,15},{8,16},{9,17... | collective-permute-start | bytes 2359304 | tf_op jit(solution)/shard_map/ppermute | solution.py:46
  60.3 5.6 %collective-permute-start.13 = (f32[64,512]{1,0:T(8,128)S(1)}, f32[64,512]{1,0:T(8,128)S(1)}, u32[]{:S(2)}, u32[]{:S(2)}) collective-permute-start(f32[64,512]{1,0:T(8,128)S(1)} %add_multiply_fusion), channel_id=1, source_target_pairs={{0,192},{32,224},{64,128},{96,160},{128,64},{160,96},{192,0},{224,... | collective-permute-start | bytes 393224 | tf_op jit(solution)/shard_map/ppermute | solution.py:51
  66.0 1.1 %copy-start.11 = (bf16[512,1536]{1,0:T(8,128)(2,1)}, bf16[512,1536]{1,0:T(8,128)(2,1)S(1)}, u32[]{:S(2)}) copy-start(bf16[512,1536]{1,0:T(8,128)(2,1)S(1)} %collective-permute-done.12.other) | copy-start | bytes 4718596
  71.4 11.1 %copy-start.13 = (f32[2,64,512]{2,1,0:T(8,128)}, f32[2,64,512]{2,1,0:T(8,128)S(1)}, u32[]{:S(2)}) copy-start(f32[2,64,512]{2,1,0:T(8,128)S(1)} %pad_maximum_fusion.2.p03) | copy-start | bytes 786436
  71.4 8.7 %collective-permute-start.16 = (f32[2,64,512]{2,1,0:T(8,128)S(1)}, f32[2,64,512]{2,1,0:T(8,128)S(1)}, u32[]{:S(2)}, u32[]{:S(2)}) collective-permute-start(f32[2,64,512]{2,1,0:T(8,128)S(1)} %pad_maximum_fusion.2.p03), channel_id=1, source_target_pairs={{0,64},{32,96},{64,0},{96,32},{128,192},{160,224},{192,128},{224,1... | collective-permute-start | bytes 786440 | tf_op jit(solution)/shard_map/ppermute | solution.py:51
  71.7 8.4 %collective-permute-start.15 = (bf16[256,512]{1,0:T(8,128)(2,1)}, bf16[256,512]{1,0:T(8,128)(2,1)S(1)}, u32[]{:S(2)}, u32[]{:S(2)}) collective-permute-start(bf16[256,512]{1,0:T(8,128)(2,1)} %get-tuple-element.94), channel_id=1, source_target_pairs={{0,2},{1,3},{2,0},{3,1},{4,6},{5,7},{6,4},{7,5},{8,10},{9,11},{10,... | collective-permute-start | bytes 786440 | tf_op jit(solution)/shard_map/ppermute | solution.py:46
  73.4 1.1 %copy-start.9 = (bf16[1536,512]{1,0:T(8,128)(2,1)}, bf16[1536,512]{1,0:T(8,128)(2,1)S(1)}, u32[]{:S(2)}) copy-start(bf16[1536,512]{1,0:T(8,128)(2,1)S(1)} %collective-permute-done.14.refs_2_) | copy-start | bytes 4718596
  80.2 2.3 %copy-start.15 = (bf16[256,512]{1,0:T(8,128)(2,1)S(1)}, bf16[256,512]{1,0:T(8,128)(2,1)}, u32[]{:S(2)}) copy-start(bf16[256,512]{1,0:T(8,128)(2,1)} %copy-done.14) | copy-start | bytes 786436
  80.8 6.2 %copy-start = (bf16[1536,512]{1,0:T(8,128)(2,1)}, bf16[1536,512]{1,0:T(8,128)(2,1)S(1)}, u32[]{:S(2)}) copy-start(bf16[1536,512]{1,0:T(8,128)(2,1)S(1)} %constant_dynamic-update-slice_fusion.refs_1_) | copy-start | bytes 4718596
  80.8 4.5 %copy-start.27 = (bf16[256,512]{1,0:T(8,128)(2,1)S(1)}, bf16[256,512]{1,0:T(8,128)(2,1)}, u32[]{:S(2)}) copy-start(bf16[256,512]{1,0:T(8,128)(2,1)} %get-tuple-element.104) | copy-start | bytes 786436
  80.8 6.1 %copy-start.12 = (f32[2,256,512]{2,1,0:T(8,128)S(1)}, f32[2,256,512]{2,1,0:T(8,128)}, u32[]{:S(2)}) copy-start(f32[2,256,512]{2,1,0:T(8,128)} %get-tuple-element.102) | copy-start | bytes 3145732
  80.8 9.0 %collective-permute-start.19 = (bf16[1536,512]{1,0:T(8,128)(2,1)S(1)}, bf16[1536,512]{1,0:T(8,128)(2,1)S(1)}, u32[]{:S(2)}, u32[]{:S(2)}) collective-permute-start(bf16[1536,512]{1,0:T(8,128)(2,1)S(1)} %constant_dynamic-update-slice_fusion.refs_1_), channel_id=1, source_target_pairs={{0,1},{1,0},{2,3},{3,2},{4,5},{5,4},{6,7},{7,6},{8,9},{9,8},{10,11... | collective-permute-start | bytes 4718600 | tf_op jit(solution)/shard_map/ppermute | solution.py:46
  82.5 17.9 %collective-permute-start.18 = (bf16[512,512]{1,0:T(8,128)(2,1)S(1)}, bf16[512,512]{1,0:T(8,128)(2,1)S(1)}, u32[]{:S(2)}, u32[]{:S(2)}) collective-permute-start(bf16[512,512]{1,0:T(8,128)(2,1)S(1)} %slice.21), channel_id=1, source_target_pairs={{0,8},{1,9},{2,10},{3,11},{4,12},{5,13},{6,14},{7,15},{8,16},{9,17... | collective-permute-start | bytes 1572872 | tf_op jit(solution)/shard_map/ppermute | solution.py:46
  82.6 17.8 %collective-permute-start.17 = (bf16[512,512]{1,0:T(8,128)(2,1)S(1)}, bf16[512,512]{1,0:T(8,128)(2,1)S(1)}, u32[]{:S(2)}, u32[]{:S(2)}) collective-permute-start(bf16[512,512]{1,0:T(8,128)(2,1)S(1)} %pad_maximum_fusion.1), channel_id=1, source_target_pairs={{0,24},{1,25},{2,26},{3,27},{4,28},{5,29},{6,30},{7,31},{8,0},{9,1... | collective-permute-start | bytes 1572872 | tf_op jit(solution)/shard_map/ppermute | solution.py:46
  85.3 11.2 %collective-permute-start.21 = (bf16[256,512]{1,0:T(8,128)(2,1)S(1)}, bf16[256,512]{1,0:T(8,128)(2,1)S(1)}, u32[]{:S(2)}, u32[]{:S(2)}) collective-permute-start(bf16[256,512]{1,0:T(8,128)(2,1)S(1)} %copy-done.27), channel_id=1, source_target_pairs={{0,2},{1,3},{2,0},{3,1},{4,6},{5,7},{6,4},{7,5},{8,10},{9,11},{10,... | collective-permute-start | bytes 786440 | tf_op jit(solution)/shard_map/ppermute | solution.py:46
  87.0 13.4 %collective-permute-start.20 = (bf16[256,512]{1,0:T(8,128)(2,1)S(1)}, bf16[256,512]{1,0:T(8,128)(2,1)S(1)}, u32[]{:S(2)}, u32[]{:S(2)}) collective-permute-start(bf16[256,512]{1,0:T(8,128)(2,1)S(1)} %fusion.1), channel_id=1, source_target_pairs={{0,4},{1,5},{2,6},{3,7},{4,0},{5,1},{6,2},{7,3},{8,12},{9,13},{10,... | collective-permute-start | bytes 786440 | tf_op jit(solution)/shard_map/ppermute | solution.py:46
  89.8 13.9 %copy-start.6 = (bf16[1,256,512]{2,1,0:T(8,128)(2,1)S(1)}, bf16[1,256,512]{2,1,0:T(8,128)(2,1)}, u32[]{:S(2)}) copy-start(bf16[1,256,512]{2,1,0:T(8,128)(2,1)} %param.10) | copy-start | bytes 786436
  89.8 1.1 copy-start.10
  96.5 3.9 %copy-start.23 = (bf16[256,512]{1,0:T(8,128)(2,1)}, bf16[256,512]{1,0:T(8,128)(2,1)S(1)}, u32[]{:S(2)}) copy-start(bf16[256,512]{1,0:T(8,128)(2,1)S(1)} %collective-permute-done.21) | copy-start | bytes 786436
  100.4 2.1 %copy-start.24 = (bf16[256,512]{1,0:T(8,128)(2,1)}, bf16[256,512]{1,0:T(8,128)(2,1)S(1)}, u32[]{:S(2)}) copy-start(bf16[256,512]{1,0:T(8,128)(2,1)S(1)} %collective-permute-done.20) | copy-start | bytes 786436
  100.4 5.9 %copy-start.16 = (bf16[512,512]{1,0:T(8,128)(2,1)}, bf16[512,512]{1,0:T(8,128)(2,1)S(1)}, u32[]{:S(2)}) copy-start(bf16[512,512]{1,0:T(8,128)(2,1)S(1)} %collective-permute-done.18.refs_5_) | copy-start | bytes 1572868
  100.4 5.9 %copy-start.17 = (bf16[512,512]{1,0:T(8,128)(2,1)}, bf16[512,512]{1,0:T(8,128)(2,1)S(1)}, u32[]{:S(2)}) copy-start(bf16[512,512]{1,0:T(8,128)(2,1)S(1)} %collective-permute-done.17.refs_3_) | copy-start | bytes 1572868
  100.4 5.8 %collective-permute-start.22 = (bf16[512,512]{1,0:T(8,128)(2,1)S(1)}, bf16[512,512]{1,0:T(8,128)(2,1)S(1)}, u32[]{:S(2)}, u32[]{:S(2)}) collective-permute-start(bf16[512,512]{1,0:T(8,128)(2,1)S(1)} %collective-permute-done.17.refs_3_), channel_id=1, source_target_pairs={{0,1},{1,0},{2,3},{3,2},{4,5},{5,4},{6,7},{7,6},{8,9},{9,8},{10,11... | collective-permute-start | bytes 1572872 | tf_op jit(solution)/shard_map/ppermute | solution.py:46
  102.5 3.8 %collective-permute-start.23 = (bf16[512,512]{1,0:T(8,128)(2,1)S(1)}, bf16[512,512]{1,0:T(8,128)(2,1)S(1)}, u32[]{:S(2)}, u32[]{:S(2)}) collective-permute-start(bf16[512,512]{1,0:T(8,128)(2,1)S(1)} %collective-permute-done.18.refs_5_), channel_id=1, source_target_pairs={{0,1},{1,0},{2,3},{3,2},{4,5},{5,4},{6,7},{7,6},{8,9},{9,8},{10,11... | collective-permute-start | bytes 1572872 | tf_op jit(solution)/shard_map/ppermute | solution.py:46
  106.3 1.0 copy-start.19
  (4 other events, 3.3 us)

commit v4 on v3

--- a/solution.py
+++ b/solution.py
@@ -318,27 +318,24 @@
     )(place, acts, gain, rinv, cot, early, *sources, *weights)
 
 
-def delta_kernel(place, glob, local, out):
-    out[...] = glob[...] - local[...]
-
-
-def delta(place, glob, local, first, stride):
+def delta_kernel(place, glob, local, keep, send):
+    rows = keep.shape[1]
+    for flip, out, row in ((0, keep, 0), (3, keep, 1), (1, send, 0), (2, send, 1)):
+        part = pl.ds(pl.multiple_of((place[3] ^ flip) * rows, rows), rows)
+        out[row] = glob[part, :] - local[part, :]
+
+
+def delta(place, glob, local):
     rows, width = glob.shape
-    block = (1, rows // Y, width)
-    theirs = pl.BlockSpec(block, lambda i, place: (place[3] ^ (first + stride * i), 0, 0))
-    parts = (Y, rows // Y, width)
+    vmem = pl.BlockSpec(memory_space=pltpu.VMEM)
     return pl.pallas_call(
         delta_kernel,
-        grid_spec=pltpu.PrefetchScalarGridSpec(
-            num_scalar_prefetch=1,
-            grid=(2,),
-            in_specs=[theirs, theirs],
-            out_specs=pl.BlockSpec(block, lambda i, place: (i, 0, 0)),
-        ),
-        out_shape=jax.ShapeDtypeStruct((2, rows // Y, width), F32),
+        in_specs=[pl.BlockSpec(memory_space=pltpu.SMEM), vmem, vmem],
+        out_specs=[vmem, vmem],
+        out_shape=[jax.ShapeDtypeStruct((2, rows // Y, width), F32)] * 2,
         compiler_params=params(),
         name="delta",
-    )(place, glob.reshape(parts), local.reshape(parts))
+    )(place, glob, local)
 
 
 def outer_kernel(place, p03, p12, glob, codes, scales, new_global, new_codes, new_scales):
@@ -405,21 +402,15 @@
     width = cot.shape[1]
     second = shift(weight, flip=1)
     near3, near1 = shift(weight, dx=1), shift(weight, dx=-1)
-    came = trade(delta(place, global_fragment, local_fragment[0], 1, 1), flip=1)
+    keep, send = delta(place, global_fragment, local_fragment[0])
+    came = trade(send, flip=1)
     rinv, *slots = normalise(place, acts, norm_gain, cot)
-    *slots, second, near3, near1, came, glob = together(
-        *slots, second, near3, near1, came, global_fragment
-    )
+    *slots, second, near3, near1, came = together(*slots, second, near3, near1, came)
 
     rows = [slots[0]] + [shift(slots[d], dx=d) for d in (1, 3, 2)]
     third = shift(jnp.concatenate([weight, second], axis=0), flip=2)
-    quarter = global_fragment.shape[0] // Y
-    own_delta = [
-        lax.dynamic_slice_in_dim(glob, (place[3] ^ flip) * quarter, quarter)
-        - lax.dynamic_slice_in_dim(local_fragment[0], (place[3] ^ flip) * quarter, quarter)
-        for flip in (0, 3)
-    ]
-    total = own_delta[0] + came[0] + trade(own_delta[1] + came[1], flip=3)
+    keep = keep + came
+    total = keep[0] + trade(keep[1], flip=3)
     came = trade(total, far=1)
     early, first, hold = backward_early(
         place, acts, norm_gain, rinv, cot, (), FIRST, (weight, second, near1, near3), hold=1
@@ -453,17 +444,17 @@
     early, third_part = backward_early(
         place, acts, norm_gain, rinv, cot, (early,), THIRD, (far, far_mate)
     )
-    new_global, new_codes, new_scales = outer_update(
-        place, p03, p12, global_fragment, momentum_codes, momentum_scales
-    )
-    across_a, across_b, early, new_scales, end, back1 = together(
-        across_a, across_b, early, new_scales, end, back1
-    )
-    mate_a, mate_b = shift(across_a, swap=1), shift(across_b, swap=1)
+    early, end, back1 = together(early, end, back1)
     weight_grad = kept[0] + back1.astype(F32) + end.astype(F32)
     gain_here = lax.dynamic_slice_in_dim(norm_gain[0], here * span, span)
     gain_grad = jnp.sum(weight.astype(F32) * weight_grad, axis=-1) / gain_here
-    mate_a, mate_b, gain_grad = together(mate_a, mate_b, gain_grad)
+    new_global, new_codes, new_scales = outer_update(
+        place, p03, p12, global_fragment, momentum_codes, momentum_scales
+    )
+    across_a, across_b, early, gain_grad, new_scales = together(
+        across_a, across_b, early, gain_grad, new_scales
+    )
+    mate_a, mate_b = shift(across_a, swap=1), shift(across_b, swap=1)
     keys, input_gradient_rows = backward_late(
         place, acts, norm_gain, rinv, cot, early, (first, second_part, third_part),
         (FIRST, SECOND, THIRD), LAST, (across_a, mate_a, across_b, mate_b),

time: 115 us -> 110 us (0.957)
  starting transfers between devices: 38.2 us -> 35.1 us
  other arithmetic: 6.95 us -> 4.85 us
    ppermute x19, starting transfers between devices: 26.7 us -> 23.6 us  [shift(): return lax.ppermute(value, 'fsdp', moves)]
    add x2, other arithmetic: 2.72 us -> 0.05 us  [the longest x1 0.04 us: body(): keep = keep + came]
    unnamed x57 -> x43, local copies, waits for them, and re-layouts: 5.93 us -> 5.75 us
  transfers between devices with their start and end apart: 24 -> 24, of which waited for: 7 -> 9; matrix products, arithmetic and copies ran while one was open for 5% -> 6% of each run, Pallas kernels for 22% -> 24%
where the time goes in v4:
time: 110 us
  Pallas kernels  36.9 us (34%)
  starting transfers between devices  35.1 us (32%)
  waiting for transfers between devices  24.5 us (22%)
  local copies, waits for them, and re-layouts  7.36 us (7%)
  other arithmetic  4.85 us (4%)
    ppermute x19, starting transfers between devices, shift(): return lax.ppermute(value, 'fsdp', moves)  23.6 us
    ppermute x19, waiting for transfers between devices, shift(): return lax.ppermute(value, 'fsdp', moves)  16.7 us
    pallas_call x3, Pallas kernels, backward_early(): pl.pallas_call(functools.partial(early_kernel, layout, len(before), hold)...  13.8 us
    ppermute x5, starting transfers between devices, trade(): return lax.ppermute(value, 'replica', moves)  11.5 us
    ppermute x5, waiting for transfers between devices, trade(): return lax.ppermute(value, 'replica', moves)  7.76 us
    pallas_call x1, Pallas kernels, backward_late(): pl.pallas_call(functools.partial(late_kernel, layout, done), in_specs=[pl...  6.82 us
    unnamed x43, local copies, waits for them, and re-layouts  5.75 us
    pallas_call x1, Pallas kernels, wgrad_part(): pl.pallas_call(wgrad_kernel, in_specs=[vmem] * (X + 1), out_specs=[vmem]...  4.26 us
  transfers between devices with their start and end apart: 24, of which 9 were waited for; matrix products, arithmetic and copies ran while one was open for 6% of the time, Pallas kernels for 24%

profile of v4, /device:TPU:1, one launch (start us, length us, event | category | flops | bytes accessed | tf_op | source)
XLA Modules:
  0.0 109.8 jit_solution(18157346782898915371)
XLA Ops:
  0.6 3.4 %collective-permute-start.2 = (bf16[256,512]{1,0:T(8,128)(2,1)}, bf16[256,512]{1,0:T(8,128)(2,1)S(1)}, u32[]{:S(2)}, u32[]{:S(2)}) collective-permute-start(bf16[256,512]{1,0:T(8,128)(2,1)} %bitcast.47), channel_id=1, source_target_pairs={{0,24},{1,25},{2,26},{3,27},{4,28},{5,29},{6,30},{7,31},{8,0},{9,1... | collective-permute-start | bytes 786440 | tf_op jit(solution)/shard_map/ppermute | solution.py:46
  4.0 1.6 %collective-permute-start = (bf16[256,512]{1,0:T(8,128)(2,1)}, bf16[256,512]{1,0:T(8,128)(2,1)S(1)}, u32[]{:S(2)}, u32[]{:S(2)}) collective-permute-start(bf16[256,512]{1,0:T(8,128)(2,1)} %bitcast.49), channel_id=1, source_target_pairs={{0,2},{1,3},{2,0},{3,1},{4,6},{5,7},{6,4},{7,5},{8,10},{9,11},{10,... | collective-permute-start | bytes 786440 | tf_op jit(solution)/shard_map/ppermute | solution.py:46
  5.7 0.6 pad_add_fusion.place
  6.3 2.1 %delta.1 = (f32[2,64,512]{2,1,0:T(8,128)}, f32[2,64,512]{2,1,0:T(8,128)}) custom-call(s32[4]{0:T(128)} %pad_add_fusion.place, f32[256,512]{1,0:T(8,128)} %glob.3, f32[256,512]{1,0:T(8,128)} %bitcast.53), custom_call_target="tpu_custom_call" | custom-call | tf_op jit(solution)/shard_map/delta/pallas_call | solution.py:331
  8.4 1.3 %collective-permute-start.3 = (f32[2,64,512]{2,1,0:T(8,128)}, f32[2,64,512]{2,1,0:T(8,128)S(1)}, u32[]{:S(2)}, u32[]{:S(2)}) collective-permute-start(f32[2,64,512]{2,1,0:T(8,128)} %get-tuple-element.69), channel_id=1, source_target_pairs={{0,64},{32,96},{64,0},{96,32},{128,192},{160,224},{192,128},{224,1... | collective-permute-start | bytes 786440 | tf_op jit(solution)/shard_map/ppermute | solution.py:51
  9.7 4.0 %normalise.1 = (f32[128,128]{1,0:T(8,128)}, bf16[128,2560]{1,0:T(8,128)(2,1)}, bf16[128,2560]{1,0:T(8,128)(2,1)}, bf16[128,2560]{1,0:T(8,128)(2,1)}, bf16[128,2560]{1,0:T(8,128)(2,1)}) custom-call(s32[4]{0:T(128)} %pad_add_fusion.place, bf16[128,8192]{1,0:T(8,128)(2,1)} %bitcast.37, f32[1,8192]{1,0:T(1,128)} %gain.9, bf16[128,512]{1,0:T(8,128)(2,1)} %bitcast.42), custom_call_target="tpu_custom_call" | custom-call | tf_op jit(solution)/shard_map/normalise/pallas_call | solution.py:81
  13.7 1.5 %collective-permute-done.3 = f32[2,64,512]{2,1,0:T(8,128)S(1)} collective-permute-done((f32[2,64,512]{2,1,0:T(8,128)}, f32[2,64,512]{2,1,0:T(8,128)S(1)}, u32[]{:S(2)}, u32[]{:S(2)}) %collective-permute-start.3) | collective-permute-done | bytes 262176 | tf_op jit(solution)/shard_map/ppermute | solution.py:51
  15.2 3.1 %collective-permute-start.7 = (bf16[512,512]{1,0:T(8,128)(2,1)S(1)}, bf16[512,512]{1,0:T(8,128)(2,1)S(1)}, u32[]{:S(2)}, u32[]{:S(2)}) collective-permute-start(bf16[512,512]{1,0:T(8,128)(2,1)S(1)} %pad_maximum_fusion), channel_id=1, source_target_pairs={{0,4},{1,5},{2,6},{3,7},{4,0},{5,1},{6,2},{7,3},{8,12},{9,13},{10,... | collective-permute-start | bytes 1572872 | tf_op jit(solution)/shard_map/ppermute | solution.py:46
  18.3 2.7 %collective-permute-start.5 = (bf16[128,2560]{1,0:T(8,128)(2,1)}, bf16[128,2560]{1,0:T(8,128)(2,1)S(1)}, u32[]{:S(2)}, u32[]{:S(2)}) collective-permute-start(bf16[128,2560]{1,0:T(8,128)(2,1)} %get-tuple-element.73), channel_id=1, source_target_pairs={{0,24},{1,25},{2,26},{3,27},{4,28},{5,29},{6,30},{7,31},{8,0},{9,1... | collective-permute-start | bytes 1966088 | tf_op jit(solution)/shard_map/ppermute | solution.py:46
  20.9 0.9 collective-permute-start.6
  21.9 2.8 %collective-permute-start.8 = (f32[64,512]{1,0:T(8,128)S(1)}, f32[64,512]{1,0:T(8,128)S(1)}, u32[]{:S(2)}, u32[]{:S(2)}) collective-permute-start(f32[64,512]{1,0:T(8,128)S(1)} %slice_bitcast_fusion), channel_id=1, source_target_pairs={{0,192},{32,224},{64,128},{96,160},{128,64},{160,96},{192,0},{224,... | collective-permute-start | bytes 393224 | tf_op jit(solution)/shard_map/ppermute | solution.py:51
  24.7 2.7 %collective-permute-done.8 = f32[64,512]{1,0:T(8,128)S(1)} collective-permute-done((f32[64,512]{1,0:T(8,128)S(1)}, f32[64,512]{1,0:T(8,128)S(1)}, u32[]{:S(2)}, u32[]{:S(2)}) %collective-permute-start.8) | collective-permute-done | bytes 131104 | tf_op jit(solution)/shard_map/ppermute | solution.py:51
  27.4 4.3 %collective-permute-start.9 = (f32[64,512]{1,0:T(8,128)S(1)}, f32[64,512]{1,0:T(8,128)S(1)}, u32[]{:S(2)}, u32[]{:S(2)}) collective-permute-start(f32[64,512]{1,0:T(8,128)S(1)} %fusion.3), channel_id=1, source_target_pairs={{0,32},{32,0},{64,96},{96,64},{128,160},{160,128},{192,224},{224,1... | collective-permute-start | bytes 393224 | tf_op jit(solution)/shard_map/ppermute | solution.py:51
  31.7 3.8 %backward_early.3 = (f32[128,512]{1,0:T(8,128)}, f32[4,128,256]{2,1,0:T(8,128)}, bf16[1024,512]{1,0:T(8,128)(2,1)}) custom-call(s32[4]{0:T(128)} %pad_add_fusion.place, bf16[128,8192]{1,0:T(8,128)(2,1)} %bitcast.38, f32[1,8192]{1,0:T(1,128)} %gain.9, f32[128,128]{1,0:T(8,128)} %get-tuple-element.64.rinv, bf16[128,512]{1,0:T(8,128)(2,1)} %bitcast.43, ...), custom_call_target="tpu_custom_call" | custom-call | tf_op jit(solution)/shard_map/backward_early/pallas_call | solution.py:239
  35.5 0.7 collective-permute-done.9
  36.2 11.2 %collective-permute-done.7.third.refs_1_ = bf16[512,512]{1,0:T(8,128)(2,1)S(1)} collective-permute-done((bf16[512,512]{1,0:T(8,128)(2,1)S(1)}, bf16[512,512]{1,0:T(8,128)(2,1)S(1)}, u32[]{:S(2)}, u32[]{:S(2)}) %collective-permute-start.7) | collective-permute-done | bytes 524320 | tf_op jit(solution)/shard_map/ppermute | solution.py:46
  47.4 0.7 collective-permute-done.6.r3
  48.2 0.2 copy-done.1
  48.6 0.4 copy-done.3
  49.0 3.3 %pack.1 = (bf16[512,1536]{1,0:T(8,128)(2,1)}, bf16[768,512]{1,0:T(8,128)(2,1)}, bf16[1536,512]{1,0:T(8,128)(2,1)}) custom-call(bf16[128,2560]{1,0:T(8,128)(2,1)} %get-tuple-element.80.r0, bf16[128,2560]{1,0:T(8,128)(2,1)} %copy-done.1, bf16[128,2560]{1,0:T(8,128)(2,1)} %copy-done.2, bf16[128,2560]{1,0:T(8,128)(2,1)} %copy-done.3, ...), custom_call_target="tpu_custom_call" | custom-call | tf_op jit(solution)/shard_map/pack/pallas_call | solution.py:138
  52.3 3.7 %collective-permute-start.12 = (bf16[512,1536]{1,0:T(8,128)(2,1)}, bf16[512,1536]{1,0:T(8,128)(2,1)S(1)}, u32[]{:S(2)}, u32[]{:S(2)}) collective-permute-start(bf16[512,1536]{1,0:T(8,128)(2,1)} %get-tuple-element.88), channel_id=1, source_target_pairs={{0,1},{1,0},{2,3},{3,2},{4,5},{5,4},{6,7},{7,6},{8,9},{9,8},{10,11... | collective-permute-start | bytes 4718600 | tf_op jit(solution)/shard_map/ppermute | solution.py:46
  56.1 2.0 %collective-permute-start.11 = (bf16[768,512]{1,0:T(8,128)(2,1)}, bf16[768,512]{1,0:T(8,128)(2,1)S(1)}, u32[]{:S(2)}, u32[]{:S(2)}) collective-permute-start(bf16[768,512]{1,0:T(8,128)(2,1)} %get-tuple-element.86), channel_id=1, source_target_pairs={{0,24},{1,25},{2,26},{3,27},{4,28},{5,29},{6,30},{7,31},{8,0},{9,1... | collective-permute-start | bytes 2359304 | tf_op jit(solution)/shard_map/ppermute | solution.py:46
  58.1 2.8 %collective-permute-start.13 = (f32[64,512]{1,0:T(8,128)S(1)}, f32[64,512]{1,0:T(8,128)S(1)}, u32[]{:S(2)}, u32[]{:S(2)}) collective-permute-start(f32[64,512]{1,0:T(8,128)S(1)} %add_multiply_fusion), channel_id=1, source_target_pairs={{0,192},{32,224},{64,128},{96,160},{128,64},{160,96},{192,0},{224,... | collective-permute-start | bytes 393224 | tf_op jit(solution)/shard_map/ppermute | solution.py:51
  60.9 3.0 %collective-permute-done.13 = f32[64,512]{1,0:T(8,128)S(1)} collective-permute-done((f32[64,512]{1,0:T(8,128)S(1)}, f32[64,512]{1,0:T(8,128)S(1)}, u32[]{:S(2)}, u32[]{:S(2)}) %collective-permute-start.13) | collective-permute-done | bytes 131104 | tf_op jit(solution)/shard_map/ppermute | solution.py:51
  63.9 1.1 %copy-done.10 = bf16[512,1536]{1,0:T(8,128)(2,1)} copy-done((bf16[512,1536]{1,0:T(8,128)(2,1)}, bf16[512,1536]{1,0:T(8,128)(2,1)S(1)}, u32[]{:S(2)}) %copy-start.10) | copy-done | bytes 1572888
  65.0 4.3 %wgrad_part.1 = (f32[2,256,512]{2,1,0:T(8,128)}, bf16[256,512]{1,0:T(8,128)(2,1)}, bf16[256,512]{1,0:T(8,128)(2,1)}) custom-call(bf16[128,2560]{1,0:T(8,128)(2,1)} %get-tuple-element.80.r0, bf16[128,2560]{1,0:T(8,128)(2,1)} %copy-done.1, bf16[128,2560]{1,0:T(8,128)(2,1)} %copy-done.2, bf16[128,2560]{1,0:T(8,128)(2,1)} %copy-done.3, bf16[512,1536]{1,0:T(8,128)(2,1)} %copy-done.10), custom_call_target="tpu_custom_call" | custom-call | tf_op jit(solution)/shard_map/wgrad_part/pallas_call | solution.py:169
  69.3 0.3 collective-permute-start.16
  69.6 0.3 collective-permute-start.15
  69.9 1.1 %copy-done.9 = bf16[1536,512]{1,0:T(8,128)(2,1)} copy-done((bf16[1536,512]{1,0:T(8,128)(2,1)}, bf16[1536,512]{1,0:T(8,128)(2,1)S(1)}, u32[]{:S(2)}) %copy-start.9) | copy-done | bytes 1572888
  71.0 4.5 %backward_early.4 = (f32[128,512]{1,0:T(8,128)}, f32[8,128,256]{2,1,0:T(8,128)}) custom-call(s32[4]{0:T(128)} %pad_add_fusion.place, bf16[128,8192]{1,0:T(8,128)(2,1)} %bitcast.39, f32[1,8192]{1,0:T(1,128)} %gain.9, f32[128,128]{1,0:T(8,128)} %get-tuple-element.64.rinv, bf16[128,512]{1,0:T(8,128)(2,1)} %bitcast.44, f32[128,512]{1,0:T(8,128)} %get-tuple-element.92.refs_0_, ...), custom_call_target="tpu_custom_call" | custom-call | tf_op jit(solution)/shard_map/backward_early/pallas_call | solution.py:239
  75.5 2.4 %collective-permute-done.10 = bf16[768,512]{1,0:T(8,128)(2,1)S(1)} collective-permute-done((bf16[768,512]{1,0:T(8,128)(2,1)}, bf16[768,512]{1,0:T(8,128)(2,1)S(1)}, u32[]{:S(2)}, u32[]{:S(2)}) %collective-permute-start.10) | collective-permute-done | bytes 786464 | tf_op jit(solution)/shard_map/ppermute | solution.py:46
  78.1 0.6 copy-done.18
  78.6 1.6 %collective-permute-start.19 = (bf16[1536,512]{1,0:T(8,128)(2,1)S(1)}, bf16[1536,512]{1,0:T(8,128)(2,1)S(1)}, u32[]{:S(2)}, u32[]{:S(2)}) collective-permute-start(bf16[1536,512]{1,0:T(8,128)(2,1)S(1)} %constant_dynamic-update-slice_fusion.refs_1_), channel_id=1, source_target_pairs={{0,1},{1,0},{2,3},{3,2},{4,5},{5,4},{6,7},{7,6},{8,9},{9,8},{10,11... | collective-permute-start | bytes 4718600 | tf_op jit(solution)/shard_map/ppermute | solution.py:46
  80.4 0.8 fusion.1
  81.3 0.8 pad_maximum_fusion.1
  82.1 0.8 slice.21
  83.0 2.7 %collective-permute-start.17 = (bf16[512,512]{1,0:T(8,128)(2,1)}, bf16[512,512]{1,0:T(8,128)(2,1)}, u32[]{:S(2)}, u32[]{:S(2)}) collective-permute-start(bf16[512,512]{1,0:T(8,128)(2,1)} %pad_maximum_fusion.1), channel_id=1, source_target_pairs={{0,24},{1,25},{2,26},{3,27},{4,28},{5,29},{6,30},{7,31},{8,0},{9,1... | collective-permute-start | bytes 1572872 | tf_op jit(solution)/shard_map/ppermute | solution.py:46
  85.6 0.7 constant_dynamic-slice_fusion
  86.3 2.7 %outer_update.1 = (f32[256,512]{1,0:T(8,128)}, bf16[256,512]{1,0:T(8,128)(2,1)}, f32[4,256]{1,0:T(4,128)}) custom-call(s32[4]{0:T(128)} %pad_add_fusion.place, f32[2,64,512]{2,1,0:T(8,128)} %copy-done.13, f32[2,64,512]{2,1,0:T(8,128)} %copy-done.18, f32[256,512]{1,0:T(8,128)} %glob.3, bf16[256,512]{1,0:T(8,128)(2,1)} %codes.1, f32[4,256]{1,0:T(4,128)} %bitcast.55), custom_call_target="tpu_custom_call" | custom-call | tf_op jit(solution)/shard_map/outer_update/pallas_call | solution.py:368
  89.0 1.1 %copy-done.8 = bf16[1536,512]{1,0:T(8,128)(2,1)} copy-done((bf16[1536,512]{1,0:T(8,128)(2,1)}, bf16[1536,512]{1,0:T(8,128)(2,1)S(1)}, u32[]{:S(2)}) %copy-start.8) | copy-done | bytes 1572888
  90.2 5.5 %backward_early.5 = (f32[128,512]{1,0:T(8,128)}, f32[12,128,256]{2,1,0:T(8,128)}) custom-call(s32[4]{0:T(128)} %pad_add_fusion.place, bf16[128,8192]{1,0:T(8,128)(2,1)} %bitcast.40, f32[1,8192]{1,0:T(1,128)} %gain.9, f32[128,128]{1,0:T(8,128)} %get-tuple-element.64.rinv, bf16[128,512]{1,0:T(8,128)(2,1)} %bitcast.45, f32[128,512]{1,0:T(8,128)} %get-tuple-element.99.refs_0_, ...), custom_call_target="tpu_custom_call" | custom-call | tf_op jit(solution)/shard_map/backward_early/pallas_call | solution.py:239
  95.7 1.9 %fusion.2 = (f32[1,256,512]{2,1,0:T(8,128)}, f32[256]{0:T(256)S(1)}) fusion(bf16[256,512]{1,0:T(8,128)(2,1)} %collective-permute-done.20, bf16[256,512]{1,0:T(8,128)(2,1)} %collective-permute-done.21, f32[2,256,512]{2,1,0:T(8,128)S(1)} %copy-done.12, bf16[1,256,512]{2,1,0:T(8,128)(2,1)S(1)} %copy-done.5), kind=kLoop, calls=%fused_computation.8 | loop fusion | flops 917248 | bytes 1836032 | tf_op jit(solution)/shard_map/broadcast_in_dim | solution.py:464
  97.6 0.6 div.42
  98.2 1.3 %collective-permute-start.22 = (bf16[512,512]{1,0:T(8,128)(2,1)}, bf16[512,512]{1,0:T(8,128)(2,1)S(1)}, u32[]{:S(2)}, u32[]{:S(2)}) collective-permute-start(bf16[512,512]{1,0:T(8,128)(2,1)} %collective-permute-done.17.refs_3_), channel_id=1, source_target_pairs={{0,1},{1,0},{2,3},{3,2},{4,5},{5,4},{6,7},{7,6},{8,9},{9,8},{10,11... | collective-permute-start | bytes 1572872 | tf_op jit(solution)/shard_map/ppermute | solution.py:46
  99.6 1.7 %collective-permute-done.22.refs_4_ = bf16[512,512]{1,0:T(8,128)(2,1)S(1)} collective-permute-done((bf16[512,512]{1,0:T(8,128)(2,1)}, bf16[512,512]{1,0:T(8,128)(2,1)S(1)}, u32[]{:S(2)}, u32[]{:S(2)}) %collective-permute-start.22) | collective-permute-done | bytes 524320 | tf_op jit(solution)/shard_map/ppermute | solution.py:46
  101.2 0.7 collective-permute-done.23.refs_6_
  102.0 0.8 copy-done.17
  102.8 6.8 %backward_late.1 = (f32[128,512]{1,0:T(8,128)}, f32[128,8192]{1,0:T(8,128)}) custom-call(s32[4]{0:T(128)} %pad_add_fusion.place, bf16[128,8192]{1,0:T(8,128)(2,1)} %bitcast.41, f32[1,8192]{1,0:T(1,128)} %gain.9, f32[128,128]{1,0:T(8,128)} %get-tuple-element.64.rinv, bf16[128,512]{1,0:T(8,128)(2,1)} %bitcast.46, f32[128,512]{1,0:T(8,128)} %get-tuple-element.109.early, ...), custom_call_target="tpu_custom_call" | custom-call | tf_op jit(solution)/shard_map/backward_late/pallas_call | solution.py:306
  (67 shorter events, 1.1 us)
Async XLA Ops:
  0.6 13.0 %collective-permute-start.2 = (bf16[256,512]{1,0:T(8,128)(2,1)}, bf16[256,512]{1,0:T(8,128)(2,1)S(1)}, u32[]{:S(2)}, u32[]{:S(2)}) collective-permute-start(bf16[256,512]{1,0:T(8,128)(2,1)} %bitcast.47), channel_id=1, source_target_pairs={{0,24},{1,25},{2,26},{3,27},{4,28},{5,29},{6,30},{7,31},{8,0},{9,1... | collective-permute-start | bytes 786440 | tf_op jit(solution)/shard_map/ppermute | solution.py:46
  4.0 9.6 %collective-permute-start.1 = (bf16[256,512]{1,0:T(8,128)(2,1)}, bf16[256,512]{1,0:T(8,128)(2,1)S(1)}, u32[]{:S(2)}, u32[]{:S(2)}) collective-permute-start(bf16[256,512]{1,0:T(8,128)(2,1)} %bitcast.48), channel_id=1, source_target_pairs={{0,8},{1,9},{2,10},{3,11},{4,12},{5,13},{6,14},{7,15},{8,16},{9,17... | collective-permute-start | bytes 786440 | tf_op jit(solution)/shard_map/ppermute | solution.py:46
  4.0 9.6 %collective-permute-start = (bf16[256,512]{1,0:T(8,128)(2,1)}, bf16[256,512]{1,0:T(8,128)(2,1)S(1)}, u32[]{:S(2)}, u32[]{:S(2)}) collective-permute-start(bf16[256,512]{1,0:T(8,128)(2,1)} %bitcast.49), channel_id=1, source_target_pairs={{0,2},{1,3},{2,0},{3,1},{4,6},{5,7},{6,4},{7,5},{8,10},{9,11},{10,... | collective-permute-start | bytes 786440 | tf_op jit(solution)/shard_map/ppermute | solution.py:46
  6.3 8.9 %copy-start.4 = (bf16[1,256,512]{2,1,0:T(8,128)(2,1)S(1)}, bf16[1,256,512]{2,1,0:T(8,128)(2,1)}, u32[]{:S(2)}) copy-start(bf16[1,256,512]{2,1,0:T(8,128)(2,1)} %param.10) | copy-start | bytes 786436
  8.4 6.8 %collective-permute-start.3 = (f32[2,64,512]{2,1,0:T(8,128)}, f32[2,64,512]{2,1,0:T(8,128)S(1)}, u32[]{:S(2)}, u32[]{:S(2)}) collective-permute-start(f32[2,64,512]{2,1,0:T(8,128)} %get-tuple-element.69), channel_id=1, source_target_pairs={{0,64},{32,96},{64,0},{96,32},{128,192},{160,224},{192,128},{224,1... | collective-permute-start | bytes 786440 | tf_op jit(solution)/shard_map/ppermute | solution.py:51
  9.7 12.2 %copy-start.19 = (f32[2,64,512]{2,1,0:T(8,128)S(1)}, f32[2,64,512]{2,1,0:T(8,128)}, u32[]{:S(2)}) copy-start(f32[2,64,512]{2,1,0:T(8,128)} %get-tuple-element.76) | copy-start | bytes 786436
  13.6 18.1 %copy-start.14 = (bf16[256,512]{1,0:T(8,128)(2,1)}, bf16[256,512]{1,0:T(8,128)(2,1)S(1)}, u32[]{:S(2)}) copy-start(bf16[256,512]{1,0:T(8,128)(2,1)S(1)} %collective-permute-done.2.refs_2_) | copy-start | bytes 786436
  13.6 18.1 %copy-start.20 = (bf16[256,512]{1,0:T(8,128)(2,1)}, bf16[256,512]{1,0:T(8,128)(2,1)S(1)}, u32[]{:S(2)}) copy-start(bf16[256,512]{1,0:T(8,128)(2,1)S(1)} %collective-permute-done.1.refs_3_) | copy-start | bytes 786436
  13.7 18.0 %copy-start.6 = (bf16[256,512]{1,0:T(8,128)(2,1)}, bf16[256,512]{1,0:T(8,128)(2,1)S(1)}, u32[]{:S(2)}) copy-start(bf16[256,512]{1,0:T(8,128)(2,1)S(1)} %collective-permute-done.refs_1_.second) | copy-start | bytes 786436
  15.2 32.2 %collective-permute-start.7 = (bf16[512,512]{1,0:T(8,128)(2,1)S(1)}, bf16[512,512]{1,0:T(8,128)(2,1)S(1)}, u32[]{:S(2)}, u32[]{:S(2)}) collective-permute-start(bf16[512,512]{1,0:T(8,128)(2,1)S(1)} %pad_maximum_fusion), channel_id=1, source_target_pairs={{0,4},{1,5},{2,6},{3,7},{4,0},{5,1},{6,2},{7,3},{8,12},{9,13},{10,... | collective-permute-start | bytes 1572872 | tf_op jit(solution)/shard_map/ppermute | solution.py:46
  18.2 29.1 %collective-permute-start.4 = (bf16[128,2560]{1,0:T(8,128)(2,1)}, bf16[128,2560]{1,0:T(8,128)(2,1)S(1)}, u32[]{:S(2)}, u32[]{:S(2)}) collective-permute-start(bf16[128,2560]{1,0:T(8,128)(2,1)} %get-tuple-element.72), channel_id=1, source_target_pairs={{0,8},{1,9},{2,10},{3,11},{4,12},{5,13},{6,14},{7,15},{8,16},{9,17... | collective-permute-start | bytes 1966088 | tf_op jit(solution)/shard_map/ppermute | solution.py:46
  18.3 29.1 %collective-permute-start.5 = (bf16[128,2560]{1,0:T(8,128)(2,1)}, bf16[128,2560]{1,0:T(8,128)(2,1)S(1)}, u32[]{:S(2)}, u32[]{:S(2)}) collective-permute-start(bf16[128,2560]{1,0:T(8,128)(2,1)} %get-tuple-element.73), channel_id=1, source_target_pairs={{0,24},{1,25},{2,26},{3,27},{4,28},{5,29},{6,30},{7,31},{8,0},{9,1... | collective-permute-start | bytes 1966088 | tf_op jit(solution)/shard_map/ppermute | solution.py:46
  20.9 27.2 %collective-permute-start.6 = (bf16[128,2560]{1,0:T(8,128)(2,1)}, bf16[128,2560]{1,0:T(8,128)(2,1)S(1)}, u32[]{:S(2)}, u32[]{:S(2)}) collective-permute-start(bf16[128,2560]{1,0:T(8,128)(2,1)} %get-tuple-element.74), channel_id=1, source_target_pairs={{0,16},{1,17},{2,18},{3,19},{4,20},{5,21},{6,22},{7,23},{8,24},{9,... | collective-permute-start | bytes 1966088 | tf_op jit(solution)/shard_map/ppermute | solution.py:46
  21.9 5.5 %collective-permute-start.8 = (f32[64,512]{1,0:T(8,128)S(1)}, f32[64,512]{1,0:T(8,128)S(1)}, u32[]{:S(2)}, u32[]{:S(2)}) collective-permute-start(f32[64,512]{1,0:T(8,128)S(1)} %slice_bitcast_fusion), channel_id=1, source_target_pairs={{0,192},{32,224},{64,128},{96,160},{128,64},{160,96},{192,0},{224,... | collective-permute-start | bytes 393224 | tf_op jit(solution)/shard_map/ppermute | solution.py:51
  27.4 8.8 %collective-permute-start.9 = (f32[64,512]{1,0:T(8,128)S(1)}, f32[64,512]{1,0:T(8,128)S(1)}, u32[]{:S(2)}, u32[]{:S(2)}) collective-permute-start(f32[64,512]{1,0:T(8,128)S(1)} %fusion.3), channel_id=1, source_target_pairs={{0,32},{32,0},{64,96},{96,64},{128,160},{160,128},{192,224},{224,1... | collective-permute-start | bytes 393224 | tf_op jit(solution)/shard_map/ppermute | solution.py:51
  47.4 0.8 copy-start.7
  47.4 1.0 copy-start.1
  47.4 1.2 %copy-start.2 = (bf16[128,2560]{1,0:T(8,128)(2,1)}, bf16[128,2560]{1,0:T(8,128)(2,1)S(1)}, u32[]{:S(2)}) copy-start(bf16[128,2560]{1,0:T(8,128)(2,1)S(1)} %collective-permute-done.5.r2) | copy-start | bytes 1966084
  48.1 0.9 copy-start.3
  52.3 11.6 %collective-permute-start.12 = (bf16[512,1536]{1,0:T(8,128)(2,1)}, bf16[512,1536]{1,0:T(8,128)(2,1)S(1)}, u32[]{:S(2)}, u32[]{:S(2)}) collective-permute-start(bf16[512,1536]{1,0:T(8,128)(2,1)} %get-tuple-element.88), channel_id=1, source_target_pairs={{0,1},{1,0},{2,3},{3,2},{4,5},{5,4},{6,7},{7,6},{8,9},{9,8},{10,11... | collective-permute-start | bytes 4718600 | tf_op jit(solution)/shard_map/ppermute | solution.py:46
  56.0 13.9 %collective-permute-start.14 = (bf16[1536,512]{1,0:T(8,128)(2,1)}, bf16[1536,512]{1,0:T(8,128)(2,1)S(1)}, u32[]{:S(2)}, u32[]{:S(2)}) collective-permute-start(bf16[1536,512]{1,0:T(8,128)(2,1)} %get-tuple-element.93), channel_id=1, source_target_pairs={{0,1},{1,0},{2,3},{3,2},{4,5},{5,4},{6,7},{7,6},{8,9},{9,8},{10,11... | collective-permute-start | bytes 4718600 | tf_op jit(solution)/shard_map/ppermute | solution.py:46
  56.1 19.4 %collective-permute-start.11 = (bf16[768,512]{1,0:T(8,128)(2,1)}, bf16[768,512]{1,0:T(8,128)(2,1)S(1)}, u32[]{:S(2)}, u32[]{:S(2)}) collective-permute-start(bf16[768,512]{1,0:T(8,128)(2,1)} %get-tuple-element.86), channel_id=1, source_target_pairs={{0,24},{1,25},{2,26},{3,27},{4,28},{5,29},{6,30},{7,31},{8,0},{9,1... | collective-permute-start | bytes 2359304 | tf_op jit(solution)/shard_map/ppermute | solution.py:46
  58.1 19.8 %collective-permute-start.10 = (bf16[768,512]{1,0:T(8,128)(2,1)}, bf16[768,512]{1,0:T(8,128)(2,1)S(1)}, u32[]{:S(2)}, u32[]{:S(2)}) collective-permute-start(bf16[768,512]{1,0:T(8,128)(2,1)} %get-tuple-element.86), channel_id=1, source_target_pairs={{0,8},{1,9},{2,10},{3,11},{4,12},{5,13},{6,14},{7,15},{8,16},{9,17... | collective-permute-start | bytes 2359304 | tf_op jit(solution)/shard_map/ppermute | solution.py:46
  58.1 5.8 %collective-permute-start.13 = (f32[64,512]{1,0:T(8,128)S(1)}, f32[64,512]{1,0:T(8,128)S(1)}, u32[]{:S(2)}, u32[]{:S(2)}) collective-permute-start(f32[64,512]{1,0:T(8,128)S(1)} %add_multiply_fusion), channel_id=1, source_target_pairs={{0,192},{32,224},{64,128},{96,160},{128,64},{160,96},{192,0},{224,... | collective-permute-start | bytes 393224 | tf_op jit(solution)/shard_map/ppermute | solution.py:51
  63.9 1.1 %copy-start.10 = (bf16[512,1536]{1,0:T(8,128)(2,1)}, bf16[512,1536]{1,0:T(8,128)(2,1)S(1)}, u32[]{:S(2)}) copy-start(bf16[512,1536]{1,0:T(8,128)(2,1)S(1)} %collective-permute-done.12.other) | copy-start | bytes 4718596
  69.3 12.8 %copy-start.13 = (f32[2,64,512]{2,1,0:T(8,128)}, f32[2,64,512]{2,1,0:T(8,128)S(1)}, u32[]{:S(2)}) copy-start(f32[2,64,512]{2,1,0:T(8,128)S(1)} %pad_maximum_fusion.2.p03) | copy-start | bytes 786436
  69.3 8.6 %collective-permute-start.16 = (f32[2,64,512]{2,1,0:T(8,128)S(1)}, f32[2,64,512]{2,1,0:T(8,128)S(1)}, u32[]{:S(2)}, u32[]{:S(2)}) collective-permute-start(f32[2,64,512]{2,1,0:T(8,128)S(1)} %pad_maximum_fusion.2.p03), channel_id=1, source_target_pairs={{0,64},{32,96},{64,0},{96,32},{128,192},{160,224},{192,128},{224,1... | collective-permute-start | bytes 786440 | tf_op jit(solution)/shard_map/ppermute | solution.py:51
  69.6 8.3 %collective-permute-start.15 = (bf16[256,512]{1,0:T(8,128)(2,1)}, bf16[256,512]{1,0:T(8,128)(2,1)S(1)}, u32[]{:S(2)}, u32[]{:S(2)}) collective-permute-start(bf16[256,512]{1,0:T(8,128)(2,1)} %get-tuple-element.95), channel_id=1, source_target_pairs={{0,2},{1,3},{2,0},{3,1},{4,6},{5,7},{6,4},{7,5},{8,10},{9,11},{10,... | collective-permute-start | bytes 786440 | tf_op jit(solution)/shard_map/ppermute | solution.py:46
  69.9 1.1 %copy-start.9 = (bf16[1536,512]{1,0:T(8,128)(2,1)}, bf16[1536,512]{1,0:T(8,128)(2,1)S(1)}, u32[]{:S(2)}) copy-start(bf16[1536,512]{1,0:T(8,128)(2,1)S(1)} %collective-permute-done.14.refs_2_) | copy-start | bytes 4718596
  77.9 0.7 copy-start.18
  77.9 2.5 %copy-start.11 = (f32[2,256,512]{2,1,0:T(8,128)S(1)}, f32[2,256,512]{2,1,0:T(8,128)}, u32[]{:S(2)}) copy-start(f32[2,256,512]{2,1,0:T(8,128)} %get-tuple-element.101) | copy-start | bytes 3145732
  78.0 3.3 %copy-start.15 = (bf16[256,512]{1,0:T(8,128)(2,1)S(1)}, bf16[256,512]{1,0:T(8,128)(2,1)}, u32[]{:S(2)}) copy-start(bf16[256,512]{1,0:T(8,128)(2,1)} %copy-done.14) | copy-start | bytes 786436
  78.6 4.3 %copy-start = (bf16[1536,512]{1,0:T(8,128)(2,1)}, bf16[1536,512]{1,0:T(8,128)(2,1)S(1)}, u32[]{:S(2)}) copy-start(bf16[1536,512]{1,0:T(8,128)(2,1)S(1)} %constant_dynamic-update-slice_fusion.refs_1_) | copy-start | bytes 4718596
  78.6 10.4 %collective-permute-start.19 = (bf16[1536,512]{1,0:T(8,128)(2,1)S(1)}, bf16[1536,512]{1,0:T(8,128)(2,1)S(1)}, u32[]{:S(2)}, u32[]{:S(2)}) collective-permute-start(bf16[1536,512]{1,0:T(8,128)(2,1)S(1)} %constant_dynamic-update-slice_fusion.refs_1_), channel_id=1, source_target_pairs={{0,1},{1,0},{2,3},{3,2},{4,5},{5,4},{6,7},{7,6},{8,9},{9,8},{10,11... | collective-permute-start | bytes 4718600 | tf_op jit(solution)/shard_map/ppermute | solution.py:46
  80.2 15.5 %collective-permute-start.21 = (bf16[256,512]{1,0:T(8,128)(2,1)}, bf16[256,512]{1,0:T(8,128)(2,1)}, u32[]{:S(2)}, u32[]{:S(2)}) collective-permute-start(bf16[256,512]{1,0:T(8,128)(2,1)} %get-tuple-element.103), channel_id=1, source_target_pairs={{0,2},{1,3},{2,0},{3,1},{4,6},{5,7},{6,4},{7,5},{8,10},{9,11},{10,... | collective-permute-start | bytes 786440 | tf_op jit(solution)/shard_map/ppermute | solution.py:46
  81.2 14.5 %collective-permute-start.20 = (bf16[256,512]{1,0:T(8,128)(2,1)}, bf16[256,512]{1,0:T(8,128)(2,1)}, u32[]{:S(2)}, u32[]{:S(2)}) collective-permute-start(bf16[256,512]{1,0:T(8,128)(2,1)} %fusion.1), channel_id=1, source_target_pairs={{0,4},{1,5},{2,6},{3,7},{4,0},{5,1},{6,2},{7,3},{8,12},{9,13},{10,... | collective-permute-start | bytes 786440 | tf_op jit(solution)/shard_map/ppermute | solution.py:46
  82.9 15.3 %collective-permute-start.18 = (bf16[512,512]{1,0:T(8,128)(2,1)}, bf16[512,512]{1,0:T(8,128)(2,1)}, u32[]{:S(2)}, u32[]{:S(2)}) collective-permute-start(bf16[512,512]{1,0:T(8,128)(2,1)} %slice.21), channel_id=1, source_target_pairs={{0,8},{1,9},{2,10},{3,11},{4,12},{5,13},{6,14},{7,15},{8,16},{9,17... | collective-permute-start | bytes 1572872 | tf_op jit(solution)/shard_map/ppermute | solution.py:46
  83.0 15.3 %collective-permute-start.17 = (bf16[512,512]{1,0:T(8,128)(2,1)}, bf16[512,512]{1,0:T(8,128)(2,1)}, u32[]{:S(2)}, u32[]{:S(2)}) collective-permute-start(bf16[512,512]{1,0:T(8,128)(2,1)} %pad_maximum_fusion.1), channel_id=1, source_target_pairs={{0,24},{1,25},{2,26},{3,27},{4,28},{5,29},{6,30},{7,31},{8,0},{9,1... | collective-permute-start | bytes 1572872 | tf_op jit(solution)/shard_map/ppermute | solution.py:46
  89.0 6.7 %copy-start.5 = (bf16[1,256,512]{2,1,0:T(8,128)(2,1)S(1)}, bf16[1,256,512]{2,1,0:T(8,128)(2,1)}, u32[]{:S(2)}) copy-start(bf16[1,256,512]{2,1,0:T(8,128)(2,1)} %param.10) | copy-start | bytes 786436
  89.0 6.7 %copy-start.12 = (f32[2,256,512]{2,1,0:T(8,128)S(1)}, f32[2,256,512]{2,1,0:T(8,128)}, u32[]{:S(2)}) copy-start(f32[2,256,512]{2,1,0:T(8,128)} %get-tuple-element.101) | copy-start | bytes 3145732
  89.0 1.1 %copy-start.8 = (bf16[1536,512]{1,0:T(8,128)(2,1)}, bf16[1536,512]{1,0:T(8,128)(2,1)S(1)}, u32[]{:S(2)}) copy-start(bf16[1536,512]{1,0:T(8,128)(2,1)S(1)} %collective-permute-done.19.refs_2_) | copy-start | bytes 4718596
  98.2 3.0 %collective-permute-start.22 = (bf16[512,512]{1,0:T(8,128)(2,1)}, bf16[512,512]{1,0:T(8,128)(2,1)S(1)}, u32[]{:S(2)}, u32[]{:S(2)}) collective-permute-start(bf16[512,512]{1,0:T(8,128)(2,1)} %collective-permute-done.17.refs_3_), channel_id=1, source_target_pairs={{0,1},{1,0},{2,3},{3,2},{4,5},{5,4},{6,7},{7,6},{8,9},{9,8},{10,11... | collective-permute-start | bytes 1572872 | tf_op jit(solution)/shard_map/ppermute | solution.py:46
  99.5 2.5 %collective-permute-start.23 = (bf16[512,512]{1,0:T(8,128)(2,1)}, bf16[512,512]{1,0:T(8,128)(2,1)S(1)}, u32[]{:S(2)}, u32[]{:S(2)}) collective-permute-start(bf16[512,512]{1,0:T(8,128)(2,1)} %collective-permute-done.18.refs_5_), channel_id=1, source_target_pairs={{0,1},{1,0},{2,3},{3,2},{4,5},{5,4},{6,7},{7,6},{8,9},{9,8},{10,11... | collective-permute-start | bytes 1572872 | tf_op jit(solution)/shard_map/ppermute | solution.py:46
  101.2 0.8 copy-start.16
  102.0 0.8 copy-start.17

commit v5 on v4

--- a/solution.py
+++ b/solution.py
@@ -405,7 +405,11 @@
     keep, send = delta(place, global_fragment, local_fragment[0])
     came = trade(send, flip=1)
     rinv, *slots = normalise(place, acts, norm_gain, cot)
-    *slots, second, near3, near1, came = together(*slots, second, near3, near1, came)
+    gain_here = lax.dynamic_slice_in_dim(norm_gain[0], here * span, span)
+    ratio = weight.astype(F32) / gain_here[:, None]
+    *slots, second, near3, near1, came, ratio = together(
+        *slots, second, near3, near1, came, ratio
+    )
 
     rows = [slots[0]] + [shift(slots[d], dx=d) for d in (1, 3, 2)]
     third = shift(jnp.concatenate([weight, second], axis=0), flip=2)
@@ -446,8 +450,7 @@
     )
     early, end, back1 = together(early, end, back1)
     weight_grad = kept[0] + back1.astype(F32) + end.astype(F32)
-    gain_here = lax.dynamic_slice_in_dim(norm_gain[0], here * span, span)
-    gain_grad = jnp.sum(weight.astype(F32) * weight_grad, axis=-1) / gain_here
+    gain_grad = jnp.sum(ratio * weight_grad, axis=-1)
     new_global, new_codes, new_scales = outer_update(
         place, p03, p12, global_fragment, momentum_codes, momentum_scales
     )

time: 110 us -> 109 us (level)
  other arithmetic: 4.85 us -> 3.39 us
    ppermute x19, waiting for transfers between devices: 16.7 us -> 18.4 us  [shift(): return lax.ppermute(value, 'fsdp', moves)]
    unnamed x43 -> x47, local copies, waits for them, and re-layouts: 5.75 us -> 5.73 us
  transfers between devices with their start and end apart: 24 -> 24, of which waited for: 9 -> 11; matrix products, arithmetic and copies ran while one was open for 6% -> 4% of each run, Pallas kernels for 24% -> 25%
where the time goes in v5:
time: 109 us; the launch traced here: 108 us
  Pallas kernels  36.9 us (34%)
  starting transfers between devices  35.3 us (32%)
  waiting for transfers between devices  25.2 us (23%)
  local copies, waits for them, and re-layouts  6.53 us (6%)
  other arithmetic  3.39 us (3%)
    ppermute x19, starting transfers between devices, shift(): return lax.ppermute(value, 'fsdp', moves)  23.7 us
    ppermute x19, waiting for transfers between devices, shift(): return lax.ppermute(value, 'fsdp', moves)  18.4 us
    pallas_call x3, Pallas kernels, backward_early(): pl.pallas_call(functools.partial(early_kernel, layout, len(before), hold)...  13.8 us
    ppermute x5, starting transfers between devices, trade(): return lax.ppermute(value, 'replica', moves)  11.5 us
    pallas_call x1, Pallas kernels, backward_late(): pl.pallas_call(functools.partial(late_kernel, layout, done), in_specs=[pl...  6.82 us
    ppermute x5, waiting for transfers between devices, trade(): return lax.ppermute(value, 'replica', moves)  6.82 us
    unnamed x47, local copies, waits for them, and re-layouts  5.73 us
    pallas_call x1, Pallas kernels, wgrad_part(): pl.pallas_call(wgrad_kernel, in_specs=[vmem] * (X + 1), out_specs=[vmem]...  4.26 us
  transfers between devices with their start and end apart: 24, of which 11 were waited for; matrix products, arithmetic and copies ran while one was open for 4% of the time, Pallas kernels for 25%

profile of v5, /device:TPU:1, one launch (start us, length us, event | category | flops | bytes accessed | tf_op | source)
XLA Modules:
  0.0 108.4 jit_solution(7601940481266287035)
XLA Ops:
  0.6 3.4 %collective-permute-start.2 = (bf16[256,512]{1,0:T(8,128)(2,1)}, bf16[256,512]{1,0:T(8,128)(2,1)S(1)}, u32[]{:S(2)}, u32[]{:S(2)}) collective-permute-start(bf16[256,512]{1,0:T(8,128)(2,1)} %bitcast.47), channel_id=1, source_target_pairs={{0,24},{1,25},{2,26},{3,27},{4,28},{5,29},{6,30},{7,31},{8,0},{9,1... | collective-permute-start | bytes 786440 | tf_op jit(solution)/shard_map/ppermute | solution.py:46
  4.0 1.6 %collective-permute-start = (bf16[256,512]{1,0:T(8,128)(2,1)}, bf16[256,512]{1,0:T(8,128)(2,1)S(1)}, u32[]{:S(2)}, u32[]{:S(2)}) collective-permute-start(bf16[256,512]{1,0:T(8,128)(2,1)} %bitcast.49), channel_id=1, source_target_pairs={{0,2},{1,3},{2,0},{3,1},{4,6},{5,7},{6,4},{7,5},{8,10},{9,11},{10,... | collective-permute-start | bytes 786440 | tf_op jit(solution)/shard_map/ppermute | solution.py:46
  5.7 0.7 pad_add_fusion.place
  6.3 2.1 %delta.1 = (f32[2,64,512]{2,1,0:T(8,128)}, f32[2,64,512]{2,1,0:T(8,128)}) custom-call(s32[4]{0:T(128)} %pad_add_fusion.place, f32[256,512]{1,0:T(8,128)} %glob.3, f32[256,512]{1,0:T(8,128)} %bitcast.53), custom_call_target="tpu_custom_call" | custom-call | tf_op jit(solution)/shard_map/delta/pallas_call | solution.py:331
  8.4 1.3 %collective-permute-start.3 = (f32[2,64,512]{2,1,0:T(8,128)}, f32[2,64,512]{2,1,0:T(8,128)S(1)}, u32[]{:S(2)}, u32[]{:S(2)}) collective-permute-start(f32[2,64,512]{2,1,0:T(8,128)} %get-tuple-element.70), channel_id=1, source_target_pairs={{0,64},{32,96},{64,0},{96,32},{128,192},{160,224},{192,128},{224,1... | collective-permute-start | bytes 786440 | tf_op jit(solution)/shard_map/ppermute | solution.py:51
  9.7 0.7 constant_dynamic-slice_fusion
  10.4 4.0 %normalise.1 = (f32[128,128]{1,0:T(8,128)}, bf16[128,2560]{1,0:T(8,128)(2,1)}, bf16[128,2560]{1,0:T(8,128)(2,1)}, bf16[128,2560]{1,0:T(8,128)(2,1)}, bf16[128,2560]{1,0:T(8,128)(2,1)}) custom-call(s32[4]{0:T(128)} %pad_add_fusion.place, bf16[128,8192]{1,0:T(8,128)(2,1)} %bitcast.37, f32[1,8192]{1,0:T(1,128)} %gain.9, bf16[128,512]{1,0:T(8,128)(2,1)} %bitcast.42), custom_call_target="tpu_custom_call" | custom-call | tf_op jit(solution)/shard_map/normalise/pallas_call | solution.py:81
  14.5 0.6 collective-permute-done.3
  15.2 3.1 %collective-permute-start.7 = (bf16[512,512]{1,0:T(8,128)(2,1)S(1)}, bf16[512,512]{1,0:T(8,128)(2,1)S(1)}, u32[]{:S(2)}, u32[]{:S(2)}) collective-permute-start(bf16[512,512]{1,0:T(8,128)(2,1)S(1)} %pad_maximum_fusion), channel_id=1, source_target_pairs={{0,4},{1,5},{2,6},{3,7},{4,0},{5,1},{6,2},{7,3},{8,12},{9,13},{10,... | collective-permute-start | bytes 1572872 | tf_op jit(solution)/shard_map/ppermute | solution.py:46
  18.3 2.7 %collective-permute-start.5 = (bf16[128,2560]{1,0:T(8,128)(2,1)S(1)}, bf16[128,2560]{1,0:T(8,128)(2,1)S(1)}, u32[]{:S(2)}, u32[]{:S(2)}) collective-permute-start(bf16[128,2560]{1,0:T(8,128)(2,1)S(1)} %copy-done.22), channel_id=1, source_target_pairs={{0,24},{1,25},{2,26},{3,27},{4,28},{5,29},{6,30},{7,31},{8,0},{9,1... | collective-permute-start | bytes 1966088 | tf_op jit(solution)/shard_map/ppermute | solution.py:46
  21.0 1.0 collective-permute-start.6
  22.0 2.8 %collective-permute-start.8 = (f32[64,512]{1,0:T(8,128)S(1)}, f32[64,512]{1,0:T(8,128)S(1)}, u32[]{:S(2)}, u32[]{:S(2)}) collective-permute-start(f32[64,512]{1,0:T(8,128)S(1)} %slice_bitcast_fusion), channel_id=1, source_target_pairs={{0,192},{32,224},{64,128},{96,160},{128,64},{160,96},{192,0},{224,... | collective-permute-start | bytes 393224 | tf_op jit(solution)/shard_map/ppermute | solution.py:51
  24.8 2.7 %collective-permute-done.8 = f32[64,512]{1,0:T(8,128)S(1)} collective-permute-done((f32[64,512]{1,0:T(8,128)S(1)}, f32[64,512]{1,0:T(8,128)S(1)}, u32[]{:S(2)}, u32[]{:S(2)}) %collective-permute-start.8) | collective-permute-done | bytes 131104 | tf_op jit(solution)/shard_map/ppermute | solution.py:51
  27.5 4.3 %collective-permute-start.9 = (f32[64,512]{1,0:T(8,128)S(1)}, f32[64,512]{1,0:T(8,128)S(1)}, u32[]{:S(2)}, u32[]{:S(2)}) collective-permute-start(f32[64,512]{1,0:T(8,128)S(1)} %fusion.3), channel_id=1, source_target_pairs={{0,32},{32,0},{64,96},{96,64},{128,160},{160,128},{192,224},{224,1... | collective-permute-start | bytes 393224 | tf_op jit(solution)/shard_map/ppermute | solution.py:51
  31.8 3.8 %backward_early.3 = (f32[128,512]{1,0:T(8,128)}, f32[4,128,256]{2,1,0:T(8,128)}, bf16[1024,512]{1,0:T(8,128)(2,1)}) custom-call(s32[4]{0:T(128)} %pad_add_fusion.place, bf16[128,8192]{1,0:T(8,128)(2,1)} %bitcast.38, f32[1,8192]{1,0:T(1,128)} %gain.9, f32[128,128]{1,0:T(8,128)} %get-tuple-element.65.rinv, bf16[128,512]{1,0:T(8,128)(2,1)} %bitcast.43, ...), custom_call_target="tpu_custom_call" | custom-call | tf_op jit(solution)/shard_map/backward_early/pallas_call | solution.py:239
  35.6 0.6 collective-permute-done.9
  36.2 11.2 %collective-permute-done.7.third.refs_1_ = bf16[512,512]{1,0:T(8,128)(2,1)S(1)} collective-permute-done((bf16[512,512]{1,0:T(8,128)(2,1)S(1)}, bf16[512,512]{1,0:T(8,128)(2,1)S(1)}, u32[]{:S(2)}, u32[]{:S(2)}) %collective-permute-start.7) | collective-permute-done | bytes 524320 | tf_op jit(solution)/shard_map/ppermute | solution.py:46
  47.5 0.7 collective-permute-done.6.r3
  48.2 0.2 copy-done.1
  48.4 0.2 copy-done.2
  48.7 0.3 copy-done.3
  49.0 3.3 %pack.1 = (bf16[512,1536]{1,0:T(8,128)(2,1)}, bf16[768,512]{1,0:T(8,128)(2,1)}, bf16[1536,512]{1,0:T(8,128)(2,1)}) custom-call(bf16[128,2560]{1,0:T(8,128)(2,1)} %get-tuple-element.81.r0, bf16[128,2560]{1,0:T(8,128)(2,1)} %copy-done.1, bf16[128,2560]{1,0:T(8,128)(2,1)} %copy-done.2, bf16[128,2560]{1,0:T(8,128)(2,1)} %copy-done.3, ...), custom_call_target="tpu_custom_call" | custom-call | tf_op jit(solution)/shard_map/pack/pallas_call | solution.py:138
  52.3 3.7 %collective-permute-start.12 = (bf16[512,1536]{1,0:T(8,128)(2,1)}, bf16[512,1536]{1,0:T(8,128)(2,1)S(1)}, u32[]{:S(2)}, u32[]{:S(2)}) collective-permute-start(bf16[512,1536]{1,0:T(8,128)(2,1)} %get-tuple-element.89), channel_id=1, source_target_pairs={{0,1},{1,0},{2,3},{3,2},{4,5},{5,4},{6,7},{7,6},{8,9},{9,8},{10,11... | collective-permute-start | bytes 4718600 | tf_op jit(solution)/shard_map/ppermute | solution.py:46
  56.1 1.8 %collective-permute-start.11 = (bf16[768,512]{1,0:T(8,128)(2,1)}, bf16[768,512]{1,0:T(8,128)(2,1)S(1)}, u32[]{:S(2)}, u32[]{:S(2)}) collective-permute-start(bf16[768,512]{1,0:T(8,128)(2,1)} %get-tuple-element.87), channel_id=1, source_target_pairs={{0,24},{1,25},{2,26},{3,27},{4,28},{5,29},{6,30},{7,31},{8,0},{9,1... | collective-permute-start | bytes 2359304 | tf_op jit(solution)/shard_map/ppermute | solution.py:46
  58.0 2.8 %collective-permute-start.13 = (f32[64,512]{1,0:T(8,128)S(1)}, f32[64,512]{1,0:T(8,128)S(1)}, u32[]{:S(2)}, u32[]{:S(2)}) collective-permute-start(f32[64,512]{1,0:T(8,128)S(1)} %add_multiply_fusion), channel_id=1, source_target_pairs={{0,192},{32,224},{64,128},{96,160},{128,64},{160,96},{192,0},{224,... | collective-permute-start | bytes 393224 | tf_op jit(solution)/shard_map/ppermute | solution.py:51
  60.8 3.0 %collective-permute-done.13 = f32[64,512]{1,0:T(8,128)S(1)} collective-permute-done((f32[64,512]{1,0:T(8,128)S(1)}, f32[64,512]{1,0:T(8,128)S(1)}, u32[]{:S(2)}, u32[]{:S(2)}) %collective-permute-start.13) | collective-permute-done | bytes 131104 | tf_op jit(solution)/shard_map/ppermute | solution.py:51
  63.7 1.1 %copy-done.9 = bf16[512,1536]{1,0:T(8,128)(2,1)} copy-done((bf16[512,1536]{1,0:T(8,128)(2,1)}, bf16[512,1536]{1,0:T(8,128)(2,1)S(1)}, u32[]{:S(2)}) %copy-start.9) | copy-done | bytes 1572888
  64.9 4.3 %wgrad_part.1 = (f32[2,256,512]{2,1,0:T(8,128)}, bf16[256,512]{1,0:T(8,128)(2,1)}, bf16[256,512]{1,0:T(8,128)(2,1)}) custom-call(bf16[128,2560]{1,0:T(8,128)(2,1)} %get-tuple-element.81.r0, bf16[128,2560]{1,0:T(8,128)(2,1)} %copy-done.1, bf16[128,2560]{1,0:T(8,128)(2,1)} %copy-done.2, bf16[128,2560]{1,0:T(8,128)(2,1)} %copy-done.3, bf16[512,1536]{1,0:T(8,128)(2,1)} %copy-done.9), custom_call_target="tpu_custom_call" | custom-call | tf_op jit(solution)/shard_map/wgrad_part/pallas_call | solution.py:169
  69.2 0.3 collective-permute-start.16
  69.4 0.3 collective-permute-start.15
  69.7 1.1 %copy-done.7 = bf16[1536,512]{1,0:T(8,128)(2,1)} copy-done((bf16[1536,512]{1,0:T(8,128)(2,1)}, bf16[1536,512]{1,0:T(8,128)(2,1)S(1)}, u32[]{:S(2)}) %copy-start.7) | copy-done | bytes 1572888
  70.9 4.5 %backward_early.4 = (f32[128,512]{1,0:T(8,128)}, f32[8,128,256]{2,1,0:T(8,128)}) custom-call(s32[4]{0:T(128)} %pad_add_fusion.place, bf16[128,8192]{1,0:T(8,128)(2,1)} %bitcast.39, f32[1,8192]{1,0:T(1,128)} %gain.9, f32[128,128]{1,0:T(8,128)} %get-tuple-element.65.rinv, bf16[128,512]{1,0:T(8,128)(2,1)} %bitcast.44, f32[128,512]{1,0:T(8,128)} %get-tuple-element.93.refs_0_, ...), custom_call_target="tpu_custom_call" | custom-call | tf_op jit(solution)/shard_map/backward_early/pallas_call | solution.py:239
  75.4 2.4 %collective-permute-done.10 = bf16[768,512]{1,0:T(8,128)(2,1)S(1)} collective-permute-done((bf16[768,512]{1,0:T(8,128)(2,1)}, bf16[768,512]{1,0:T(8,128)(2,1)S(1)}, u32[]{:S(2)}, u32[]{:S(2)}) %collective-permute-start.10) | collective-permute-done | bytes 786464 | tf_op jit(solution)/shard_map/ppermute | solution.py:46
  77.9 0.6 copy-done.18
  78.5 1.6 %collective-permute-start.19 = (bf16[1536,512]{1,0:T(8,128)(2,1)S(1)}, bf16[1536,512]{1,0:T(8,128)(2,1)S(1)}, u32[]{:S(2)}, u32[]{:S(2)}) collective-permute-start(bf16[1536,512]{1,0:T(8,128)(2,1)S(1)} %constant_dynamic-update-slice_fusion.refs_1_), channel_id=1, source_target_pairs={{0,1},{1,0},{2,3},{3,2},{4,5},{5,4},{6,7},{7,6},{8,9},{9,8},{10,11... | collective-permute-start | bytes 4718600 | tf_op jit(solution)/shard_map/ppermute | solution.py:46
  80.0 0.2 collective-permute-start.21
  80.3 0.1 collective-permute-start.20
  80.7 2.7 %collective-permute-start.17 = (bf16[512,512]{1,0:T(8,128)(2,1)S(1)}, bf16[512,512]{1,0:T(8,128)(2,1)S(1)}, u32[]{:S(2)}, u32[]{:S(2)}) collective-permute-start(bf16[512,512]{1,0:T(8,128)(2,1)S(1)} %pad_maximum_fusion.1), channel_id=1, source_target_pairs={{0,24},{1,25},{2,26},{3,27},{4,28},{5,29},{6,30},{7,31},{8,0},{9,1... | collective-permute-start | bytes 1572872 | tf_op jit(solution)/shard_map/ppermute | solution.py:46
  83.3 2.7 %outer_update.1 = (f32[256,512]{1,0:T(8,128)}, bf16[256,512]{1,0:T(8,128)(2,1)}, f32[4,256]{1,0:T(4,128)}) custom-call(s32[4]{0:T(128)} %pad_add_fusion.place, f32[2,64,512]{2,1,0:T(8,128)} %copy-done.10, f32[2,64,512]{2,1,0:T(8,128)} %copy-done.18, f32[256,512]{1,0:T(8,128)} %glob.3, bf16[256,512]{1,0:T(8,128)(2,1)} %codes.1, f32[4,256]{1,0:T(4,128)} %bitcast.55), custom_call_target="tpu_custom_call" | custom-call | tf_op jit(solution)/shard_map/outer_update/pallas_call | solution.py:368
  86.0 1.1 %copy-done.8 = bf16[1536,512]{1,0:T(8,128)(2,1)} copy-done((bf16[1536,512]{1,0:T(8,128)(2,1)}, bf16[1536,512]{1,0:T(8,128)(2,1)S(1)}, u32[]{:S(2)}) %copy-start.8) | copy-done | bytes 1572888
  87.2 5.5 %backward_early.5 = (f32[128,512]{1,0:T(8,128)}, f32[12,128,256]{2,1,0:T(8,128)}) custom-call(s32[4]{0:T(128)} %pad_add_fusion.place, bf16[128,8192]{1,0:T(8,128)(2,1)} %bitcast.40, f32[1,8192]{1,0:T(1,128)} %gain.9, f32[128,128]{1,0:T(8,128)} %get-tuple-element.65.rinv, bf16[128,512]{1,0:T(8,128)(2,1)} %bitcast.45, f32[128,512]{1,0:T(8,128)} %get-tuple-element.100.refs_0_, ...), custom_call_target="tpu_custom_call" | custom-call | tf_op jit(solution)/shard_map/backward_early/pallas_call | solution.py:239
  92.8 1.7 %collective-permute-done.20 = bf16[256,512]{1,0:T(8,128)(2,1)} collective-permute-done((bf16[256,512]{1,0:T(8,128)(2,1)S(1)}, bf16[256,512]{1,0:T(8,128)(2,1)}, u32[]{:S(2)}, u32[]{:S(2)}) %collective-permute-start.20) | collective-permute-done | bytes 262176 | tf_op jit(solution)/shard_map/ppermute | solution.py:46
  94.5 2.4 %fusion.2 = (f32[1,256,512]{2,1,0:T(8,128)}, f32[256]{0:T(256)}) fusion(bf16[256,512]{1,0:T(8,128)(2,1)} %collective-permute-done.20, bf16[256,512]{1,0:T(8,128)(2,1)S(1)} %collective-permute-done.21, f32[2,256,512]{2,1,0:T(8,128)S(1)} %copy-done.11, f32[256,512]{1,0:T(8,128)S(1)} %convert_divide_fusion), kind=kLoop, calls=%fused_computation.9 | loop fusion | flops 786176 | bytes 2098176 | tf_op jit(solution)/shard_map/broadcast_in_dim | solution.py:467
  97.0 1.3 %collective-permute-start.22 = (bf16[512,512]{1,0:T(8,128)(2,1)S(1)}, bf16[512,512]{1,0:T(8,128)(2,1)S(1)}, u32[]{:S(2)}, u32[]{:S(2)}) collective-permute-start(bf16[512,512]{1,0:T(8,128)(2,1)S(1)} %collective-permute-done.17.refs_3_), channel_id=1, source_target_pairs={{0,1},{1,0},{2,3},{3,2},{4,5},{5,4},{6,7},{7,6},{8,9},{9,8},{10,11... | collective-permute-start | bytes 1572872 | tf_op jit(solution)/shard_map/ppermute | solution.py:46
  98.4 1.4 %collective-permute-done.22.refs_4_ = bf16[512,512]{1,0:T(8,128)(2,1)S(1)} collective-permute-done((bf16[512,512]{1,0:T(8,128)(2,1)S(1)}, bf16[512,512]{1,0:T(8,128)(2,1)S(1)}, u32[]{:S(2)}, u32[]{:S(2)}) %collective-permute-start.22) | collective-permute-done | bytes 524320 | tf_op jit(solution)/shard_map/ppermute | solution.py:46
  99.8 0.7 collective-permute-done.23.refs_6_
  100.6 0.7 copy-done.17
  101.4 6.8 %backward_late.1 = (f32[128,512]{1,0:T(8,128)}, f32[128,8192]{1,0:T(8,128)}) custom-call(s32[4]{0:T(128)} %pad_add_fusion.place, bf16[128,8192]{1,0:T(8,128)(2,1)} %bitcast.41, f32[1,8192]{1,0:T(1,128)} %gain.9, f32[128,128]{1,0:T(8,128)} %get-tuple-element.65.rinv, bf16[128,512]{1,0:T(8,128)(2,1)} %bitcast.46, f32[128,512]{1,0:T(8,128)} %get-tuple-element.111.early, ...), custom_call_target="tpu_custom_call" | custom-call | tf_op jit(solution)/shard_map/backward_late/pallas_call | solution.py:306
  (71 shorter events, 1.1 us)
Async XLA Ops:
  0.6 13.8 %collective-permute-start.2 = (bf16[256,512]{1,0:T(8,128)(2,1)}, bf16[256,512]{1,0:T(8,128)(2,1)S(1)}, u32[]{:S(2)}, u32[]{:S(2)}) collective-permute-start(bf16[256,512]{1,0:T(8,128)(2,1)} %bitcast.47), channel_id=1, source_target_pairs={{0,24},{1,25},{2,26},{3,27},{4,28},{5,29},{6,30},{7,31},{8,0},{9,1... | collective-permute-start | bytes 786440 | tf_op jit(solution)/shard_map/ppermute | solution.py:46
  4.0 10.5 %collective-permute-start.1 = (bf16[256,512]{1,0:T(8,128)(2,1)}, bf16[256,512]{1,0:T(8,128)(2,1)S(1)}, u32[]{:S(2)}, u32[]{:S(2)}) collective-permute-start(bf16[256,512]{1,0:T(8,128)(2,1)} %bitcast.48), channel_id=1, source_target_pairs={{0,8},{1,9},{2,10},{3,11},{4,12},{5,13},{6,14},{7,15},{8,16},{9,17... | collective-permute-start | bytes 786440 | tf_op jit(solution)/shard_map/ppermute | solution.py:46
  4.0 10.5 %collective-permute-start = (bf16[256,512]{1,0:T(8,128)(2,1)}, bf16[256,512]{1,0:T(8,128)(2,1)S(1)}, u32[]{:S(2)}, u32[]{:S(2)}) collective-permute-start(bf16[256,512]{1,0:T(8,128)(2,1)} %bitcast.49), channel_id=1, source_target_pairs={{0,2},{1,3},{2,0},{3,1},{4,6},{5,7},{6,4},{7,5},{8,10},{9,11},{10,... | collective-permute-start | bytes 786440 | tf_op jit(solution)/shard_map/ppermute | solution.py:46
  6.3 8.0 %copy-start.5 = (bf16[1,256,512]{2,1,0:T(8,128)(2,1)S(1)}, bf16[1,256,512]{2,1,0:T(8,128)(2,1)}, u32[]{:S(2)}) copy-start(bf16[1,256,512]{2,1,0:T(8,128)(2,1)} %param.10) | copy-start | bytes 786436
  8.4 6.8 %collective-permute-start.3 = (f32[2,64,512]{2,1,0:T(8,128)}, f32[2,64,512]{2,1,0:T(8,128)S(1)}, u32[]{:S(2)}, u32[]{:S(2)}) collective-permute-start(f32[2,64,512]{2,1,0:T(8,128)} %get-tuple-element.70), channel_id=1, source_target_pairs={{0,64},{32,96},{64,0},{96,32},{128,192},{160,224},{192,128},{224,1... | collective-permute-start | bytes 786440 | tf_op jit(solution)/shard_map/ppermute | solution.py:51
  10.4 11.6 %copy-start.19 = (f32[2,64,512]{2,1,0:T(8,128)S(1)}, f32[2,64,512]{2,1,0:T(8,128)}, u32[]{:S(2)}) copy-start(f32[2,64,512]{2,1,0:T(8,128)} %get-tuple-element.77) | copy-start | bytes 786436
  14.3 4.0 %copy-start.22 = (bf16[128,2560]{1,0:T(8,128)(2,1)S(1)}, bf16[128,2560]{1,0:T(8,128)(2,1)}, u32[]{:S(2)}) copy-start(bf16[128,2560]{1,0:T(8,128)(2,1)} %get-tuple-element.74) | copy-start | bytes 1966084
  14.3 6.6 %copy-start.21 = (bf16[128,2560]{1,0:T(8,128)(2,1)S(1)}, bf16[128,2560]{1,0:T(8,128)(2,1)}, u32[]{:S(2)}) copy-start(bf16[128,2560]{1,0:T(8,128)(2,1)} %get-tuple-element.75) | copy-start | bytes 1966084
  14.5 17.3 %copy-start.12 = (bf16[256,512]{1,0:T(8,128)(2,1)}, bf16[256,512]{1,0:T(8,128)(2,1)S(1)}, u32[]{:S(2)}) copy-start(bf16[256,512]{1,0:T(8,128)(2,1)S(1)} %collective-permute-done.2.refs_2_) | copy-start | bytes 786436
  14.5 17.3 %copy-start.20 = (bf16[256,512]{1,0:T(8,128)(2,1)}, bf16[256,512]{1,0:T(8,128)(2,1)S(1)}, u32[]{:S(2)}) copy-start(bf16[256,512]{1,0:T(8,128)(2,1)S(1)} %collective-permute-done.1.refs_3_) | copy-start | bytes 786436
  14.5 17.3 %copy-start.4 = (bf16[256,512]{1,0:T(8,128)(2,1)}, bf16[256,512]{1,0:T(8,128)(2,1)S(1)}, u32[]{:S(2)}) copy-start(bf16[256,512]{1,0:T(8,128)(2,1)S(1)} %collective-permute-done.refs_1_.second) | copy-start | bytes 786436
  15.2 32.2 %collective-permute-start.7 = (bf16[512,512]{1,0:T(8,128)(2,1)S(1)}, bf16[512,512]{1,0:T(8,128)(2,1)S(1)}, u32[]{:S(2)}, u32[]{:S(2)}) collective-permute-start(bf16[512,512]{1,0:T(8,128)(2,1)S(1)} %pad_maximum_fusion), channel_id=1, source_target_pairs={{0,4},{1,5},{2,6},{3,7},{4,0},{5,1},{6,2},{7,3},{8,12},{9,13},{10,... | collective-permute-start | bytes 1572872 | tf_op jit(solution)/shard_map/ppermute | solution.py:46
  18.3 29.1 %collective-permute-start.4 = (bf16[128,2560]{1,0:T(8,128)(2,1)}, bf16[128,2560]{1,0:T(8,128)(2,1)S(1)}, u32[]{:S(2)}, u32[]{:S(2)}) collective-permute-start(bf16[128,2560]{1,0:T(8,128)(2,1)} %get-tuple-element.73), channel_id=1, source_target_pairs={{0,8},{1,9},{2,10},{3,11},{4,12},{5,13},{6,14},{7,15},{8,16},{9,17... | collective-permute-start | bytes 1966088 | tf_op jit(solution)/shard_map/ppermute | solution.py:46
  18.3 29.1 %collective-permute-start.5 = (bf16[128,2560]{1,0:T(8,128)(2,1)S(1)}, bf16[128,2560]{1,0:T(8,128)(2,1)S(1)}, u32[]{:S(2)}, u32[]{:S(2)}) collective-permute-start(bf16[128,2560]{1,0:T(8,128)(2,1)S(1)} %copy-done.22), channel_id=1, source_target_pairs={{0,24},{1,25},{2,26},{3,27},{4,28},{5,29},{6,30},{7,31},{8,0},{9,1... | collective-permute-start | bytes 1966088 | tf_op jit(solution)/shard_map/ppermute | solution.py:46
  21.0 27.2 %collective-permute-start.6 = (bf16[128,2560]{1,0:T(8,128)(2,1)S(1)}, bf16[128,2560]{1,0:T(8,128)(2,1)S(1)}, u32[]{:S(2)}, u32[]{:S(2)}) collective-permute-start(bf16[128,2560]{1,0:T(8,128)(2,1)S(1)} %copy-done.21), channel_id=1, source_target_pairs={{0,16},{1,17},{2,18},{3,19},{4,20},{5,21},{6,22},{7,23},{8,24},{9,... | collective-permute-start | bytes 1966088 | tf_op jit(solution)/shard_map/ppermute | solution.py:46
  22.0 5.5 %collective-permute-start.8 = (f32[64,512]{1,0:T(8,128)S(1)}, f32[64,512]{1,0:T(8,128)S(1)}, u32[]{:S(2)}, u32[]{:S(2)}) collective-permute-start(f32[64,512]{1,0:T(8,128)S(1)} %slice_bitcast_fusion), channel_id=1, source_target_pairs={{0,192},{32,224},{64,128},{96,160},{128,64},{160,96},{192,0},{224,... | collective-permute-start | bytes 393224 | tf_op jit(solution)/shard_map/ppermute | solution.py:51
  27.5 8.7 %collective-permute-start.9 = (f32[64,512]{1,0:T(8,128)S(1)}, f32[64,512]{1,0:T(8,128)S(1)}, u32[]{:S(2)}, u32[]{:S(2)}) collective-permute-start(f32[64,512]{1,0:T(8,128)S(1)} %fusion.3), channel_id=1, source_target_pairs={{0,32},{32,0},{64,96},{96,64},{128,160},{160,128},{192,224},{224,1... | collective-permute-start | bytes 393224 | tf_op jit(solution)/shard_map/ppermute | solution.py:51
  47.4 0.8 copy-start.6
  47.4 1.0 copy-start.1
  47.4 1.2 %copy-start.2 = (bf16[128,2560]{1,0:T(8,128)(2,1)}, bf16[128,2560]{1,0:T(8,128)(2,1)S(1)}, u32[]{:S(2)}) copy-start(bf16[128,2560]{1,0:T(8,128)(2,1)S(1)} %collective-permute-done.5.r2) | copy-start | bytes 1966084
  48.2 0.8 copy-start.3
  52.3 11.4 %collective-permute-start.12 = (bf16[512,1536]{1,0:T(8,128)(2,1)}, bf16[512,1536]{1,0:T(8,128)(2,1)S(1)}, u32[]{:S(2)}, u32[]{:S(2)}) collective-permute-start(bf16[512,1536]{1,0:T(8,128)(2,1)} %get-tuple-element.89), channel_id=1, source_target_pairs={{0,1},{1,0},{2,3},{3,2},{4,5},{5,4},{6,7},{7,6},{8,9},{9,8},{10,11... | collective-permute-start | bytes 4718600 | tf_op jit(solution)/shard_map/ppermute | solution.py:46
  56.0 13.7 %collective-permute-start.14 = (bf16[1536,512]{1,0:T(8,128)(2,1)}, bf16[1536,512]{1,0:T(8,128)(2,1)S(1)}, u32[]{:S(2)}, u32[]{:S(2)}) collective-permute-start(bf16[1536,512]{1,0:T(8,128)(2,1)} %get-tuple-element.94), channel_id=1, source_target_pairs={{0,1},{1,0},{2,3},{3,2},{4,5},{5,4},{6,7},{7,6},{8,9},{9,8},{10,11... | collective-permute-start | bytes 4718600 | tf_op jit(solution)/shard_map/ppermute | solution.py:46
  56.1 19.3 %collective-permute-start.11 = (bf16[768,512]{1,0:T(8,128)(2,1)}, bf16[768,512]{1,0:T(8,128)(2,1)S(1)}, u32[]{:S(2)}, u32[]{:S(2)}) collective-permute-start(bf16[768,512]{1,0:T(8,128)(2,1)} %get-tuple-element.87), channel_id=1, source_target_pairs={{0,24},{1,25},{2,26},{3,27},{4,28},{5,29},{6,30},{7,31},{8,0},{9,1... | collective-permute-start | bytes 2359304 | tf_op jit(solution)/shard_map/ppermute | solution.py:46
  57.9 19.8 %collective-permute-start.10 = (bf16[768,512]{1,0:T(8,128)(2,1)}, bf16[768,512]{1,0:T(8,128)(2,1)S(1)}, u32[]{:S(2)}, u32[]{:S(2)}) collective-permute-start(bf16[768,512]{1,0:T(8,128)(2,1)} %get-tuple-element.87), channel_id=1, source_target_pairs={{0,8},{1,9},{2,10},{3,11},{4,12},{5,13},{6,14},{7,15},{8,16},{9,17... | collective-permute-start | bytes 2359304 | tf_op jit(solution)/shard_map/ppermute | solution.py:46
  58.0 5.8 %collective-permute-start.13 = (f32[64,512]{1,0:T(8,128)S(1)}, f32[64,512]{1,0:T(8,128)S(1)}, u32[]{:S(2)}, u32[]{:S(2)}) collective-permute-start(f32[64,512]{1,0:T(8,128)S(1)} %add_multiply_fusion), channel_id=1, source_target_pairs={{0,192},{32,224},{64,128},{96,160},{128,64},{160,96},{192,0},{224,... | collective-permute-start | bytes 393224 | tf_op jit(solution)/shard_map/ppermute | solution.py:51
  63.7 1.1 %copy-start.9 = (bf16[512,1536]{1,0:T(8,128)(2,1)}, bf16[512,1536]{1,0:T(8,128)(2,1)S(1)}, u32[]{:S(2)}) copy-start(bf16[512,1536]{1,0:T(8,128)(2,1)S(1)} %collective-permute-done.12.other) | copy-start | bytes 4718596
  69.2 11.3 %copy-start.10 = (f32[2,64,512]{2,1,0:T(8,128)}, f32[2,64,512]{2,1,0:T(8,128)S(1)}, u32[]{:S(2)}) copy-start(f32[2,64,512]{2,1,0:T(8,128)S(1)} %pad_maximum_fusion.2.p03) | copy-start | bytes 786436
  69.2 8.6 %collective-permute-start.16 = (f32[2,64,512]{2,1,0:T(8,128)S(1)}, f32[2,64,512]{2,1,0:T(8,128)S(1)}, u32[]{:S(2)}, u32[]{:S(2)}) collective-permute-start(f32[2,64,512]{2,1,0:T(8,128)S(1)} %pad_maximum_fusion.2.p03), channel_id=1, source_target_pairs={{0,64},{32,96},{64,0},{96,32},{128,192},{160,224},{192,128},{224,1... | collective-permute-start | bytes 786440 | tf_op jit(solution)/shard_map/ppermute | solution.py:51
  69.4 8.3 %collective-permute-start.15 = (bf16[256,512]{1,0:T(8,128)(2,1)}, bf16[256,512]{1,0:T(8,128)(2,1)S(1)}, u32[]{:S(2)}, u32[]{:S(2)}) collective-permute-start(bf16[256,512]{1,0:T(8,128)(2,1)} %get-tuple-element.96), channel_id=1, source_target_pairs={{0,2},{1,3},{2,0},{3,1},{4,6},{5,7},{6,4},{7,5},{8,10},{9,11},{10,... | collective-permute-start | bytes 786440 | tf_op jit(solution)/shard_map/ppermute | solution.py:46
  69.7 1.1 %copy-start.7 = (bf16[1536,512]{1,0:T(8,128)(2,1)}, bf16[1536,512]{1,0:T(8,128)(2,1)S(1)}, u32[]{:S(2)}) copy-start(bf16[1536,512]{1,0:T(8,128)(2,1)S(1)} %collective-permute-done.14.refs_2_) | copy-start | bytes 4718596
  77.8 0.7 copy-start.18
  77.8 2.5 %copy-start.11 = (f32[2,256,512]{2,1,0:T(8,128)S(1)}, f32[2,256,512]{2,1,0:T(8,128)}, u32[]{:S(2)}) copy-start(f32[2,256,512]{2,1,0:T(8,128)} %get-tuple-element.102) | copy-start | bytes 3145732
  77.8 2.6 %copy-start.13 = (bf16[256,512]{1,0:T(8,128)(2,1)S(1)}, bf16[256,512]{1,0:T(8,128)(2,1)}, u32[]{:S(2)}) copy-start(bf16[256,512]{1,0:T(8,128)(2,1)} %copy-done.12) | copy-start | bytes 786436
  78.5 2.1 %copy-start = (bf16[1536,512]{1,0:T(8,128)(2,1)}, bf16[1536,512]{1,0:T(8,128)(2,1)S(1)}, u32[]{:S(2)}) copy-start(bf16[1536,512]{1,0:T(8,128)(2,1)S(1)} %constant_dynamic-update-slice_fusion.refs_1_) | copy-start | bytes 4718596
  78.5 7.6 %collective-permute-start.19 = (bf16[1536,512]{1,0:T(8,128)(2,1)S(1)}, bf16[1536,512]{1,0:T(8,128)(2,1)S(1)}, u32[]{:S(2)}, u32[]{:S(2)}) collective-permute-start(bf16[1536,512]{1,0:T(8,128)(2,1)S(1)} %constant_dynamic-update-slice_fusion.refs_1_), channel_id=1, source_target_pairs={{0,1},{1,0},{2,3},{3,2},{4,5},{5,4},{6,7},{7,6},{8,9},{9,8},{10,11... | collective-permute-start | bytes 4718600 | tf_op jit(solution)/shard_map/ppermute | solution.py:46
  80.0 12.8 %collective-permute-start.21 = (bf16[256,512]{1,0:T(8,128)(2,1)}, bf16[256,512]{1,0:T(8,128)(2,1)S(1)}, u32[]{:S(2)}, u32[]{:S(2)}) collective-permute-start(bf16[256,512]{1,0:T(8,128)(2,1)} %get-tuple-element.104), channel_id=1, source_target_pairs={{0,2},{1,3},{2,0},{3,1},{4,6},{5,7},{6,4},{7,5},{8,10},{9,11},{10,... | collective-permute-start | bytes 786440 | tf_op jit(solution)/shard_map/ppermute | solution.py:46
  80.3 14.2 %collective-permute-start.20 = (bf16[256,512]{1,0:T(8,128)(2,1)S(1)}, bf16[256,512]{1,0:T(8,128)(2,1)}, u32[]{:S(2)}, u32[]{:S(2)}) collective-permute-start(bf16[256,512]{1,0:T(8,128)(2,1)S(1)} %fusion.1), channel_id=1, source_target_pairs={{0,4},{1,5},{2,6},{3,7},{4,0},{5,1},{6,2},{7,3},{8,12},{9,13},{10,... | collective-permute-start | bytes 786440 | tf_op jit(solution)/shard_map/ppermute | solution.py:46
  80.6 16.4 %collective-permute-start.18 = (bf16[512,512]{1,0:T(8,128)(2,1)S(1)}, bf16[512,512]{1,0:T(8,128)(2,1)S(1)}, u32[]{:S(2)}, u32[]{:S(2)}) collective-permute-start(bf16[512,512]{1,0:T(8,128)(2,1)S(1)} %slice.21), channel_id=1, source_target_pairs={{0,8},{1,9},{2,10},{3,11},{4,12},{5,13},{6,14},{7,15},{8,16},{9,17... | collective-permute-start | bytes 1572872 | tf_op jit(solution)/shard_map/ppermute | solution.py:46
  80.7 16.3 %collective-permute-start.17 = (bf16[512,512]{1,0:T(8,128)(2,1)S(1)}, bf16[512,512]{1,0:T(8,128)(2,1)S(1)}, u32[]{:S(2)}, u32[]{:S(2)}) collective-permute-start(bf16[512,512]{1,0:T(8,128)(2,1)S(1)} %pad_maximum_fusion.1), channel_id=1, source_target_pairs={{0,24},{1,25},{2,26},{3,27},{4,28},{5,29},{6,30},{7,31},{8,0},{9,1... | collective-permute-start | bytes 1572872 | tf_op jit(solution)/shard_map/ppermute | solution.py:46
  86.0 1.1 %copy-start.8 = (bf16[1536,512]{1,0:T(8,128)(2,1)}, bf16[1536,512]{1,0:T(8,128)(2,1)S(1)}, u32[]{:S(2)}) copy-start(bf16[1536,512]{1,0:T(8,128)(2,1)S(1)} %collective-permute-done.19.refs_2_) | copy-start | bytes 4718596
  97.0 3.6 %copy-start.14 = (bf16[512,512]{1,0:T(8,128)(2,1)}, bf16[512,512]{1,0:T(8,128)(2,1)S(1)}, u32[]{:S(2)}) copy-start(bf16[512,512]{1,0:T(8,128)(2,1)S(1)} %collective-permute-done.18.refs_5_) | copy-start | bytes 1572868
  97.0 3.6 %copy-start.15 = (bf16[512,512]{1,0:T(8,128)(2,1)}, bf16[512,512]{1,0:T(8,128)(2,1)S(1)}, u32[]{:S(2)}) copy-start(bf16[512,512]{1,0:T(8,128)(2,1)S(1)} %collective-permute-done.17.refs_3_) | copy-start | bytes 1572868
  97.0 2.9 %collective-permute-start.22 = (bf16[512,512]{1,0:T(8,128)(2,1)S(1)}, bf16[512,512]{1,0:T(8,128)(2,1)S(1)}, u32[]{:S(2)}, u32[]{:S(2)}) collective-permute-start(bf16[512,512]{1,0:T(8,128)(2,1)S(1)} %collective-permute-done.17.refs_3_), channel_id=1, source_target_pairs={{0,1},{1,0},{2,3},{3,2},{4,5},{5,4},{6,7},{7,6},{8,9},{9,8},{10,11... | collective-permute-start | bytes 1572872 | tf_op jit(solution)/shard_map/ppermute | solution.py:46
  98.3 2.3 %collective-permute-start.23 = (bf16[512,512]{1,0:T(8,128)(2,1)S(1)}, bf16[512,512]{1,0:T(8,128)(2,1)S(1)}, u32[]{:S(2)}, u32[]{:S(2)}) collective-permute-start(bf16[512,512]{1,0:T(8,128)(2,1)S(1)} %collective-permute-done.18.refs_5_), channel_id=1, source_target_pairs={{0,1},{1,0},{2,3},{3,2},{4,5},{5,4},{6,7},{7,6},{8,9},{9,8},{10,11... | collective-permute-start | bytes 1572872 | tf_op jit(solution)/shard_map/ppermute | solution.py:46
  99.8 0.8 copy-start.16
  100.6 0.8 copy-start.17
